TPU v7x, 32 devices: a whole 2x2x4 slice. The times are simulated.
32 devices in a mesh: animal: 8 (over y, x, core), marker: 4 (over z).
Axes of the slice: x: 2, y: 2, z: 4, core: 2. Of those that a mesh axis runs over, the one named last changes fastest.
Arguments:
- genotypes: bfloat16 [24576, 25600], P('animal', 'marker'), may hold values from -4 to 4
- direction: bfloat16 [25600, 256], P('marker'), may hold values from -6 to 6
- ridge: float32 [25600], P('marker'), may hold values from 0.5 to 2
- send_list: int32 [8, 8, 2], P('animal'), may hold values from 0 to 23, as said below
- rel_index: int32 [192, 4], P('animal'), may hold values from 0 to 39, as said below
- rel_count: int32 [192], P('animal'), may hold values from 1 to 4, as said below
- rel_prec: bfloat16 [192, 4, 128, 128], P('animal'), may hold values from -0.375 to 0.375
Outputs:
- gradient: float32 [25600, 256], P(('marker', 'animal'))
Inputs may be any that keep to these rules, and one draw needn't show every extreme that they name: `send_list`: every entry names one of the sender's own 24 blocks. `rel_index`: entry j of block g indexes g's device's source table; entry 0 is g's own block, g % 24. `rel_count`: the first block of every device has 4 live slots.
All inputs are finite; a program needn't handle non-finite values.
Results may differ from a plain program's by a relative error of at most 0.0033.
Values may be sent and summed in bfloat16 or wider, within the bound.
No kernel may reach another device: no remote copies, remote signals or barrier semaphores. Data moves between devices by JAX's collectives and lax.ppermute only.
A program may use at most 128 MiB of HBM per device.

v0:
```python
import math

import jax
import jax.numpy as jnp
from jax import lax
from jax.sharding import PartitionSpec as P

MARKERS = 25600
BLK = 128


def pedigree(animal_rows, send_list, rel_index, rel_count, rel_prec):
    block_total = animal_rows.shape[0] // BLK
    col_total = animal_rows.shape[1]
    blocked = animal_rows.reshape(block_total, BLK, col_total)
    outgoing = blocked[send_list[0]]
    incoming = lax.all_to_all(outgoing, "animal", split_axis=0, concat_axis=0, tiled=True)
    source_table = jnp.concatenate([blocked, incoming.reshape(-1, BLK, col_total)], axis=0)
    active = jnp.arange(rel_index.shape[1], dtype=jnp.int32)[None, :] < rel_count[:, None]
    gathered = source_table[rel_index]
    gathered = jnp.where(active[:, :, None, None], gathered, jnp.zeros_like(gathered))
    accumulated = jnp.einsum(
        "bjrc,bjck->brk", rel_prec, gathered, preferred_element_type=jnp.float32
    )
    return accumulated.astype(jnp.bfloat16).reshape(block_total * BLK, col_total)


def local(genotypes, direction, ridge, send_list, rel_index, rel_count, rel_prec):
    anim_rows = genotypes.shape[0]
    mark_rows = genotypes.shape[1]
    group_count = lax.axis_size("animal")
    input_scale = 1.0 / math.sqrt(MARKERS)
    partial_value = jnp.dot(genotypes, direction, preferred_element_type=jnp.float32)
    summed = lax.psum_scatter(partial_value, "marker", scatter_dimension=1, tiled=True)
    shared = (summed * input_scale).astype(jnp.bfloat16)
    relative_sum = pedigree(shared, send_list, rel_index, rel_count, rel_prec)
    effects = lax.all_gather(relative_sum, "marker", axis=1, tiled=True)
    row_count = mark_rows // group_count
    gradient = lax.psum_scatter(
        lax.dot_general(
            genotypes, effects, (((0,), (0,)), ((), ())), preferred_element_type=jnp.float32
        ),
        "animal",
        scatter_dimension=0,
        tiled=True,
    )
    output_scale = 1.0 / math.sqrt(group_count * anim_rows)
    row_start = lax.axis_index("animal") * row_count
    own_ridge = lax.dynamic_slice_in_dim(ridge, row_start, row_count, 0)
    own_direction = lax.dynamic_slice_in_dim(direction, row_start, row_count, 0)
    return gradient * output_scale + own_ridge[:, None] * own_direction.astype(jnp.float32)


def solution(mesh):
    in_specs = (
        P("animal", "marker"),
        P("marker", None),
        P("marker"),
        P("animal", None, None),
        P("animal", None),
        P("animal"),
        P("animal", None, None, None),
    )
    out_specs = P(("marker", "animal"), None)
    return jax.shard_map(local, mesh=mesh, in_specs=in_specs, out_specs=out_specs, check_vma=False)
```

profile of v0, /device:TPU:8, one launch (start us, length us, event | category | flops | bytes accessed | tf_op | source)
XLA Modules:
  0.0 252.2 jit_solution(10962922775582331644)
XLA Ops:
  6.5 0.0 copy-start
  6.5 0.0 reduce-scatter.5.cloned.1.call-start
  6.5 1.9 copy-done
  8.5 18.8 %fusion.15 = f32[3072,256]{0,1:T(8,128)} fusion(bf16[3072,6400]{1,0:T(8,128)(2,1)} %param.7, bf16[6400,256]{1,0:T(8,128)(2,1)S(1)} %copy-done), kind=kOutput, calls=%fused_computation.23 | convolution fusion | flops 10066329600 | bytes 45744128 | tf_op jit(solution)/shard_map/dot_general | solution.py:33
  27.2 0.0 copy-start.2
  27.2 0.0 copy-start.1
  27.2 0.0 copy-start.3
  27.2 0.0 reduce-scatter.5.cloned.1.call-update
  27.3 0.6 copy-done.2
  27.9 0.1 copy.20
  28.0 0.1 reshape.64
  28.1 0.0 copy-done.1
  28.1 0.1 copy.23
  28.2 0.1 reshape.72
  28.3 60.1 %reduce-scatter.5.cloned.1.call-done = f32[3072,64]{0,1:T(8,128)} async-done(((f32[3072,256]{0,1:T(8,128)}), f32[3072,64]{0,1:T(8,128)}) %reduce-scatter.5.cloned.1.call-update) | async-done | bytes 786448 | tf_op jit(solution)/shard_map/reduce_scatter | solution.py:34
  88.4 2.0 copy_bitcast_fusion.1
  90.4 2.3 gather_fusion
  92.7 3.7 %all-to-all-start = ((bf16[8,2,128,64]{2,3,1,0:T(8,128)(2,1)}), bf16[8,2,128,64]{2,3,1,0:T(8,128)(2,1)S(1)}, u32[]{:S(2)}, u32[]{:S(2)}) async-start(bf16[8,2,128,64]{2,3,1,0:T(8,128)(2,1)} %bitcast.1), calls=%async_computation.1 | async-start | bytes 524288 | tf_op jit(solution)/shard_map/all_to_all | solution.py:17
  96.3 0.0 all-gather.2.cloned.1.call-start
  96.4 0.0 copy-done.3
  96.4 0.1 iota_compare_fusion
  96.5 6.8 %all-to-all-done = bf16[8,2,128,64]{2,3,1,0:T(8,128)(2,1)S(1)} async-done(((bf16[8,2,128,64]{2,3,1,0:T(8,128)(2,1)}), bf16[8,2,128,64]{2,3,1,0:T(8,128)(2,1)S(1)}, u32[]{:S(2)}, u32[]{:S(2)}) %all-to-all-start) | async-done | bytes 262176 | tf_op jit(solution)/shard_map/all_to_all | solution.py:17
  103.3 1.9 pad_maximum_fusion
  105.1 3.0 %gather_fusion.1 = bf16[96,128,64]{1,2,0:T(8,128)(2,1)} fusion(bf16[40,128,64]{1,2,0:T(8,128)(2,1)} %pad_maximum_fusion, s32[1024]{0:T(1024)S(1)} %pad_clamp_fusion), kind=kCustom, calls=%fused_computation.1 | custom fusion | bytes 3146112 | tf_op jit(solution)/shard_map/gather | solution.py:20
  108.2 3.6 %fusion.9 = bf16[24,8,8,128]{3,2,1,0:T(8,128)(2,1)S(1)} fusion(bf16[24,4,128,128]{3,2,1,0:T(8,128)(2,1)} %param.13, bf16[24,4,128,64]{2,3,1,0:T(8,128)(2,1)} %bitcast.33, pred[24,4]{1,0:T(8,128)(4,1)S(1)} %iota_compare_fusion), kind=kOutput, calls=%fused_computation.8 | convolution fusion | flops 202309632 | bytes 5111904 | tf_op jit(solution)/shard_map/bjrc,bjck->brk/dot_general | solution.py:22
  111.8 0.8 copy.35
  112.6 0.0 all-gather.2.cloned.1.call-update
  112.6 0.0 reduce-scatter.7.cloned.1.call-start
  112.7 34.9 %all-gather.2.cloned.1.call-done = bf16[3072,256]{0,1:T(8,128)(2,1)} async-done(((bf16[3072,64]{0,1:T(8,128)(2,1)}), bf16[3072,256]{0,1:T(8,128)(2,1)}) %all-gather.2.cloned.1.call-update) | async-done | bytes 1572880 | tf_op jit(solution)/shard_map/all_gather | solution.py:37
  147.5 19.8 %convolution_bitcast_fusion = f32[6400,256]{0,1:T(8,128)} fusion(bf16[3072,256]{0,1:T(8,128)(2,1)} %all-gather.2.cloned.1.call-done, bf16[3072,6400]{1,0:T(8,128)(2,1)} %param.7), kind=kOutput, calls=%fused_computation.2 | convolution fusion | flops 10066329600 | bytes 47448064 | tf_op jit(solution)/shard_map/dot_general | solution.py:40
  167.3 8.2 %copy.28 = f32[6400,256]{1,0:T(8,128)} copy(f32[6400,256]{0,1:T(8,128)} %convolution_bitcast_fusion) | data formatting | bytes 13107200
  175.5 0.0 reduce-scatter.7.cloned.1.call-update
  175.5 0.8 constant_dynamic-slice_fusion
  176.3 2.0 copy.30
  178.3 0.8 dynamic_slice.6
  179.0 59.5 %reduce-scatter.7.cloned.1.call-done = f32[800,256]{1,0:T(8,128)} async-done(((f32[6400,256]{1,0:T(8,128)}), f32[800,256]{1,0:T(8,128)}) %reduce-scatter.7.cloned.1.call-update) | async-done | bytes 819216
  238.6 2.4 copy.29
  241.0 2.4 multiply_add_fusion
  243.3 2.3 copy.26
  (4 shorter events, 0.0 us)
Async XLA Ops:
  6.5 1.9 copy-start
  6.5 81.9 %reduce-scatter.5.cloned.1.call-start = ((), (), s32[]{:S(2)}) async-start(), calls=%async_computation.3 | async-start | bytes 3932160 | tf_op jit(solution)/shard_map/reduce_scatter | solution.py:34
  27.2 0.7 copy-start.2
  27.2 0.8 copy-start.1
  27.2 69.1 %copy-start.3 = (s32[24]{0:T(128)S(1)}, s32[24]{0:T(128)}, u32[]{:S(2)}) copy-start(s32[24]{0:T(128)} %param.12) | copy-start | bytes 292
  92.7 10.6 %all-to-all-start = ((bf16[8,2,128,64]{2,3,1,0:T(8,128)(2,1)}), bf16[8,2,128,64]{2,3,1,0:T(8,128)(2,1)S(1)}, u32[]{:S(2)}, u32[]{:S(2)}) async-start(bf16[8,2,128,64]{2,3,1,0:T(8,128)(2,1)} %bitcast.1), calls=%async_computation.1 | async-start | bytes 524288 | tf_op jit(solution)/shard_map/all_to_all | solution.py:17
  96.3 51.2 %all-gather.2.cloned.1.call-start = ((), (), s32[]{:S(2)}) async-start(), calls=%async_computation.4 | async-start | bytes 1966080 | tf_op jit(solution)/shard_map/all_gather | solution.py:37
  112.6 125.9 %reduce-scatter.7.cloned.1.call-start = ((), (), s32[]{:S(2)}) async-start(), calls=%async_computation.5 | async-start | bytes 7372800
Sparse Core Ops, SparseCore 0:
  27.4 60.9 reduce-scatter.4
  112.7 34.7 all-gather.1
  175.6 62.8 reduce-scatter.6
where the time goes:
time: 255 us; the launch traced here: 252 us
  waiting for transfers between devices  161 us (63%)
  matrix products  42.1 us (17%)
  local copies, waits for them, and re-layouts  25.5 us (10%)
  between operations  13.2 us (5%)
  other arithmetic  6.34 us (2%)
  starting transfers between devices  3.74 us (1%)
    reduce_scatter x1, waiting for transfers between devices, local(): lax.psum_scatter(partial_value, 'marker', scatter_dimension=1, tiled=True)  60.1 us
    unnamed x4, waiting for transfers between devices  59.6 us
    all_gather x1, waiting for transfers between devices, local(): effects = lax.all_gather(relative_sum, 'marker', axis=1, tiled=True)  34.9 us
    dot_general x1, matrix products, local(): lax.dot_general(genotypes, effects, (((0,), (0,)), ((), ())), preferred_e...  19.8 us
    dot_general x1, matrix products, local(): jnp.dot(genotypes, direction, preferred_element_type=jnp.float32)  18.8 us
    unnamed x11, local copies, waits for them, and re-layouts  15.1 us
    all_to_all x1, waiting for transfers between devices, pedigree(): lax.all_to_all(outgoing, 'animal', split_axis=0, concat_axis=0, tiled=True)  6.79 us
  transfers between devices with their start and end apart: 4, of which 4 were waited for; matrix products, arithmetic and copies ran while one was open for 2% of the time, Pallas kernels for 0%

commit v1 on v0

v1 whole, which is shorter than its diff:
```python
import functools
import math

import jax
import jax.numpy as jnp
from jax import lax
from jax.experimental import pallas as pl
from jax.experimental.pallas import tpu as pltpu
from jax.sharding import PartitionSpec as P

MARKERS = 25600
BLK = 128
MARK = 16
VMEM_LIMIT = 56 * 1024 * 1024


def divisor(total, unit, most):
    best = unit
    for size in range(unit, most + 1, unit):
        if total % size == 0:
            best = size
    return best


def forward_kernel(scale, devices, place_ref, geno_ref, direction_ref, own_ref, *rest):
    sent, turned = rest[:-1], rest[-1]
    blocks, share, _ = own_ref.shape
    product = scale * jnp.dot(geno_ref[...], direction_ref[...], preferred_element_type=jnp.float32)
    largest = jnp.max(jnp.abs(product), axis=(0, 1), keepdims=True)
    power = jnp.clip(jnp.ceil(jnp.log2(largest)), -100.0, 120.0)
    grow = jnp.exp2(14.0 - power)
    turned[...] = product.T
    for shift in range(devices):
        first = pl.multiple_of(lax.rem(place_ref[0] + shift, devices) * share, share)
        for b in range(blocks):
            piece = turned[pl.ds(first, share), b * BLK : (b + 1) * BLK]
            if shift == 0:
                own_ref[b] = piece
            else:
                coded = jnp.round(piece * grow).astype(jnp.int32).astype(jnp.int16)
                sent[shift - 1][b * share : (b + 1) * share] = coded
        if shift > 0:
            mark = jnp.broadcast_to(power, (MARK, BLK)).astype(jnp.int32).astype(jnp.int16)
            sent[shift - 1][blocks * share :] = mark


def forward_product(genotypes, direction, place, devices, scale, first, rows, tile):
    depth, cols = direction.shape
    start = first // tile
    share = cols // devices
    blocks = tile // BLK
    coded = blocks * share + MARK
    steps = rows // tile
    return pl.pallas_call(
        functools.partial(forward_kernel, scale, devices),
        grid_spec=pltpu.PrefetchScalarGridSpec(
            num_scalar_prefetch=1,
            grid=(steps,),
            in_specs=[
                pl.BlockSpec((tile, depth), lambda i, *_: (start + i, 0)),
                pl.BlockSpec((depth, cols), lambda i, *_: (0, 0), pipeline_mode=pl.Buffered(1)),
            ],
            out_specs=[pl.BlockSpec((blocks, share, BLK), lambda i, *_: (i, 0, 0))]
            + [pl.BlockSpec((coded, BLK), lambda i, *_: (i, 0))] * (devices - 1),
            scratch_shapes=[pltpu.VMEM((cols, tile), jnp.float32)],
        ),
        out_shape=[jax.ShapeDtypeStruct((steps * blocks, share, BLK), jnp.float32)]
        + [jax.ShapeDtypeStruct((steps * coded, BLK), jnp.int16)] * (devices - 1),
        compiler_params=pltpu.CompilerParams(vmem_limit_bytes=VMEM_LIMIT),
        cost_estimate=pl.CostEstimate(
            flops=2 * rows * depth * cols,
            bytes_accessed=2 * (rows + cols) * depth + 2 * rows * cols,
            transcendentals=0,
        ),
        name="forward_product",
    )(place, genotypes, direction)


def settle_kernel(parts, blocks, list_ref, *refs):
    owns, coded, (sum_ref, out_ref) = refs[:parts], refs[parts:-2], refs[-2:]
    share = sum_ref.shape[1]
    size = blocks * share + MARK
    at = 0
    for part, own in enumerate(owns):
        for step in range(own.shape[0] // blocks):
            row = step * size
            total = own[step * blocks : (step + 1) * blocks]
            for ref in coded[part::parts]:
                power = ref[row + blocks * share : row + size].astype(jnp.float32)[:1]
                steps = ref[row : row + blocks * share].astype(jnp.float32)
                total = total + (steps * jnp.exp2(power - 14.0)).reshape(blocks, share, BLK)
            sum_ref[at : at + blocks] = total.astype(sum_ref.dtype)
            at += blocks
    for i in range(out_ref.shape[0]):
        out_ref[i] = sum_ref[list_ref[i]]


def settle(owns, coded, send_list, blocks):
    block_total = sum(own.shape[0] for own in owns)
    share = owns[0].shape[1]
    sends = send_list.size
    flat = [ref for one in coded for ref in one]
    return pl.pallas_call(
        functools.partial(settle_kernel, len(owns), blocks),
        grid_spec=pltpu.PrefetchScalarGridSpec(
            num_scalar_prefetch=1,
            grid=(1,),
            in_specs=[pl.BlockSpec(x.shape, lambda i, *_, n=x.ndim: (0,) * n) for x in (*owns, *flat)],
            out_specs=[
                pl.BlockSpec((block_total, share, BLK), lambda i, *_: (0, 0, 0)),
                pl.BlockSpec((sends, share, BLK), lambda i, *_: (0, 0, 0)),
            ],
        ),
        out_shape=[
            jax.ShapeDtypeStruct((block_total, share, BLK), jnp.bfloat16),
            jax.ShapeDtypeStruct((sends, share, BLK), jnp.bfloat16),
        ],
        compiler_params=pltpu.CompilerParams(vmem_limit_bytes=VMEM_LIMIT),
        name="settle",
    )(send_list.reshape(-1), *owns, *flat)


def pedigree_kernel(group, own_total, index_ref, count_ref, own_ref, far_ref, prec_ref, out_ref, table):
    step = pl.program_id(0)

    @pl.when(step == 0)
    def _():
        table[:own_total] = own_ref[...]
        table[own_total:] = far_ref[...]

    for b in range(group):
        block = step * group + b
        total = None
        for j in range(prec_ref.shape[1]):
            source = table[index_ref[block, j]]
            source = jnp.where(j < count_ref[block], source, jnp.zeros_like(source))
            term = lax.dot_general(
                source, prec_ref[b, j], (((1,), (1,)), ((), ())), preferred_element_type=jnp.float32
            )
            total = term if total is None else total + term
        out_ref[b] = total.astype(out_ref.dtype)


def pedigree(blocked, incoming, rel_index, rel_count, rel_prec):
    block_total, share, _ = blocked.shape
    far_total = incoming.shape[0]
    slots = rel_prec.shape[1]
    group = divisor(block_total, 1, 6)
    return pl.pallas_call(
        functools.partial(pedigree_kernel, group, block_total),
        grid_spec=pltpu.PrefetchScalarGridSpec(
            num_scalar_prefetch=2,
            grid=(block_total // group,),
            in_specs=[
                pl.BlockSpec((block_total, share, BLK), lambda i, *_: (0, 0, 0), pipeline_mode=pl.Buffered(1)),
                pl.BlockSpec((far_total, share, BLK), lambda i, *_: (0, 0, 0), pipeline_mode=pl.Buffered(1)),
                pl.BlockSpec((group, slots, BLK, BLK), lambda i, *_: (i, 0, 0, 0)),
            ],
            out_specs=pl.BlockSpec((group, share, BLK), lambda i, *_: (i, 0, 0)),
            scratch_shapes=[pltpu.VMEM((block_total + far_total, share, BLK), jnp.bfloat16)],
        ),
        out_shape=jax.ShapeDtypeStruct(blocked.shape, jnp.bfloat16),
        compiler_params=pltpu.CompilerParams(vmem_limit_bytes=VMEM_LIMIT),
        name="pedigree",
    )(rel_index, rel_count, blocked, incoming, rel_prec)


def backward_kernel(scale, devices, place_ref, geno_ref, *refs):
    shares, (low_ref, high_ref, effects) = refs[:devices], refs[devices:]
    half = low_ref.shape[1]
    blocks, share, _ = shares[0].shape

    @pl.when(pl.program_id(0) == 0)
    def _():
        for shift in range(devices):
            origin = lax.rem(place_ref[0] + devices - shift, devices)
            first = pl.multiple_of(origin * share, share)
            for b in range(blocks):
                effects[pl.ds(first, share), b * BLK : (b + 1) * BLK] = shares[shift][b]

    product = scale * jnp.dot(effects[...], geno_ref[...], preferred_element_type=jnp.float32).T
    low_ref[...] = product[:, :half]
    high_ref[...] = product[:, half:]


def backward_product(genotypes, shares, place, scale):
    rows, width = genotypes.shape
    devices = len(shares)
    cols = devices * shares[0].shape[1]
    tile = divisor(width, 2 * BLK, 5 * BLK)
    return pl.pallas_call(
        functools.partial(backward_kernel, scale, devices),
        grid_spec=pltpu.PrefetchScalarGridSpec(
            num_scalar_prefetch=1,
            grid=(width // tile,),
            in_specs=[pl.BlockSpec((rows, tile), lambda i, *_: (0, i))]
            + [pl.BlockSpec(s.shape, lambda i, *_: (0, 0, 0), pipeline_mode=pl.Buffered(1)) for s in shares],
            out_specs=[pl.BlockSpec((tile, cols // 2), lambda i, *_: (i, 0))] * 2,
            scratch_shapes=[pltpu.VMEM((cols, rows), jnp.bfloat16)],
        ),
        out_shape=[jax.ShapeDtypeStruct((width, cols // 2), jnp.float32)] * 2,
        compiler_params=pltpu.CompilerParams(vmem_limit_bytes=VMEM_LIMIT),
        cost_estimate=pl.CostEstimate(
            flops=2 * rows * width * cols,
            bytes_accessed=2 * rows * (width + cols) + 4 * width * cols,
            transcendentals=0,
        ),
        name="backward_product",
    )(place, genotypes, *shares)


def turn(value, devices, shift):
    return lax.ppermute(value, "marker", [(d, (d + shift) % devices) for d in range(devices)])


def halving_sum(blocks, devices, bits):
    levels = devices.bit_length() - 1
    here = lax.axis_index("animal")
    total = blocks.reshape((2,) * levels + blocks.shape[1:])
    left = list(range(levels - 1, -1, -1))
    for bit in bits:
        axis = left.index(bit)
        mine = (here >> bit) & 1
        sent = lax.dynamic_index_in_dim(total, 1 - mine, axis, keepdims=False)
        kept = lax.dynamic_index_in_dim(total, mine, axis, keepdims=False)
        pairs = [(d, d ^ (1 << bit)) for d in range(devices)]
        got = lax.ppermute(sent.astype(jnp.bfloat16), "animal", pairs)
        total = kept + got.astype(jnp.float32)
        left.pop(axis)
    return total


def local(genotypes, direction, ridge, send_list, rel_index, rel_count, rel_prec):
    rows, width = genotypes.shape
    half = direction.shape[1] // 2
    groups = lax.axis_size("animal")
    devices = lax.axis_size("marker")
    place = lax.axis_index("marker").reshape(1)
    parts = 2
    part_rows = rows // parts
    tile = divisor(part_rows, BLK, 4 * BLK)

    owns, coded = [], [[] for _ in range(1, devices)]
    for part in range(parts):
        own, *sent = forward_product(
            genotypes, direction, place, devices, 1.0 / math.sqrt(MARKERS), part * part_rows, part_rows, tile
        )
        owns.append(own)
        for shift in range(1, devices):
            coded[shift - 1].append(turn(sent[shift - 1], devices, shift))
    own, outgoing = settle(owns, coded, send_list, tile // BLK)

    share = own.shape[1]
    outgoing = outgoing.reshape(groups, -1, share, BLK)
    incoming = lax.all_to_all(outgoing, "animal", split_axis=0, concat_axis=0, tiled=True)
    incoming = incoming.reshape(-1, share, BLK)
    relative = pedigree(own, incoming, rel_index, rel_count, rel_prec)
    shares = [relative] + [turn(relative, devices, shift) for shift in range(1, devices)]

    own_rows = width // groups
    low, high = [
        product.reshape(groups, own_rows, half)
        for product in backward_product(genotypes, shares, place, 1.0 / math.sqrt(groups * rows))
    ]
    levels = list(range(groups.bit_length() - 1))
    gradient = jnp.concatenate(
        [
            halving_sum(low, groups, levels),
            halving_sum(high, groups, levels[:1] + levels[:0:-1]),
        ],
        axis=1,
    )
    start = lax.axis_index("animal") * own_rows
    own_ridge = lax.dynamic_slice_in_dim(ridge, start, own_rows, 0)
    own_direction = lax.dynamic_slice_in_dim(direction, start, own_rows, 0)
    return gradient + own_ridge[:, None] * own_direction.astype(jnp.float32)


def solution(mesh):
    in_specs = (
        P("animal", "marker"),
        P("marker", None),
        P("marker"),
        P("animal", None, None),
        P("animal", None),
        P("animal"),
        P("animal", None, None, None),
    )
    out_specs = P(("marker", "animal"), None)
    return jax.shard_map(local, mesh=mesh, in_specs=in_specs, out_specs=out_specs, check_vma=False)
```

time: 255 us -> 180 us (0.71)
  waiting for transfers between devices: 161 us -> 79 us
  Pallas kernels: 0 us -> 62.4 us
  matrix products: 42.1 us -> 0 us
  starting transfers between devices: 3.74 us -> 20.2 us
  local copies, waits for them, and re-layouts: 25.5 us -> 9.12 us
  between operations: 13.2 us -> 0.11 us
    ppermute x0 -> x15, waiting for transfers between devices: none -> 72.7 us  [the longest x9 58.5 us: turn(): lax.ppermute(value, 'marker', [(d, (d + shift) % devices) for d in range(...]
    pallas_call x0 -> x5, Pallas kernels: none -> 62.4 us  [the longest x1 30 us: backward_product(): pl.pallas_call(functools.partial(backward_kernel, scale, devices), grid_s...]
    reduce_scatter x1 -> x0, waiting for transfers between devices: 60.1 us -> none  [local(): lax.psum_scatter(partial_value, 'marker', scatter_dimension=1, tiled=True)]
    unnamed x4 -> x0, waiting for transfers between devices: 59.6 us -> none
    dot_general x3 -> x0, matrix products: 42.1 us -> none  [the longest x1 19.8 us: local(): lax.dot_general(genotypes, effects, (((0,), (0,)), ((), ())), preferred_e...]
    all_gather x1 -> x0, waiting for transfers between devices: 34.9 us -> none  [local(): effects = lax.all_gather(relative_sum, 'marker', axis=1, tiled=True)]
    ppermute x0 -> x15, starting transfers between devices: none -> 16.5 us  [the longest x9 12.7 us: turn(): lax.ppermute(value, 'marker', [(d, (d + shift) % devices) for d in range(...]
    unnamed x11 -> x32, local copies, waits for them, and re-layouts: 15.1 us -> 2.91 us
  transfers between devices with their start and end apart: 4 -> 16, of which waited for: 4 -> 13; matrix products, arithmetic and copies ran while one was open for 2% -> 6% of each run, Pallas kernels for 0% -> 6%
where the time goes in v1:
time: 180 us; the launch traced here: 179 us
  waiting for transfers between devices  79 us (44%)
  Pallas kernels  62.4 us (35%)
  starting transfers between devices  20.2 us (11%)
  local copies, waits for them, and re-layouts  9.12 us (5%)
  other arithmetic  7.62 us (4%)
    ppermute x9, waiting for transfers between devices, turn(): lax.ppermute(value, 'marker', [(d, (d + shift) % devices) for d in range(...  58.5 us
    pallas_call x1, Pallas kernels, backward_product(): pl.pallas_call(functools.partial(backward_kernel, scale, devices), grid_s...  30 us
    pallas_call x2, Pallas kernels, forward_product(): pl.pallas_call(functools.partial(forward_kernel, scale, devices), grid_sp...  23.1 us
    ppermute x6, waiting for transfers between devices, halving_sum(): got = lax.ppermute(sent.astype(jnp.bfloat16), 'animal', pairs)  14.3 us
    ppermute x9, starting transfers between devices, turn(): lax.ppermute(value, 'marker', [(d, (d + shift) % devices) for d in range(...  12.7 us
    all_to_all x1, waiting for transfers between devices, local(): lax.all_to_all(outgoing, 'animal', split_axis=0, concat_axis=0, tiled=True)  6.25 us
    pallas_call x1, Pallas kernels, pedigree(): pl.pallas_call(functools.partial(pedigree_kernel, group, block_total), gr...  5.97 us
    add x6, other arithmetic, halving_sum(): total = kept + got.astype(jnp.float32)  5.54 us
  transfers between devices with their start and end apart: 16, of which 13 were waited for; matrix products, arithmetic and copies ran while one was open for 6% of the time, Pallas kernels for 6%

profile of v1, /device:TPU:8, one launch (start us, length us, event | category | flops | bytes accessed | tf_op | source)
XLA Modules:
  0.0 178.5 jit_solution(232414664077438219)
XLA Ops:
  0.0 11.6 %forward_product.2 = (f32[12,64,128]{2,1,0:T(8,128)}, s16[816,128]{1,0:T(8,128)(2,1)}, s16[816,128]{1,0:T(8,128)(2,1)}, s16[816,128]{1,0:T(8,128)(2,1)}) custom-call(s32[1]{0:T(128)} %bitcast.place_ref, bf16[3072,6400]{1,0:T(8,128)(2,1)} %geno_ref.5, bf16[6400,256]{1,0:T(8,128)(2,1)} %direction_ref.3), custom_call_target="tpu_custom_call" | custom-call | flops 5033164800 | bytes 23724032 | tf_op jit(solution)/shard_map/forward_product/pallas_call | solution.py:54
  11.6 0.0 copy-start.12
  11.6 1.6 collective-permute-start
  13.2 11.6 %forward_product.3 = (f32[12,64,128]{2,1,0:T(8,128)}, s16[816,128]{1,0:T(8,128)(2,1)}, s16[816,128]{1,0:T(8,128)(2,1)}, s16[816,128]{1,0:T(8,128)(2,1)}) custom-call(s32[1]{0:T(128)} %bitcast.place_ref, bf16[3072,6400]{1,0:T(8,128)(2,1)} %geno_ref.5, bf16[6400,256]{1,0:T(8,128)(2,1)} %direction_ref.3), custom_call_target="tpu_custom_call" | custom-call | flops 5033164800 | bytes 23724032 | tf_op jit(solution)/shard_map/forward_product/pallas_call | solution.py:54
  24.8 1.6 collective-permute-start.1
  26.4 0.0 copy-done.14
  26.4 1.2 collective-permute-start.2
  27.6 1.7 collective-permute-start.3
  29.3 0.0 copy-done.13
  29.3 0.5 collective-permute-start.4
  29.8 0.0 collective-permute-done.refs_2_
  29.8 2.2 %collective-permute-start.5 = (s16[816,128]{1,0:T(8,128)(2,1)}, s16[816,128]{1,0:T(8,128)(2,1)S(1)}, u32[]{:S(2)}, u32[]{:S(2)}) collective-permute-start(s16[816,128]{1,0:T(8,128)(2,1)} %get-tuple-element.24), channel_id=1, source_target_pairs={{0,3},{1,0},{2,1},{3,2},{4,7},{5,4},{6,5},{7,6},{8,11},{9,8},{10,9... | collective-permute-start | bytes 626696 | tf_op jit(solution)/shard_map/ppermute | solution.py:213
  32.0 0.0 copy-done.12
  32.0 0.1 copy.13
  32.1 0.7 reshape.20.list_ref
  32.8 17.5 %collective-permute-done.1.refs_3_ = s16[816,128]{1,0:T(8,128)(2,1)S(1)} collective-permute-done((s16[816,128]{1,0:T(8,128)(2,1)}, s16[816,128]{1,0:T(8,128)(2,1)S(1)}, u32[]{:S(2)}, u32[]{:S(2)}) %collective-permute-start.1) | collective-permute-done | bytes 208928 | tf_op jit(solution)/shard_map/ppermute | solution.py:213
  50.2 4.4 %collective-permute-done.2.refs_4_ = s16[816,128]{1,0:T(8,128)(2,1)S(1)} collective-permute-done((s16[816,128]{1,0:T(8,128)(2,1)S(1)}, s16[816,128]{1,0:T(8,128)(2,1)S(1)}, u32[]{:S(2)}, u32[]{:S(2)}) %collective-permute-start.2) | collective-permute-done | bytes 208928 | tf_op jit(solution)/shard_map/ppermute | solution.py:213
  54.6 3.1 %collective-permute-done.3.refs_5_ = s16[816,128]{1,0:T(8,128)(2,1)S(1)} collective-permute-done((s16[816,128]{1,0:T(8,128)(2,1)}, s16[816,128]{1,0:T(8,128)(2,1)S(1)}, u32[]{:S(2)}, u32[]{:S(2)}) %collective-permute-start.3) | collective-permute-done | bytes 208928 | tf_op jit(solution)/shard_map/ppermute | solution.py:213
  57.7 0.0 collective-permute-done.4.refs_6_
  57.7 1.6 collective-permute-done.5.refs_7_
  59.3 0.0 copy-done.5
  59.3 0.0 copy-done.6
  59.3 0.0 copy-done.7
  59.3 0.0 copy-done.8
  59.3 0.0 copy-done.9
  59.3 0.7 copy-done.10
  60.0 3.4 %settle.1 = (bf16[24,64,128]{2,1,0:T(8,128)(2,1)}, bf16[16,64,128]{2,1,0:T(8,128)(2,1)}) custom-call(s32[16]{0:T(128)} %reshape.20.list_ref, f32[12,64,128]{2,1,0:T(8,128)} %get-tuple-element.17.refs_0_, f32[12,64,128]{2,1,0:T(8,128)} %get-tuple-element.18.refs_1_, s16[816,128]{1,0:T(8,128)(2,1)} %copy-done.5, s16[816,128]{1,0:T(8,128)(2,1)} %copy-done.6, ...), custom_call_target="tpu_custom_call" | custom-call | tf_op jit(solution)/shard_map/settle/pallas_call | solution.py:103
  63.4 3.7 %all-to-all-start = ((bf16[8,2,64,128]{3,2,1,0:T(8,128)(2,1)}), bf16[8,2,64,128]{3,2,1,0:T(8,128)(2,1)S(1)}, u32[]{:S(2)}, u32[]{:S(2)}) async-start(bf16[8,2,64,128]{3,2,1,0:T(8,128)(2,1)} %bitcast.38), calls=%async_computation | async-start | bytes 524288 | tf_op jit(solution)/shard_map/all_to_all | solution.py:255
  67.1 0.7 copy.14.index_ref
  67.8 6.3 %all-to-all-done = bf16[8,2,64,128]{3,2,1,0:T(8,128)(2,1)S(1)} async-done(((bf16[8,2,64,128]{3,2,1,0:T(8,128)(2,1)}), bf16[8,2,64,128]{3,2,1,0:T(8,128)(2,1)S(1)}, u32[]{:S(2)}, u32[]{:S(2)}) %all-to-all-start) | async-done | bytes 262176 | tf_op jit(solution)/shard_map/all_to_all | solution.py:255
  74.0 0.7 copy-done.1
  74.7 6.0 %pedigree.1.refs_0_ = bf16[24,64,128]{2,1,0:T(8,128)(2,1)} custom-call(s32[24,4]{1,0:T(8,128)} %copy.14.index_ref, s32[24]{0:T(128)} %count_ref.1, bf16[24,64,128]{2,1,0:T(8,128)(2,1)} %get-tuple-element.25.own_ref, bf16[16,64,128]{2,1,0:T(8,128)(2,1)} %bitcast.37, bf16[24,4,128,128]{3,2,1,0:T(8,128)(2,1)} %prec_ref.1), custom_call_target="tpu_custom_call" | custom-call | tf_op jit(solution)/shard_map/pedigree/pallas_call | solution.py:149
  80.7 0.0 collective-permute-start.6
  80.7 1.8 %collective-permute-start.7 = (bf16[24,64,128]{2,1,0:T(8,128)(2,1)}, bf16[24,64,128]{2,1,0:T(8,128)(2,1)S(1)}, u32[]{:S(2)}, u32[]{:S(2)}) collective-permute-start(bf16[24,64,128]{2,1,0:T(8,128)(2,1)} %pedigree.1.refs_0_), channel_id=1, source_target_pairs={{0,2},{1,3},{2,0},{3,1},{4,6},{5,7},{6,4},{7,5},{8,10},{9,11},{10,... | collective-permute-start | bytes 1179656 | tf_op jit(solution)/shard_map/ppermute | solution.py:213
  82.5 2.0 %collective-permute-start.8 = (bf16[24,64,128]{2,1,0:T(8,128)(2,1)}, bf16[24,64,128]{2,1,0:T(8,128)(2,1)S(1)}, u32[]{:S(2)}, u32[]{:S(2)}) collective-permute-start(bf16[24,64,128]{2,1,0:T(8,128)(2,1)} %pedigree.1.refs_0_), channel_id=1, source_target_pairs={{0,3},{1,0},{2,1},{3,2},{4,7},{5,4},{6,5},{7,6},{8,11},{9,8},{10,9... | collective-permute-start | bytes 1179656 | tf_op jit(solution)/shard_map/ppermute | solution.py:213
  84.6 8.4 %collective-permute-done.6.refs_1_ = bf16[24,64,128]{2,1,0:T(8,128)(2,1)S(1)} collective-permute-done((bf16[24,64,128]{2,1,0:T(8,128)(2,1)}, bf16[24,64,128]{2,1,0:T(8,128)(2,1)S(1)}, u32[]{:S(2)}, u32[]{:S(2)}) %collective-permute-start.6) | collective-permute-done | bytes 393248 | tf_op jit(solution)/shard_map/ppermute | solution.py:213
  93.0 21.3 %collective-permute-done.7.refs_2_ = bf16[24,64,128]{2,1,0:T(8,128)(2,1)S(1)} collective-permute-done((bf16[24,64,128]{2,1,0:T(8,128)(2,1)}, bf16[24,64,128]{2,1,0:T(8,128)(2,1)S(1)}, u32[]{:S(2)}, u32[]{:S(2)}) %collective-permute-start.7) | collective-permute-done | bytes 393248 | tf_op jit(solution)/shard_map/ppermute | solution.py:213
  114.3 2.2 %collective-permute-done.8.refs_3_ = bf16[24,64,128]{2,1,0:T(8,128)(2,1)S(1)} collective-permute-done((bf16[24,64,128]{2,1,0:T(8,128)(2,1)}, bf16[24,64,128]{2,1,0:T(8,128)(2,1)S(1)}, u32[]{:S(2)}, u32[]{:S(2)}) %collective-permute-start.8) | collective-permute-done | bytes 393248 | tf_op jit(solution)/shard_map/ppermute | solution.py:213
  116.5 0.0 copy-done.3
  116.5 0.8 copy-done.4
  117.3 30.0 %backward_product.1 = (f32[6400,128]{1,0:T(8,128)}, f32[6400,128]{1,0:T(8,128)}) custom-call(s32[1]{0:T(128)} %bitcast.place_ref, bf16[3072,6400]{1,0:T(8,128)(2,1)} %geno_ref.5, bf16[24,64,128]{2,1,0:T(8,128)(2,1)} %pedigree.1.refs_0_, bf16[24,64,128]{2,1,0:T(8,128)(2,1)} %copy-done.2, bf16[24,64,128]{2,1,0:T(8,128)(2,1)} %copy-done.3, ...), custom_call_target="tpu_custom_call" | custom-call | flops 10066329600 | bytes 47448064 | tf_op jit(solution)/shard_map/backward_product/pallas_call | solution.py:191
  147.2 1.5 fusion
  148.8 0.1 collective-permute-start.9
  148.9 1.5 fusion.1
  150.4 0.5 collective-permute-start.12
  151.0 0.3 collective-permute-done.9
  151.3 2.0 %bitcast_add_fusion.1 = f32[2,2,800,128]{3,2,0,1:T(8,128)S(1)} fusion(bf16[2,2,800,128]{3,2,0,1:T(8,128)(2,1)} %collective-permute-done.9, f32[2,2,2,800,128]{4,3,2,1,0:T(8,128)} %bitcast.36, s32[]{:T(128)S(6)} %select_n.32), kind=kLoop, calls=%fused_computation.3 | loop fusion | flops 819200 | bytes 4096004 | tf_op jit(solution)/shard_map/add | solution.py:228
  153.3 0.8 fusion.2
  154.1 1.3 collective-permute-start.10
  155.4 0.0 collective-permute-done.12
  155.4 0.0 copy-done
  155.4 1.3 bitcast_add_fusion
  156.8 0.8 fusion.3
  157.6 0.4 collective-permute-start.13
  158.0 0.8 dynamic_slice.58
  158.8 7.2 %collective-permute-done.10 = bf16[2,800,128]{2,1,0:T(8,128)(2,1)} collective-permute-done((bf16[2,800,128]{2,1,0:T(8,128)(2,1)}, bf16[2,800,128]{2,1,0:T(8,128)(2,1)}, u32[]{:S(2)}, u32[]{:S(2)}) %collective-permute-start.10) | collective-permute-done | bytes 409632 | tf_op jit(solution)/shard_map/ppermute | solution.py:227
  166.0 1.1 bitcast_add_fusion.3
  167.1 0.6 collective-permute-start.11
  167.7 1.4 collective-permute-done.13
  169.2 1.1 bitcast_add_fusion.2
  170.3 0.8 collective-permute-start.14
  171.1 2.4 %collective-permute-done.11 = bf16[800,128]{1,0:T(8,128)(2,1)S(1)} collective-permute-done((bf16[800,128]{1,0:T(8,128)(2,1)S(1)}, bf16[800,128]{1,0:T(8,128)(2,1)S(1)}, u32[]{:S(2)}, u32[]{:S(2)}) %collective-permute-start.11) | collective-permute-done | bytes 204832 | tf_op jit(solution)/shard_map/ppermute | solution.py:227
  173.6 2.8 %collective-permute-done.14 = bf16[800,128]{1,0:T(8,128)(2,1)S(1)} collective-permute-done((bf16[800,128]{1,0:T(8,128)(2,1)S(1)}, bf16[800,128]{1,0:T(8,128)(2,1)S(1)}, u32[]{:S(2)}, u32[]{:S(2)}) %collective-permute-start.14) | collective-permute-done | bytes 204832 | tf_op jit(solution)/shard_map/ppermute | solution.py:227
  176.4 2.1 %maximum_add_fusion = f32[800,256]{1,0:T(8,128)} fusion(f32[800,128]{1,0:T(8,128)S(1)} %bitcast_add_fusion.4, f32[800,128]{1,0:T(8,128)S(1)} %bitcast_add_fusion.5, bf16[6400,256]{1,0:T(8,128)(2,1)} %direction_ref.3, s32[]{:T(128)S(6)} %select_n.38, f32[800]{0:T(1024)S(1)} %dynamic_slice.58), kind=kLoop, calls=%fused_computation.6 | loop fusion | flops 819200 | bytes 2051204 | tf_op jit(solution)/shard_map/add | solution.py:276
  (20 shorter events, 0.2 us)
Async XLA Ops:
  11.6 14.8 %copy-start.14 = (s16[816,128]{1,0:T(8,128)(2,1)S(1)}, s16[816,128]{1,0:T(8,128)(2,1)}, u32[]{:S(2)}) copy-start(s16[816,128]{1,0:T(8,128)(2,1)} %get-tuple-element.21) | copy-start | bytes 626692
  11.6 17.7 %copy-start.13 = (s16[816,128]{1,0:T(8,128)(2,1)S(1)}, s16[816,128]{1,0:T(8,128)(2,1)}, u32[]{:S(2)}) copy-start(s16[816,128]{1,0:T(8,128)(2,1)} %get-tuple-element.23) | copy-start | bytes 626692
  11.6 20.4 %copy-start.12 = (s32[1,8,2]{1,2,0:T(2,128)S(1)}, s32[1,8,2]{1,2,0:T(2,128)}, u32[]{:S(2)}) copy-start(s32[1,8,2]{1,2,0:T(2,128)} %param.10) | copy-start | bytes 196
  11.6 18.2 %collective-permute-start = (s16[816,128]{1,0:T(8,128)(2,1)}, s16[816,128]{1,0:T(8,128)(2,1)S(1)}, u32[]{:S(2)}, u32[]{:S(2)}) collective-permute-start(s16[816,128]{1,0:T(8,128)(2,1)} %get-tuple-element.19), channel_id=1, source_target_pairs={{0,1},{1,2},{2,3},{3,0},{4,5},{5,6},{6,7},{7,4},{8,9},{9,10},{10,1... | collective-permute-start | bytes 626696 | tf_op jit(solution)/shard_map/ppermute | solution.py:213
  24.8 42.3 %copy-start.11 = (s32[24,4]{0,1:T(4,128)S(1)}, s32[24,4]{0,1:T(4,128)}, u32[]{:S(2)}) copy-start(s32[24,4]{0,1:T(4,128)} %param.11) | copy-start | bytes 1156
  24.8 25.4 %collective-permute-start.1 = (s16[816,128]{1,0:T(8,128)(2,1)}, s16[816,128]{1,0:T(8,128)(2,1)S(1)}, u32[]{:S(2)}, u32[]{:S(2)}) collective-permute-start(s16[816,128]{1,0:T(8,128)(2,1)} %get-tuple-element.20), channel_id=1, source_target_pairs={{0,1},{1,2},{2,3},{3,0},{4,5},{5,6},{6,7},{7,4},{8,9},{9,10},{10,1... | collective-permute-start | bytes 626696 | tf_op jit(solution)/shard_map/ppermute | solution.py:213
  26.4 28.2 %collective-permute-start.2 = (s16[816,128]{1,0:T(8,128)(2,1)S(1)}, s16[816,128]{1,0:T(8,128)(2,1)S(1)}, u32[]{:S(2)}, u32[]{:S(2)}) collective-permute-start(s16[816,128]{1,0:T(8,128)(2,1)S(1)} %copy-done.14), channel_id=1, source_target_pairs={{0,2},{1,3},{2,0},{3,1},{4,6},{5,7},{6,4},{7,5},{8,10},{9,11},{10,... | collective-permute-start | bytes 626696 | tf_op jit(solution)/shard_map/ppermute | solution.py:213
  27.6 30.1 %collective-permute-start.3 = (s16[816,128]{1,0:T(8,128)(2,1)}, s16[816,128]{1,0:T(8,128)(2,1)S(1)}, u32[]{:S(2)}, u32[]{:S(2)}) collective-permute-start(s16[816,128]{1,0:T(8,128)(2,1)} %get-tuple-element.22), channel_id=1, source_target_pairs={{0,2},{1,3},{2,0},{3,1},{4,6},{5,7},{6,4},{7,5},{8,10},{9,11},{10,... | collective-permute-start | bytes 626696 | tf_op jit(solution)/shard_map/ppermute | solution.py:213
  29.3 28.4 %collective-permute-start.4 = (s16[816,128]{1,0:T(8,128)(2,1)S(1)}, s16[816,128]{1,0:T(8,128)(2,1)S(1)}, u32[]{:S(2)}, u32[]{:S(2)}) collective-permute-start(s16[816,128]{1,0:T(8,128)(2,1)S(1)} %copy-done.13), channel_id=1, source_target_pairs={{0,3},{1,0},{2,1},{3,2},{4,7},{5,4},{6,5},{7,6},{8,11},{9,8},{10,9... | collective-permute-start | bytes 626696 | tf_op jit(solution)/shard_map/ppermute | solution.py:213
  29.8 29.5 %copy-start.5 = (s16[816,128]{1,0:T(8,128)(2,1)}, s16[816,128]{1,0:T(8,128)(2,1)S(1)}, u32[]{:S(2)}) copy-start(s16[816,128]{1,0:T(8,128)(2,1)S(1)} %collective-permute-done.refs_2_) | copy-start | bytes 626692
  29.8 29.5 %collective-permute-start.5 = (s16[816,128]{1,0:T(8,128)(2,1)}, s16[816,128]{1,0:T(8,128)(2,1)S(1)}, u32[]{:S(2)}, u32[]{:S(2)}) collective-permute-start(s16[816,128]{1,0:T(8,128)(2,1)} %get-tuple-element.24), channel_id=1, source_target_pairs={{0,3},{1,0},{2,1},{3,2},{4,7},{5,4},{6,5},{7,6},{8,11},{9,8},{10,9... | collective-permute-start | bytes 626696 | tf_op jit(solution)/shard_map/ppermute | solution.py:213
  50.2 9.1 %copy-start.6 = (s16[816,128]{1,0:T(8,128)(2,1)}, s16[816,128]{1,0:T(8,128)(2,1)S(1)}, u32[]{:S(2)}) copy-start(s16[816,128]{1,0:T(8,128)(2,1)S(1)} %collective-permute-done.1.refs_3_) | copy-start | bytes 626692
  54.6 4.7 %copy-start.7 = (s16[816,128]{1,0:T(8,128)(2,1)}, s16[816,128]{1,0:T(8,128)(2,1)S(1)}, u32[]{:S(2)}) copy-start(s16[816,128]{1,0:T(8,128)(2,1)S(1)} %collective-permute-done.2.refs_4_) | copy-start | bytes 626692
  57.7 1.6 copy-start.8
  57.7 1.6 copy-start.9
  59.3 0.7 copy-start.10
  63.4 10.7 %all-to-all-start = ((bf16[8,2,64,128]{3,2,1,0:T(8,128)(2,1)}), bf16[8,2,64,128]{3,2,1,0:T(8,128)(2,1)S(1)}, u32[]{:S(2)}, u32[]{:S(2)}) async-start(bf16[8,2,64,128]{3,2,1,0:T(8,128)(2,1)} %bitcast.38), calls=%async_computation | async-start | bytes 524288 | tf_op jit(solution)/shard_map/all_to_all | solution.py:255
  74.0 0.7 copy-start.1
  80.7 12.3 %collective-permute-start.6 = (bf16[24,64,128]{2,1,0:T(8,128)(2,1)}, bf16[24,64,128]{2,1,0:T(8,128)(2,1)S(1)}, u32[]{:S(2)}, u32[]{:S(2)}) collective-permute-start(bf16[24,64,128]{2,1,0:T(8,128)(2,1)} %pedigree.1.refs_0_), channel_id=1, source_target_pairs={{0,1},{1,2},{2,3},{3,0},{4,5},{5,6},{6,7},{7,4},{8,9},{9,10},{10,1... | collective-permute-start | bytes 1179656 | tf_op jit(solution)/shard_map/ppermute | solution.py:213
  80.7 33.6 %collective-permute-start.7 = (bf16[24,64,128]{2,1,0:T(8,128)(2,1)}, bf16[24,64,128]{2,1,0:T(8,128)(2,1)S(1)}, u32[]{:S(2)}, u32[]{:S(2)}) collective-permute-start(bf16[24,64,128]{2,1,0:T(8,128)(2,1)} %pedigree.1.refs_0_), channel_id=1, source_target_pairs={{0,2},{1,3},{2,0},{3,1},{4,6},{5,7},{6,4},{7,5},{8,10},{9,11},{10,... | collective-permute-start | bytes 1179656 | tf_op jit(solution)/shard_map/ppermute | solution.py:213
  82.5 34.0 %collective-permute-start.8 = (bf16[24,64,128]{2,1,0:T(8,128)(2,1)}, bf16[24,64,128]{2,1,0:T(8,128)(2,1)S(1)}, u32[]{:S(2)}, u32[]{:S(2)}) collective-permute-start(bf16[24,64,128]{2,1,0:T(8,128)(2,1)} %pedigree.1.refs_0_), channel_id=1, source_target_pairs={{0,3},{1,0},{2,1},{3,2},{4,7},{5,4},{6,5},{7,6},{8,11},{9,8},{10,9... | collective-permute-start | bytes 1179656 | tf_op jit(solution)/shard_map/ppermute | solution.py:213
  93.0 23.6 %copy-start.2 = (bf16[24,64,128]{2,1,0:T(8,128)(2,1)}, bf16[24,64,128]{2,1,0:T(8,128)(2,1)S(1)}, u32[]{:S(2)}) copy-start(bf16[24,64,128]{2,1,0:T(8,128)(2,1)S(1)} %collective-permute-done.6.refs_1_) | copy-start | bytes 1179652
  114.3 2.2 %copy-start.3 = (bf16[24,64,128]{2,1,0:T(8,128)(2,1)}, bf16[24,64,128]{2,1,0:T(8,128)(2,1)S(1)}, u32[]{:S(2)}) copy-start(bf16[24,64,128]{2,1,0:T(8,128)(2,1)S(1)} %collective-permute-done.7.refs_2_) | copy-start | bytes 1179652
  116.5 0.8 copy-start.4
  148.8 2.5 %collective-permute-start.9 = (bf16[2,2,800,128]{3,2,0,1:T(8,128)(2,1)S(1)}, bf16[2,2,800,128]{3,2,0,1:T(8,128)(2,1)}, u32[]{:S(2)}, u32[]{:S(2)}) collective-permute-start(bf16[2,2,800,128]{3,2,0,1:T(8,128)(2,1)S(1)} %fusion), channel_id=1, source_target_pairs={{0,4},{4,0},{8,12},{12,8},{16,20},{20,16},{24,28},{28,24},{1,5},{5... | collective-permute-start | bytes 2457608 | tf_op jit(solution)/shard_map/ppermute | solution.py:227
  150.4 5.0 %collective-permute-start.12 = (bf16[2,2,800,128]{3,2,1,0:T(8,128)(2,1)S(1)}, bf16[2,2,800,128]{3,2,1,0:T(8,128)(2,1)}, u32[]{:S(2)}, u32[]{:S(2)}) collective-permute-start(bf16[2,2,800,128]{3,2,1,0:T(8,128)(2,1)S(1)} %fusion.1), channel_id=1, source_target_pairs={{0,4},{4,0},{8,12},{12,8},{16,20},{20,16},{24,28},{28,24},{1,5},{5... | collective-permute-start | bytes 2457608 | tf_op jit(solution)/shard_map/ppermute | solution.py:227
  151.0 4.5 %copy-start = (f32[6400,128]{1,0:T(8,128)S(1)}, f32[6400,128]{1,0:T(8,128)}, u32[]{:S(2)}) copy-start(f32[6400,128]{1,0:T(8,128)} %get-tuple-element.28) | copy-start | bytes 9830404
  154.1 11.9 %collective-permute-start.10 = (bf16[2,800,128]{2,1,0:T(8,128)(2,1)}, bf16[2,800,128]{2,1,0:T(8,128)(2,1)}, u32[]{:S(2)}, u32[]{:S(2)}) collective-permute-start(bf16[2,800,128]{2,1,0:T(8,128)(2,1)} %fusion.2), channel_id=1, source_target_pairs={{0,8},{4,12},{8,0},{12,4},{16,24},{20,28},{24,16},{28,20},{1,9},{5... | collective-permute-start | bytes 1228808 | tf_op jit(solution)/shard_map/ppermute | solution.py:227
  157.6 11.6 %collective-permute-start.13 = (bf16[2,800,128]{2,1,0:T(8,128)(2,1)}, bf16[2,800,128]{2,1,0:T(8,128)(2,1)}, u32[]{:S(2)}, u32[]{:S(2)}) collective-permute-start(bf16[2,800,128]{2,1,0:T(8,128)(2,1)} %fusion.3), channel_id=1, source_target_pairs={{0,16},{4,20},{8,24},{12,28},{16,0},{20,4},{24,8},{28,12},{1,17},{... | collective-permute-start | bytes 1228808 | tf_op jit(solution)/shard_map/ppermute | solution.py:227
  167.1 6.4 %collective-permute-start.11 = (bf16[800,128]{1,0:T(8,128)(2,1)S(1)}, bf16[800,128]{1,0:T(8,128)(2,1)S(1)}, u32[]{:S(2)}, u32[]{:S(2)}) collective-permute-start(bf16[800,128]{1,0:T(8,128)(2,1)S(1)} %fusion.4), channel_id=1, source_target_pairs={{0,16},{4,20},{8,24},{12,28},{16,0},{20,4},{24,8},{28,12},{1,17},{... | collective-permute-start | bytes 614408 | tf_op jit(solution)/shard_map/ppermute | solution.py:227
  170.3 6.1 %collective-permute-start.14 = (bf16[800,128]{1,0:T(8,128)(2,1)S(1)}, bf16[800,128]{1,0:T(8,128)(2,1)S(1)}, u32[]{:S(2)}, u32[]{:S(2)}) collective-permute-start(bf16[800,128]{1,0:T(8,128)(2,1)S(1)} %fusion.5), channel_id=1, source_target_pairs={{0,8},{4,12},{8,0},{12,4},{16,24},{20,28},{24,16},{28,20},{1,9},{5... | collective-permute-start | bytes 614408 | tf_op jit(solution)/shard_map/ppermute | solution.py:227

commit v2 on v1

--- a/solution.py
+++ b/solution.py
@@ -25,7 +25,14 @@
 def forward_kernel(scale, devices, place_ref, geno_ref, direction_ref, own_ref, *rest):
     sent, turned = rest[:-1], rest[-1]
     blocks, share, _ = own_ref.shape
-    product = scale * jnp.dot(geno_ref[...], direction_ref[...], preferred_element_type=jnp.float32)
+    middle = geno_ref.shape[0] // 2
+    product = scale * jnp.concatenate(
+        [
+            jnp.dot(geno_ref[rows, :], direction_ref[...], preferred_element_type=jnp.float32)
+            for rows in (slice(0, middle), slice(middle, None))
+        ],
+        axis=0,
+    )
     largest = jnp.max(jnp.abs(product), axis=(0, 1), keepdims=True)
     power = jnp.clip(jnp.ceil(jnp.log2(largest)), -100.0, 120.0)
     grow = jnp.exp2(14.0 - power)
@@ -120,7 +127,7 @@
     )(send_list.reshape(-1), *owns, *flat)
 
 
-def pedigree_kernel(group, own_total, index_ref, count_ref, own_ref, far_ref, prec_ref, out_ref, table):
+def pedigree_kernel(group, own_total, start, index_ref, count_ref, own_ref, far_ref, prec_ref, out_ref, table):
     step = pl.program_id(0)
 
     @pl.when(step == 0)
@@ -129,7 +136,7 @@
         table[own_total:] = far_ref[...]
 
     for b in range(group):
-        block = step * group + b
+        block = start + step * group + b
         total = None
         for j in range(prec_ref.shape[1]):
             source = table[index_ref[block, j]]
@@ -141,72 +148,91 @@
         out_ref[b] = total.astype(out_ref.dtype)
 
 
-def pedigree(blocked, incoming, rel_index, rel_count, rel_prec):
+def pedigree(blocked, incoming, rel_index, rel_count, rel_prec, start, count):
     block_total, share, _ = blocked.shape
     far_total = incoming.shape[0]
     slots = rel_prec.shape[1]
-    group = divisor(block_total, 1, 6)
+    group = divisor(math.gcd(count, start), 1, 6)
+    first = start // group
     return pl.pallas_call(
-        functools.partial(pedigree_kernel, group, block_total),
+        functools.partial(pedigree_kernel, group, block_total, start),
         grid_spec=pltpu.PrefetchScalarGridSpec(
             num_scalar_prefetch=2,
-            grid=(block_total // group,),
+            grid=(count // group,),
             in_specs=[
                 pl.BlockSpec((block_total, share, BLK), lambda i, *_: (0, 0, 0), pipeline_mode=pl.Buffered(1)),
                 pl.BlockSpec((far_total, share, BLK), lambda i, *_: (0, 0, 0), pipeline_mode=pl.Buffered(1)),
-                pl.BlockSpec((group, slots, BLK, BLK), lambda i, *_: (i, 0, 0, 0)),
+                pl.BlockSpec((group, slots, BLK, BLK), lambda i, *_: (first + i, 0, 0, 0)),
             ],
             out_specs=pl.BlockSpec((group, share, BLK), lambda i, *_: (i, 0, 0)),
             scratch_shapes=[pltpu.VMEM((block_total + far_total, share, BLK), jnp.bfloat16)],
         ),
-        out_shape=jax.ShapeDtypeStruct(blocked.shape, jnp.bfloat16),
+        out_shape=jax.ShapeDtypeStruct((count, share, BLK), jnp.bfloat16),
         compiler_params=pltpu.CompilerParams(vmem_limit_bytes=VMEM_LIMIT),
         name="pedigree",
     )(rel_index, rel_count, blocked, incoming, rel_prec)
 
 
 def backward_kernel(scale, devices, place_ref, geno_ref, *refs):
-    shares, (low_ref, high_ref, effects) = refs[:devices], refs[devices:]
+    shares, sums = refs[:devices], refs[devices:-3]
+    low_ref, high_ref, effects = refs[-3:]
     half = low_ref.shape[1]
     blocks, share, _ = shares[0].shape
 
     @pl.when(pl.program_id(0) == 0)
     def _():
-        for shift in range(devices):
-            origin = lax.rem(place_ref[0] + devices - shift, devices)
-            first = pl.multiple_of(origin * share, share)
-            for b in range(blocks):
-                effects[pl.ds(first, share), b * BLK : (b + 1) * BLK] = shares[shift][b]
-
-    product = scale * jnp.dot(effects[...], geno_ref[...], preferred_element_type=jnp.float32).T
-    low_ref[...] = product[:, :half]
-    high_ref[...] = product[:, half:]
-
-
-def backward_product(genotypes, shares, place, scale):
-    rows, width = genotypes.shape
+        for b in range(blocks):
+            pieces = []
+            for origin in range(devices):
+                piece = shares[0][b]
+                for shift in range(1, devices):
+                    here = place_ref[0] == (origin + shift) % devices
+                    piece = jnp.where(here, shares[shift][b], piece)
+                pieces.append(piece)
+            effects[b * BLK : (b + 1) * BLK, :] = jnp.concatenate(pieces, axis=0).T
+
+    middle = geno_ref.shape[0] // 2
+    product = scale * sum(
+        lax.dot_general(
+            geno_ref[rows, :], effects[rows, :], (((0,), (0,)), ((), ())), preferred_element_type=jnp.float32
+        )
+        for rows in (slice(0, middle), slice(middle, None))
+    )
+    low, high = product[:, :half], product[:, half:]
+    if sums:
+        low, high = low + sums[0][...], high + sums[1][...]
+    low_ref[...] = low
+    high_ref[...] = high
+
+
+def backward_product(genotypes, shares, place, scale, part, sums=()):
+    width = genotypes.shape[1]
     devices = len(shares)
+    rows = shares[0].shape[0] * BLK
     cols = devices * shares[0].shape[1]
-    tile = divisor(width, 2 * BLK, 5 * BLK)
+    tile = divisor(width, BLK, 5 * BLK)
+    half = pl.BlockSpec((tile, cols // 2), lambda i, *_: (i, 0))
     return pl.pallas_call(
         functools.partial(backward_kernel, scale, devices),
         grid_spec=pltpu.PrefetchScalarGridSpec(
             num_scalar_prefetch=1,
             grid=(width // tile,),
-            in_specs=[pl.BlockSpec((rows, tile), lambda i, *_: (0, i))]
-            + [pl.BlockSpec(s.shape, lambda i, *_: (0, 0, 0), pipeline_mode=pl.Buffered(1)) for s in shares],
-            out_specs=[pl.BlockSpec((tile, cols // 2), lambda i, *_: (i, 0))] * 2,
-            scratch_shapes=[pltpu.VMEM((cols, rows), jnp.bfloat16)],
+            in_specs=[pl.BlockSpec((rows, tile), lambda i, *_: (part, i))]
+            + [pl.BlockSpec(s.shape, lambda i, *_: (0, 0, 0), pipeline_mode=pl.Buffered(1)) for s in shares]
+            + [half] * len(sums),
+            out_specs=[half] * 2,
+            scratch_shapes=[pltpu.VMEM((rows, cols), jnp.bfloat16)],
         ),
         out_shape=[jax.ShapeDtypeStruct((width, cols // 2), jnp.float32)] * 2,
+        input_output_aliases={2 + devices + k: k for k in range(len(sums))},
         compiler_params=pltpu.CompilerParams(vmem_limit_bytes=VMEM_LIMIT),
         cost_estimate=pl.CostEstimate(
             flops=2 * rows * width * cols,
-            bytes_accessed=2 * rows * (width + cols) + 4 * width * cols,
+            bytes_accessed=2 * rows * (width + cols) + 4 * width * cols * (2 if sums else 1),
             transcendentals=0,
         ),
         name="backward_product",
-    )(place, genotypes, *shares)
+    )(place, genotypes, *shares, *sums)
 
 
 def turn(value, devices, shift):
@@ -254,14 +280,17 @@
     outgoing = outgoing.reshape(groups, -1, share, BLK)
     incoming = lax.all_to_all(outgoing, "animal", split_axis=0, concat_axis=0, tiled=True)
     incoming = incoming.reshape(-1, share, BLK)
-    relative = pedigree(own, incoming, rel_index, rel_count, rel_prec)
-    shares = [relative] + [turn(relative, devices, shift) for shift in range(1, devices)]
+    part_blocks = part_rows // BLK
+    shares = []
+    for part in range(parts):
+        relative = pedigree(own, incoming, rel_index, rel_count, rel_prec, part * part_blocks, part_blocks)
+        shares.append([relative] + [turn(relative, devices, shift) for shift in range(1, devices)])
 
     own_rows = width // groups
-    low, high = [
-        product.reshape(groups, own_rows, half)
-        for product in backward_product(genotypes, shares, place, 1.0 / math.sqrt(groups * rows))
-    ]
+    sums = ()
+    for part in range(parts):
+        sums = backward_product(genotypes, shares[part], place, 1.0 / math.sqrt(groups * rows), part, sums)
+    low, high = [total.reshape(groups, own_rows, half) for total in sums]
     levels = list(range(groups.bit_length() - 1))
     gradient = jnp.concatenate(
         [

time: 180 us -> 170 us (0.944)
  waiting for transfers between devices: 79 us -> 61.6 us
  Pallas kernels: 62.4 us -> 66.5 us
  starting transfers between devices: 20.2 us -> 23.2 us
  local copies, waits for them, and re-layouts: 9.12 us -> 11 us
    ppermute x9 -> x12, waiting for transfers between devices: 58.5 us -> 41.9 us  [turn(): lax.ppermute(value, 'marker', [(d, (d + shift) % devices) for d in range(...]
    ppermute x9 -> x12, starting transfers between devices: 12.7 us -> 15.6 us  [turn(): lax.ppermute(value, 'marker', [(d, (d + shift) % devices) for d in range(...]
    pallas_call x1 -> x2, Pallas kernels: 5.97 us -> 8.23 us  [pedigree(): pl.pallas_call(functools.partial(pedigree_kernel, group, block_total, sta...]
    pallas_call x1 -> x2, Pallas kernels: 30 us -> 31.5 us  [backward_product(): pl.pallas_call(functools.partial(backward_kernel, scale, devices), grid_s...]
    unnamed x32 -> x42, local copies, waits for them, and re-layouts: 2.91 us -> 4.26 us
  transfers between devices with their start and end apart: 16 -> 19, of which waited for: 13 -> 11; matrix products, arithmetic and copies ran while one was open for 6% -> 5% of each run, Pallas kernels for 6% -> 18%
where the time goes in v2:
time: 170 us; the launch traced here: 169 us
  Pallas kernels  66.5 us (39%)
  waiting for transfers between devices  61.6 us (36%)
  starting transfers between devices  23.2 us (14%)
  local copies, waits for them, and re-layouts  11 us (6%)
  other arithmetic  6.2 us (4%)
    ppermute x12, waiting for transfers between devices, turn(): lax.ppermute(value, 'marker', [(d, (d + shift) % devices) for d in range(...  41.9 us
    pallas_call x2, Pallas kernels, backward_product(): pl.pallas_call(functools.partial(backward_kernel, scale, devices), grid_s...  31.5 us
    pallas_call x2, Pallas kernels, forward_product(): pl.pallas_call(functools.partial(forward_kernel, scale, devices), grid_sp...  23.3 us
    ppermute x12, starting transfers between devices, turn(): lax.ppermute(value, 'marker', [(d, (d + shift) % devices) for d in range(...  15.6 us
    ppermute x6, waiting for transfers between devices, halving_sum(): got = lax.ppermute(sent.astype(jnp.bfloat16), 'animal', pairs)  13.5 us
    pallas_call x2, Pallas kernels, pedigree(): pl.pallas_call(functools.partial(pedigree_kernel, group, block_total, sta...  8.23 us
    all_to_all x1, waiting for transfers between devices, local(): lax.all_to_all(outgoing, 'animal', split_axis=0, concat_axis=0, tiled=True)  6.25 us
    convert_element_type x6, local copies, waits for them, and re-layouts, halving_sum(): got = lax.ppermute(sent.astype(jnp.bfloat16), 'animal', pairs)  5.27 us
  transfers between devices with their start and end apart: 19, of which 11 were waited for; matrix products, arithmetic and copies ran while one was open for 5% of the time, Pallas kernels for 18%

profile of v2, /device:TPU:8, one launch (start us, length us, event | category | flops | bytes accessed | tf_op | source)
XLA Modules:
  0.0 168.6 jit_solution(2100385033546007542)
XLA Ops:
  0.0 11.7 %forward_product.2 = (f32[12,64,128]{2,1,0:T(8,128)}, s16[816,128]{1,0:T(8,128)(2,1)}, s16[816,128]{1,0:T(8,128)(2,1)}, s16[816,128]{1,0:T(8,128)(2,1)}) custom-call(s32[1]{0:T(128)} %bitcast.place_ref, bf16[3072,6400]{1,0:T(8,128)(2,1)} %geno_ref.7, bf16[6400,256]{1,0:T(8,128)(2,1)} %direction_ref.3), custom_call_target="tpu_custom_call" | custom-call | flops 5033164800 | bytes 23724032 | tf_op jit(solution)/shard_map/forward_product/pallas_call | solution.py:61
  11.7 0.0 copy-start.17
  11.7 0.0 copy-start.16
  11.7 1.6 collective-permute-start
  13.3 11.7 %forward_product.3 = (f32[12,64,128]{2,1,0:T(8,128)}, s16[816,128]{1,0:T(8,128)(2,1)}, s16[816,128]{1,0:T(8,128)(2,1)}, s16[816,128]{1,0:T(8,128)(2,1)}) custom-call(s32[1]{0:T(128)} %bitcast.place_ref, bf16[3072,6400]{1,0:T(8,128)(2,1)} %geno_ref.7, bf16[6400,256]{1,0:T(8,128)(2,1)} %direction_ref.3), custom_call_target="tpu_custom_call" | custom-call | flops 5033164800 | bytes 23724032 | tf_op jit(solution)/shard_map/forward_product/pallas_call | solution.py:61
  25.0 1.6 collective-permute-start.1
  26.6 1.2 collective-permute-start.2
  27.8 1.7 %collective-permute-start.3 = (s16[816,128]{1,0:T(8,128)(2,1)}, s16[816,128]{1,0:T(8,128)(2,1)S(1)}, u32[]{:S(2)}, u32[]{:S(2)}) collective-permute-start(s16[816,128]{1,0:T(8,128)(2,1)} %get-tuple-element.24), channel_id=1, source_target_pairs={{0,2},{1,3},{2,0},{3,1},{4,6},{5,7},{6,4},{7,5},{8,10},{9,11},{10,... | collective-permute-start | bytes 626696 | tf_op jit(solution)/shard_map/ppermute | solution.py:239
  29.5 0.4 collective-permute-start.4
  29.9 0.0 collective-permute-done.refs_2_
  29.9 2.2 %collective-permute-start.5 = (s16[816,128]{1,0:T(8,128)(2,1)}, s16[816,128]{1,0:T(8,128)(2,1)S(1)}, u32[]{:S(2)}, u32[]{:S(2)}) collective-permute-start(s16[816,128]{1,0:T(8,128)(2,1)} %get-tuple-element.26), channel_id=1, source_target_pairs={{0,3},{1,0},{2,1},{3,2},{4,7},{5,4},{6,5},{7,6},{8,11},{9,8},{10,9... | collective-permute-start | bytes 626696 | tf_op jit(solution)/shard_map/ppermute | solution.py:239
  32.2 0.1 copy.16
  32.3 0.7 reshape.20.list_ref
  32.9 17.4 %collective-permute-done.1.refs_3_ = s16[816,128]{1,0:T(8,128)(2,1)S(1)} collective-permute-done((s16[816,128]{1,0:T(8,128)(2,1)}, s16[816,128]{1,0:T(8,128)(2,1)S(1)}, u32[]{:S(2)}, u32[]{:S(2)}) %collective-permute-start.1) | collective-permute-done | bytes 208928 | tf_op jit(solution)/shard_map/ppermute | solution.py:239
  50.4 4.4 %collective-permute-done.2.refs_4_ = s16[816,128]{1,0:T(8,128)(2,1)S(1)} collective-permute-done((s16[816,128]{1,0:T(8,128)(2,1)S(1)}, s16[816,128]{1,0:T(8,128)(2,1)S(1)}, u32[]{:S(2)}, u32[]{:S(2)}) %collective-permute-start.2) | collective-permute-done | bytes 208928 | tf_op jit(solution)/shard_map/ppermute | solution.py:239
  54.8 3.1 %collective-permute-done.3.refs_5_ = s16[816,128]{1,0:T(8,128)(2,1)S(1)} collective-permute-done((s16[816,128]{1,0:T(8,128)(2,1)}, s16[816,128]{1,0:T(8,128)(2,1)S(1)}, u32[]{:S(2)}, u32[]{:S(2)}) %collective-permute-start.3) | collective-permute-done | bytes 208928 | tf_op jit(solution)/shard_map/ppermute | solution.py:239
  57.9 0.0 collective-permute-done.4.refs_6_
  57.9 1.6 collective-permute-done.5.refs_7_
  59.5 0.6 copy-done.9
  60.1 3.4 %settle.1 = (bf16[24,64,128]{2,1,0:T(8,128)(2,1)}, bf16[16,64,128]{2,1,0:T(8,128)(2,1)}) custom-call(s32[16]{0:T(128)} %reshape.20.list_ref, f32[12,64,128]{2,1,0:T(8,128)} %get-tuple-element.19.refs_0_, f32[12,64,128]{2,1,0:T(8,128)} %get-tuple-element.20.refs_1_, s16[816,128]{1,0:T(8,128)(2,1)} %copy-done.4, s16[816,128]{1,0:T(8,128)(2,1)} %copy-done.5, ...), custom_call_target="tpu_custom_call" | custom-call | tf_op jit(solution)/shard_map/settle/pallas_call | solution.py:110
  63.5 3.7 %all-to-all-start = ((bf16[8,2,64,128]{3,2,1,0:T(8,128)(2,1)}), bf16[8,2,64,128]{3,2,1,0:T(8,128)(2,1)S(1)}, u32[]{:S(2)}, u32[]{:S(2)}) async-start(bf16[8,2,64,128]{3,2,1,0:T(8,128)(2,1)} %bitcast.39), calls=%async_computation | async-start | bytes 524288 | tf_op jit(solution)/shard_map/all_to_all | solution.py:281
  67.2 0.7 copy.17.index_ref
  67.9 6.2 %all-to-all-done = bf16[8,2,64,128]{3,2,1,0:T(8,128)(2,1)S(1)} async-done(((bf16[8,2,64,128]{3,2,1,0:T(8,128)(2,1)}), bf16[8,2,64,128]{3,2,1,0:T(8,128)(2,1)S(1)}, u32[]{:S(2)}, u32[]{:S(2)}) %all-to-all-start) | async-done | bytes 262176 | tf_op jit(solution)/shard_map/all_to_all | solution.py:281
  74.2 0.7 copy-done.3
  74.9 4.1 %pedigree.3.refs_0_ = bf16[12,64,128]{2,1,0:T(8,128)(2,1)} custom-call(s32[24,4]{1,0:T(8,128)} %copy.17.index_ref, s32[24]{0:T(128)} %count_ref.3, bf16[24,64,128]{2,1,0:T(8,128)(2,1)} %get-tuple-element.27.own_ref, bf16[16,64,128]{2,1,0:T(8,128)(2,1)} %bitcast.37, bf16[24,4,128,128]{3,2,1,0:T(8,128)(2,1)} %prec_ref.3), custom_call_target="tpu_custom_call" | custom-call | tf_op jit(solution)/shard_map/pedigree/pallas_call | solution.py:157
  79.0 1.9 %collective-permute-start.10 = (bf16[12,64,128]{2,1,0:T(8,128)(2,1)}, bf16[12,64,128]{2,1,0:T(8,128)(2,1)S(1)}, u32[]{:S(2)}, u32[]{:S(2)}) collective-permute-start(bf16[12,64,128]{2,1,0:T(8,128)(2,1)} %pedigree.3.refs_0_), channel_id=1, source_target_pairs={{0,2},{1,3},{2,0},{3,1},{4,6},{5,7},{6,4},{7,5},{8,10},{9,11},{10,... | collective-permute-start | bytes 589832 | tf_op jit(solution)/shard_map/ppermute | solution.py:239
  80.9 0.0 collective-permute-start.11
  80.9 2.0 %collective-permute-start.9 = (bf16[12,64,128]{2,1,0:T(8,128)(2,1)}, bf16[12,64,128]{2,1,0:T(8,128)(2,1)S(1)}, u32[]{:S(2)}, u32[]{:S(2)}) collective-permute-start(bf16[12,64,128]{2,1,0:T(8,128)(2,1)} %pedigree.3.refs_0_), channel_id=1, source_target_pairs={{0,1},{1,2},{2,3},{3,0},{4,5},{5,6},{6,7},{7,4},{8,9},{9,10},{10,1... | collective-permute-start | bytes 589832 | tf_op jit(solution)/shard_map/ppermute | solution.py:239
  82.9 4.1 %pedigree.2.refs_0_ = bf16[12,64,128]{2,1,0:T(8,128)(2,1)} custom-call(s32[24,4]{1,0:T(8,128)} %copy.17.index_ref, s32[24]{0:T(128)} %count_ref.3, bf16[24,64,128]{2,1,0:T(8,128)(2,1)} %get-tuple-element.27.own_ref, bf16[16,64,128]{2,1,0:T(8,128)(2,1)} %bitcast.38, bf16[24,4,128,128]{3,2,1,0:T(8,128)(2,1)} %prec_ref.3), custom_call_target="tpu_custom_call" | custom-call | tf_op jit(solution)/shard_map/pedigree/pallas_call | solution.py:157
  87.0 0.0 collective-permute-start.6
  87.0 2.9 %collective-permute-start.7 = (bf16[12,64,128]{2,1,0:T(8,128)(2,1)}, bf16[12,64,128]{2,1,0:T(8,128)(2,1)S(1)}, u32[]{:S(2)}, u32[]{:S(2)}) collective-permute-start(bf16[12,64,128]{2,1,0:T(8,128)(2,1)} %pedigree.2.refs_0_), channel_id=1, source_target_pairs={{0,2},{1,3},{2,0},{3,1},{4,6},{5,7},{6,4},{7,5},{8,10},{9,11},{10,... | collective-permute-start | bytes 589832 | tf_op jit(solution)/shard_map/ppermute | solution.py:239
  89.9 2.1 %collective-permute-done.10.refs_2_ = bf16[12,64,128]{2,1,0:T(8,128)(2,1)S(1)} collective-permute-done((bf16[12,64,128]{2,1,0:T(8,128)(2,1)}, bf16[12,64,128]{2,1,0:T(8,128)(2,1)S(1)}, u32[]{:S(2)}, u32[]{:S(2)}) %collective-permute-start.10) | collective-permute-done | bytes 196640 | tf_op jit(solution)/shard_map/ppermute | solution.py:239
  91.9 0.0 collective-permute-start.8
  91.9 13.3 %collective-permute-done.11.refs_3_ = bf16[12,64,128]{2,1,0:T(8,128)(2,1)S(1)} collective-permute-done((bf16[12,64,128]{2,1,0:T(8,128)(2,1)}, bf16[12,64,128]{2,1,0:T(8,128)(2,1)S(1)}, u32[]{:S(2)}, u32[]{:S(2)}) %collective-permute-start.11) | collective-permute-done | bytes 196640 | tf_op jit(solution)/shard_map/ppermute | solution.py:239
  105.3 0.0 collective-permute-done.9.refs_1_
  105.3 0.7 copy-done.11
  105.9 0.7 copy-done.12
  106.6 15.2 %backward_product.2 = (f32[6400,128]{1,0:T(8,128)}, f32[6400,128]{1,0:T(8,128)}) custom-call(s32[1]{0:T(128)} %bitcast.place_ref, bf16[3072,6400]{1,0:T(8,128)(2,1)} %geno_ref.7, bf16[12,64,128]{2,1,0:T(8,128)(2,1)} %pedigree.3.refs_0_, bf16[12,64,128]{2,1,0:T(8,128)(2,1)} %copy-done.12, bf16[12,64,128]{2,1,0:T(8,128)(2,1)} %copy-done.10, ...), custom_call_target="tpu_custom_call" | custom-call | flops 5033164800 | bytes 27000832 | tf_op jit(solution)/shard_map/backward_product/pallas_call | solution.py:215
  121.8 0.0 collective-permute-done.7.refs_2_
  121.8 0.0 collective-permute-done.8.refs_3_
  121.8 0.6 copy-done.13
  122.5 0.1 copy-done.14
  122.5 0.0 copy-done.15
  122.6 16.4 %backward_product.3 = (f32[6400,128]{1,0:T(8,128)}, f32[6400,128]{1,0:T(8,128)}) custom-call(s32[1]{0:T(128)} %bitcast.place_ref, bf16[3072,6400]{1,0:T(8,128)(2,1)} %geno_ref.7, bf16[12,64,128]{2,1,0:T(8,128)(2,1)} %pedigree.2.refs_0_, bf16[12,64,128]{2,1,0:T(8,128)(2,1)} %copy-done.13, ...), custom_call_target="tpu_custom_call", output_to_operand_aliasing={{0}: (6, {}), {1}: (7, {})} | custom-call | flops 5033164800 | bytes 33554432 | tf_op jit(solution)/shard_map/backward_product/pallas_call | solution.py:215
  138.9 2.6 %fusion = bf16[2,2,800,128]{3,2,0,1:T(8,128)(2,1)} fusion(f32[2,2,2,800,128]{4,3,2,1,0:T(8,128)} %bitcast.33, s32[]{:T(128)S(6)} %select_n.33), kind=kLoop, calls=%fused_computation.4 | loop fusion | bytes 1638404 | tf_op jit(solution)/shard_map/convert_element_type | solution.py:253
  141.6 0.0 collective-permute-start.12
  141.6 2.4 %fusion.1 = bf16[2,2,800,128]{3,2,1,0:T(8,128)(2,1)} fusion(f32[2,2,2,800,128]{4,3,2,1,0:T(8,128)} %bitcast.35, s32[]{:T(128)S(6)} %select_n.33), kind=kLoop, calls=%fused_computation.5 | loop fusion | bytes 1638404 | tf_op jit(solution)/shard_map/convert_element_type | solution.py:253
  144.0 0.5 collective-permute-start.15
  144.5 1.4 bitcast_add_fusion.1
  146.0 0.1 fusion.2
  146.1 1.0 collective-permute-start.13
  147.1 1.3 bitcast_add_fusion
  148.4 0.1 fusion.3
  148.5 0.7 collective-permute-start.16
  149.2 0.8 dynamic_slice.58
  150.0 7.5 %collective-permute-done.13 = bf16[2,800,128]{2,1,0:T(8,128)(2,1)S(1)} collective-permute-done((bf16[2,800,128]{2,1,0:T(8,128)(2,1)S(1)}, bf16[2,800,128]{2,1,0:T(8,128)(2,1)S(1)}, u32[]{:S(2)}, u32[]{:S(2)}) %collective-permute-start.13) | collective-permute-done | bytes 409632 | tf_op jit(solution)/shard_map/ppermute | solution.py:253
  157.5 1.2 bitcast_add_fusion.3
  158.8 0.6 collective-permute-start.14
  159.4 0.7 collective-permute-done.16
  160.1 0.1 bitcast_add_fusion.2
  160.2 1.0 collective-permute-start.17
  161.2 3.8 %collective-permute-done.14 = bf16[800,128]{1,0:T(8,128)(2,1)S(1)} collective-permute-done((bf16[800,128]{1,0:T(8,128)(2,1)S(1)}, bf16[800,128]{1,0:T(8,128)(2,1)S(1)}, u32[]{:S(2)}, u32[]{:S(2)}) %collective-permute-start.14) | collective-permute-done | bytes 204832 | tf_op jit(solution)/shard_map/ppermute | solution.py:253
  165.0 1.5 collective-permute-done.17
  166.5 2.1 %maximum_add_fusion = f32[800,256]{1,0:T(8,128)} fusion(f32[800,128]{1,0:T(8,128)S(1)} %bitcast_add_fusion.4, f32[800,128]{1,0:T(8,128)S(1)} %bitcast_add_fusion.5, bf16[6400,256]{1,0:T(8,128)(2,1)} %direction_ref.3, s32[]{:T(128)S(6)} %select_n.38, f32[800]{0:T(1024)S(1)} %dynamic_slice.58), kind=kLoop, calls=%fused_computation.6 | loop fusion | flops 819200 | bytes 2051204 | tf_op jit(solution)/shard_map/add | solution.py:305
  (38 shorter events, 0.2 us)
Async XLA Ops:
  11.7 14.9 %copy-start.19 = (s16[816,128]{1,0:T(8,128)(2,1)S(1)}, s16[816,128]{1,0:T(8,128)(2,1)}, u32[]{:S(2)}) copy-start(s16[816,128]{1,0:T(8,128)(2,1)} %get-tuple-element.23) | copy-start | bytes 626692
  11.7 17.8 %copy-start.18 = (s16[816,128]{1,0:T(8,128)(2,1)S(1)}, s16[816,128]{1,0:T(8,128)(2,1)}, u32[]{:S(2)}) copy-start(s16[816,128]{1,0:T(8,128)(2,1)} %get-tuple-element.25) | copy-start | bytes 626692
  11.7 20.5 %copy-start.17 = (s32[1,8,2]{1,2,0:T(2,128)S(1)}, s32[1,8,2]{1,2,0:T(2,128)}, u32[]{:S(2)}) copy-start(s32[1,8,2]{1,2,0:T(2,128)} %param.10) | copy-start | bytes 196
  11.7 55.6 %copy-start.16 = (s32[24,4]{0,1:T(4,128)S(1)}, s32[24,4]{0,1:T(4,128)}, u32[]{:S(2)}) copy-start(s32[24,4]{0,1:T(4,128)} %param.11) | copy-start | bytes 1156
  11.7 18.2 %collective-permute-start = (s16[816,128]{1,0:T(8,128)(2,1)}, s16[816,128]{1,0:T(8,128)(2,1)S(1)}, u32[]{:S(2)}, u32[]{:S(2)}) collective-permute-start(s16[816,128]{1,0:T(8,128)(2,1)} %get-tuple-element.21), channel_id=1, source_target_pairs={{0,1},{1,2},{2,3},{3,0},{4,5},{5,6},{6,7},{7,4},{8,9},{9,10},{10,1... | collective-permute-start | bytes 626696 | tf_op jit(solution)/shard_map/ppermute | solution.py:239
  25.0 25.4 %collective-permute-start.1 = (s16[816,128]{1,0:T(8,128)(2,1)}, s16[816,128]{1,0:T(8,128)(2,1)S(1)}, u32[]{:S(2)}, u32[]{:S(2)}) collective-permute-start(s16[816,128]{1,0:T(8,128)(2,1)} %get-tuple-element.22), channel_id=1, source_target_pairs={{0,1},{1,2},{2,3},{3,0},{4,5},{5,6},{6,7},{7,4},{8,9},{9,10},{10,1... | collective-permute-start | bytes 626696 | tf_op jit(solution)/shard_map/ppermute | solution.py:239
  26.6 28.2 %collective-permute-start.2 = (s16[816,128]{1,0:T(8,128)(2,1)S(1)}, s16[816,128]{1,0:T(8,128)(2,1)S(1)}, u32[]{:S(2)}, u32[]{:S(2)}) collective-permute-start(s16[816,128]{1,0:T(8,128)(2,1)S(1)} %copy-done.19), channel_id=1, source_target_pairs={{0,2},{1,3},{2,0},{3,1},{4,6},{5,7},{6,4},{7,5},{8,10},{9,11},{10,... | collective-permute-start | bytes 626696 | tf_op jit(solution)/shard_map/ppermute | solution.py:239
  27.8 30.1 %collective-permute-start.3 = (s16[816,128]{1,0:T(8,128)(2,1)}, s16[816,128]{1,0:T(8,128)(2,1)S(1)}, u32[]{:S(2)}, u32[]{:S(2)}) collective-permute-start(s16[816,128]{1,0:T(8,128)(2,1)} %get-tuple-element.24), channel_id=1, source_target_pairs={{0,2},{1,3},{2,0},{3,1},{4,6},{5,7},{6,4},{7,5},{8,10},{9,11},{10,... | collective-permute-start | bytes 626696 | tf_op jit(solution)/shard_map/ppermute | solution.py:239
  29.5 28.4 %collective-permute-start.4 = (s16[816,128]{1,0:T(8,128)(2,1)S(1)}, s16[816,128]{1,0:T(8,128)(2,1)S(1)}, u32[]{:S(2)}, u32[]{:S(2)}) collective-permute-start(s16[816,128]{1,0:T(8,128)(2,1)S(1)} %copy-done.18), channel_id=1, source_target_pairs={{0,3},{1,0},{2,1},{3,2},{4,7},{5,4},{6,5},{7,6},{8,11},{9,8},{10,9... | collective-permute-start | bytes 626696 | tf_op jit(solution)/shard_map/ppermute | solution.py:239
  29.9 29.5 %copy-start.4 = (s16[816,128]{1,0:T(8,128)(2,1)}, s16[816,128]{1,0:T(8,128)(2,1)S(1)}, u32[]{:S(2)}) copy-start(s16[816,128]{1,0:T(8,128)(2,1)S(1)} %collective-permute-done.refs_2_) | copy-start | bytes 626692
  29.9 29.5 %collective-permute-start.5 = (s16[816,128]{1,0:T(8,128)(2,1)}, s16[816,128]{1,0:T(8,128)(2,1)S(1)}, u32[]{:S(2)}, u32[]{:S(2)}) collective-permute-start(s16[816,128]{1,0:T(8,128)(2,1)} %get-tuple-element.26), channel_id=1, source_target_pairs={{0,3},{1,0},{2,1},{3,2},{4,7},{5,4},{6,5},{7,6},{8,11},{9,8},{10,9... | collective-permute-start | bytes 626696 | tf_op jit(solution)/shard_map/ppermute | solution.py:239
  50.4 9.1 %copy-start.5 = (s16[816,128]{1,0:T(8,128)(2,1)}, s16[816,128]{1,0:T(8,128)(2,1)S(1)}, u32[]{:S(2)}) copy-start(s16[816,128]{1,0:T(8,128)(2,1)S(1)} %collective-permute-done.1.refs_3_) | copy-start | bytes 626692
  54.8 4.7 %copy-start.6 = (s16[816,128]{1,0:T(8,128)(2,1)}, s16[816,128]{1,0:T(8,128)(2,1)S(1)}, u32[]{:S(2)}) copy-start(s16[816,128]{1,0:T(8,128)(2,1)S(1)} %collective-permute-done.2.refs_4_) | copy-start | bytes 626692
  57.9 1.6 copy-start.7
  57.9 1.6 copy-start.8
  59.5 0.7 copy-start.9
  63.5 10.7 %all-to-all-start = ((bf16[8,2,64,128]{3,2,1,0:T(8,128)(2,1)}), bf16[8,2,64,128]{3,2,1,0:T(8,128)(2,1)S(1)}, u32[]{:S(2)}, u32[]{:S(2)}) async-start(bf16[8,2,64,128]{3,2,1,0:T(8,128)(2,1)} %bitcast.39), calls=%async_computation | async-start | bytes 524288 | tf_op jit(solution)/shard_map/all_to_all | solution.py:281
  74.2 0.7 copy-start.3
  79.0 12.9 %collective-permute-start.10 = (bf16[12,64,128]{2,1,0:T(8,128)(2,1)}, bf16[12,64,128]{2,1,0:T(8,128)(2,1)S(1)}, u32[]{:S(2)}, u32[]{:S(2)}) collective-permute-start(bf16[12,64,128]{2,1,0:T(8,128)(2,1)} %pedigree.3.refs_0_), channel_id=1, source_target_pairs={{0,2},{1,3},{2,0},{3,1},{4,6},{5,7},{6,4},{7,5},{8,10},{9,11},{10,... | collective-permute-start | bytes 589832 | tf_op jit(solution)/shard_map/ppermute | solution.py:239
  80.9 24.4 %collective-permute-start.11 = (bf16[12,64,128]{2,1,0:T(8,128)(2,1)}, bf16[12,64,128]{2,1,0:T(8,128)(2,1)S(1)}, u32[]{:S(2)}, u32[]{:S(2)}) collective-permute-start(bf16[12,64,128]{2,1,0:T(8,128)(2,1)} %pedigree.3.refs_0_), channel_id=1, source_target_pairs={{0,3},{1,0},{2,1},{3,2},{4,7},{5,4},{6,5},{7,6},{8,11},{9,8},{10,9... | collective-permute-start | bytes 589832 | tf_op jit(solution)/shard_map/ppermute | solution.py:239
  80.9 24.4 %collective-permute-start.9 = (bf16[12,64,128]{2,1,0:T(8,128)(2,1)}, bf16[12,64,128]{2,1,0:T(8,128)(2,1)S(1)}, u32[]{:S(2)}, u32[]{:S(2)}) collective-permute-start(bf16[12,64,128]{2,1,0:T(8,128)(2,1)} %pedigree.3.refs_0_), channel_id=1, source_target_pairs={{0,1},{1,2},{2,3},{3,0},{4,5},{5,6},{6,7},{7,4},{8,9},{9,10},{10,1... | collective-permute-start | bytes 589832 | tf_op jit(solution)/shard_map/ppermute | solution.py:239
  87.0 34.8 %collective-permute-start.6 = (bf16[12,64,128]{2,1,0:T(8,128)(2,1)}, bf16[12,64,128]{2,1,0:T(8,128)(2,1)S(1)}, u32[]{:S(2)}, u32[]{:S(2)}) collective-permute-start(bf16[12,64,128]{2,1,0:T(8,128)(2,1)} %pedigree.2.refs_0_), channel_id=1, source_target_pairs={{0,1},{1,2},{2,3},{3,0},{4,5},{5,6},{6,7},{7,4},{8,9},{9,10},{10,1... | collective-permute-start | bytes 589832 | tf_op jit(solution)/shard_map/ppermute | solution.py:239
  87.0 34.8 %collective-permute-start.7 = (bf16[12,64,128]{2,1,0:T(8,128)(2,1)}, bf16[12,64,128]{2,1,0:T(8,128)(2,1)S(1)}, u32[]{:S(2)}, u32[]{:S(2)}) collective-permute-start(bf16[12,64,128]{2,1,0:T(8,128)(2,1)} %pedigree.2.refs_0_), channel_id=1, source_target_pairs={{0,2},{1,3},{2,0},{3,1},{4,6},{5,7},{6,4},{7,5},{8,10},{9,11},{10,... | collective-permute-start | bytes 589832 | tf_op jit(solution)/shard_map/ppermute | solution.py:239
  91.9 13.3 %copy-start.10 = (bf16[12,64,128]{2,1,0:T(8,128)(2,1)}, bf16[12,64,128]{2,1,0:T(8,128)(2,1)S(1)}, u32[]{:S(2)}) copy-start(bf16[12,64,128]{2,1,0:T(8,128)(2,1)S(1)} %collective-permute-done.10.refs_2_) | copy-start | bytes 589828
  91.9 29.9 %collective-permute-start.8 = (bf16[12,64,128]{2,1,0:T(8,128)(2,1)}, bf16[12,64,128]{2,1,0:T(8,128)(2,1)S(1)}, u32[]{:S(2)}, u32[]{:S(2)}) collective-permute-start(bf16[12,64,128]{2,1,0:T(8,128)(2,1)} %pedigree.2.refs_0_), channel_id=1, source_target_pairs={{0,3},{1,0},{2,1},{3,2},{4,7},{5,4},{6,5},{7,6},{8,11},{9,8},{10,9... | collective-permute-start | bytes 589832 | tf_op jit(solution)/shard_map/ppermute | solution.py:239
  105.3 0.7 copy-start.11
  105.9 0.7 copy-start.12
  121.8 0.7 copy-start.13
  121.8 0.7 copy-start.14
  121.8 0.8 copy-start.15
  138.9 5.6 %copy-start = (f32[6400,128]{1,0:T(8,128)S(1)}, f32[6400,128]{1,0:T(8,128)}, u32[]{:S(2)}) copy-start(f32[6400,128]{1,0:T(8,128)} %get-tuple-element.31) | copy-start | bytes 9830404
  141.6 2.9 %collective-permute-start.12 = (bf16[2,2,800,128]{3,2,0,1:T(8,128)(2,1)}, bf16[2,2,800,128]{3,2,0,1:T(8,128)(2,1)}, u32[]{:S(2)}, u32[]{:S(2)}) collective-permute-start(bf16[2,2,800,128]{3,2,0,1:T(8,128)(2,1)} %fusion), channel_id=1, source_target_pairs={{0,4},{4,0},{8,12},{12,8},{16,20},{20,16},{24,28},{28,24},{1,5},{5... | collective-permute-start | bytes 2457608 | tf_op jit(solution)/shard_map/ppermute | solution.py:253
  144.0 3.1 %collective-permute-start.15 = (bf16[2,2,800,128]{3,2,1,0:T(8,128)(2,1)}, bf16[2,2,800,128]{3,2,1,0:T(8,128)(2,1)}, u32[]{:S(2)}, u32[]{:S(2)}) collective-permute-start(bf16[2,2,800,128]{3,2,1,0:T(8,128)(2,1)} %fusion.1), channel_id=1, source_target_pairs={{0,4},{4,0},{8,12},{12,8},{16,20},{20,16},{24,28},{28,24},{1,5},{5... | collective-permute-start | bytes 2457608 | tf_op jit(solution)/shard_map/ppermute | solution.py:253
  144.5 2.6 %copy-start.1 = (f32[6400,128]{1,0:T(8,128)S(1)}, f32[6400,128]{1,0:T(8,128)}, u32[]{:S(2)}) copy-start(f32[6400,128]{1,0:T(8,128)} %get-tuple-element.32) | copy-start | bytes 9830404
  146.0 2.4 %copy-start.2 = (f32[2,2,800,128]{3,2,0,1:T(8,128)}, f32[2,2,800,128]{3,2,0,1:T(8,128)S(1)}, u32[]{:S(2)}) copy-start(f32[2,2,800,128]{3,2,0,1:T(8,128)S(1)} %bitcast_add_fusion.1) | copy-start | bytes 4915204
  146.1 11.5 %collective-permute-start.13 = (bf16[2,800,128]{2,1,0:T(8,128)(2,1)S(1)}, bf16[2,800,128]{2,1,0:T(8,128)(2,1)S(1)}, u32[]{:S(2)}, u32[]{:S(2)}) collective-permute-start(bf16[2,800,128]{2,1,0:T(8,128)(2,1)S(1)} %fusion.2), channel_id=1, source_target_pairs={{0,8},{4,12},{8,0},{12,4},{16,24},{20,28},{24,16},{28,20},{1,9},{5... | collective-permute-start | bytes 1228808 | tf_op jit(solution)/shard_map/ppermute | solution.py:253
  148.5 11.6 %collective-permute-start.16 = (bf16[2,800,128]{2,1,0:T(8,128)(2,1)S(1)}, bf16[2,800,128]{2,1,0:T(8,128)(2,1)S(1)}, u32[]{:S(2)}, u32[]{:S(2)}) collective-permute-start(bf16[2,800,128]{2,1,0:T(8,128)(2,1)S(1)} %fusion.3), channel_id=1, source_target_pairs={{0,16},{4,20},{8,24},{12,28},{16,0},{20,4},{24,8},{28,12},{1,17},{... | collective-permute-start | bytes 1228808 | tf_op jit(solution)/shard_map/ppermute | solution.py:253
  158.8 6.2 %collective-permute-start.14 = (bf16[800,128]{1,0:T(8,128)(2,1)S(1)}, bf16[800,128]{1,0:T(8,128)(2,1)S(1)}, u32[]{:S(2)}, u32[]{:S(2)}) collective-permute-start(bf16[800,128]{1,0:T(8,128)(2,1)S(1)} %fusion.4), channel_id=1, source_target_pairs={{0,16},{4,20},{8,24},{12,28},{16,0},{20,4},{24,8},{28,12},{1,17},{... | collective-permute-start | bytes 614408 | tf_op jit(solution)/shard_map/ppermute | solution.py:253
  160.2 6.3 %collective-permute-start.17 = (bf16[800,128]{1,0:T(8,128)(2,1)S(1)}, bf16[800,128]{1,0:T(8,128)(2,1)S(1)}, u32[]{:S(2)}, u32[]{:S(2)}) collective-permute-start(bf16[800,128]{1,0:T(8,128)(2,1)S(1)} %fusion.5), channel_id=1, source_target_pairs={{0,8},{4,12},{8,0},{12,4},{16,24},{20,28},{24,16},{28,20},{1,9},{5... | collective-permute-start | bytes 614408 | tf_op jit(solution)/shard_map/ppermute | solution.py:253

commit v3 on v2

--- a/solution.py
+++ b/solution.py
@@ -22,14 +22,13 @@
     return best
 
 
-def forward_kernel(scale, devices, place_ref, geno_ref, direction_ref, own_ref, *rest):
+def forward_kernel(scale, devices, place_ref, upper_ref, lower_ref, direction_ref, own_ref, *rest):
     sent, turned = rest[:-1], rest[-1]
     blocks, share, _ = own_ref.shape
-    middle = geno_ref.shape[0] // 2
     product = scale * jnp.concatenate(
         [
-            jnp.dot(geno_ref[rows, :], direction_ref[...], preferred_element_type=jnp.float32)
-            for rows in (slice(0, middle), slice(middle, None))
+            jnp.dot(geno_ref[...], direction_ref[...], preferred_element_type=jnp.float32)
+            for geno_ref in (upper_ref, lower_ref)
         ],
         axis=0,
     )
@@ -64,7 +63,8 @@
             num_scalar_prefetch=1,
             grid=(steps,),
             in_specs=[
-                pl.BlockSpec((tile, depth), lambda i, *_: (start + i, 0)),
+                pl.BlockSpec((tile // 2, depth), lambda i, *_: (2 * (start + i), 0)),
+                pl.BlockSpec((tile // 2, depth), lambda i, *_: (2 * (start + i) + 1, 0)),
                 pl.BlockSpec((depth, cols), lambda i, *_: (0, 0), pipeline_mode=pl.Buffered(1)),
             ],
             out_specs=[pl.BlockSpec((blocks, share, BLK), lambda i, *_: (i, 0, 0))]
@@ -80,7 +80,7 @@
             transcendentals=0,
         ),
         name="forward_product",
-    )(place, genotypes, direction)
+    )(place, genotypes, genotypes, direction)
 
 
 def settle_kernel(parts, blocks, list_ref, *refs):
@@ -173,8 +173,8 @@
     )(rel_index, rel_count, blocked, incoming, rel_prec)
 
 
-def backward_kernel(scale, devices, place_ref, geno_ref, *refs):
-    shares, sums = refs[:devices], refs[devices:-3]
+def backward_kernel(scale, devices, lanes, place_ref, *refs):
+    geno, shares, sums = refs[:lanes], refs[lanes : lanes + devices], refs[lanes + devices : -3]
     low_ref, high_ref, effects = refs[-3:]
     half = low_ref.shape[1]
     blocks, share, _ = shares[0].shape
@@ -191,40 +191,39 @@
                 pieces.append(piece)
             effects[b * BLK : (b + 1) * BLK, :] = jnp.concatenate(pieces, axis=0).T
 
-    middle = geno_ref.shape[0] // 2
-    product = scale * sum(
-        lax.dot_general(
-            geno_ref[rows, :], effects[rows, :], (((0,), (0,)), ((), ())), preferred_element_type=jnp.float32
+    for lane, geno_ref in enumerate(geno):
+        tile = geno_ref.shape[1]
+        rows = slice(lane * tile, (lane + 1) * tile)
+        product = scale * lax.dot_general(
+            geno_ref[...], effects[...], (((0,), (0,)), ((), ())), preferred_element_type=jnp.float32
         )
-        for rows in (slice(0, middle), slice(middle, None))
-    )
-    low, high = product[:, :half], product[:, half:]
-    if sums:
-        low, high = low + sums[0][...], high + sums[1][...]
-    low_ref[...] = low
-    high_ref[...] = high
-
-
-def backward_product(genotypes, shares, place, scale, part, sums=()):
+        low, high = product[:, :half], product[:, half:]
+        if sums:
+            low, high = low + sums[0][rows, :], high + sums[1][rows, :]
+        low_ref[rows, :] = low.astype(low_ref.dtype)
+        high_ref[rows, :] = high.astype(high_ref.dtype)
+
+
+def backward_product(genotypes, shares, place, scale, part, kind, sums=()):
     width = genotypes.shape[1]
     devices = len(shares)
     rows = shares[0].shape[0] * BLK
     cols = devices * shares[0].shape[1]
-    tile = divisor(width, BLK, 5 * BLK)
-    half = pl.BlockSpec((tile, cols // 2), lambda i, *_: (i, 0))
+    lanes = 2 if width % (2 * BLK) == 0 else 1
+    tile = divisor(width // lanes, BLK, 5 * BLK)
+    half = pl.BlockSpec((lanes * tile, cols // 2), lambda i, *_: (i, 0))
     return pl.pallas_call(
-        functools.partial(backward_kernel, scale, devices),
+        functools.partial(backward_kernel, scale, devices, lanes),
         grid_spec=pltpu.PrefetchScalarGridSpec(
             num_scalar_prefetch=1,
-            grid=(width // tile,),
-            in_specs=[pl.BlockSpec((rows, tile), lambda i, *_: (part, i))]
+            grid=(width // (lanes * tile),),
+            in_specs=[pl.BlockSpec((rows, tile), lambda i, *_, k=k: (part, lanes * i + k)) for k in range(lanes)]
             + [pl.BlockSpec(s.shape, lambda i, *_: (0, 0, 0), pipeline_mode=pl.Buffered(1)) for s in shares]
             + [half] * len(sums),
             out_specs=[half] * 2,
             scratch_shapes=[pltpu.VMEM((rows, cols), jnp.bfloat16)],
         ),
-        out_shape=[jax.ShapeDtypeStruct((width, cols // 2), jnp.float32)] * 2,
-        input_output_aliases={2 + devices + k: k for k in range(len(sums))},
+        out_shape=[jax.ShapeDtypeStruct((width, cols // 2), kind)] * 2,
         compiler_params=pltpu.CompilerParams(vmem_limit_bytes=VMEM_LIMIT),
         cost_estimate=pl.CostEstimate(
             flops=2 * rows * width * cols,
@@ -232,7 +231,7 @@
             transcendentals=0,
         ),
         name="backward_product",
-    )(place, genotypes, *shares, *sums)
+    )(place, *[genotypes] * lanes, *shares, *sums)
 
 
 def turn(value, devices, shift):
@@ -242,18 +241,19 @@
 def halving_sum(blocks, devices, bits):
     levels = devices.bit_length() - 1
     here = lax.axis_index("animal")
-    total = blocks.reshape((2,) * levels + blocks.shape[1:])
+    terms = [blocks.reshape((2,) * levels + blocks.shape[1:])]
     left = list(range(levels - 1, -1, -1))
     for bit in bits:
         axis = left.index(bit)
         mine = (here >> bit) & 1
-        sent = lax.dynamic_index_in_dim(total, 1 - mine, axis, keepdims=False)
-        kept = lax.dynamic_index_in_dim(total, mine, axis, keepdims=False)
-        pairs = [(d, d ^ (1 << bit)) for d in range(devices)]
-        got = lax.ppermute(sent.astype(jnp.bfloat16), "animal", pairs)
-        total = kept + got.astype(jnp.float32)
+        sent, kept = [
+            [lax.dynamic_index_in_dim(term, side, axis, keepdims=False) for term in terms]
+            for side in (1 - mine, mine)
+        ]
+        sent = sum(term.astype(jnp.float32) for term in sent).astype(jnp.bfloat16)
+        terms = kept + [lax.ppermute(sent, "animal", [(d, d ^ (1 << bit)) for d in range(devices)])]
         left.pop(axis)
-    return total
+    return sum(term.astype(jnp.float32) for term in terms)
 
 
 def local(genotypes, direction, ridge, send_list, rel_index, rel_count, rel_prec):
@@ -272,6 +272,10 @@
             genotypes, direction, place, devices, 1.0 / math.sqrt(MARKERS), part * part_rows, part_rows, tile
         )
         owns.append(own)
+        if part > 0:
+            sent, earlier = lax.optimization_barrier((sent, [one[-1] for one in coded]))
+            for one, value in zip(coded, earlier):
+                one[-1] = value
         for shift in range(1, devices):
             coded[shift - 1].append(turn(sent[shift - 1], devices, shift))
     own, outgoing = settle(owns, coded, send_list, tile // BLK)
@@ -289,7 +293,8 @@
     own_rows = width // groups
     sums = ()
     for part in range(parts):
-        sums = backward_product(genotypes, shares[part], place, 1.0 / math.sqrt(groups * rows), part, sums)
+        kind = jnp.float32 if part < parts - 1 else jnp.bfloat16
+        sums = backward_product(genotypes, shares[part], place, 1.0 / math.sqrt(groups * rows), part, kind, sums)
     low, high = [total.reshape(groups, own_rows, half) for total in sums]
     levels = list(range(groups.bit_length() - 1))
     gradient = jnp.concatenate(

time: 170 us -> 161 us (0.947)
  waiting for transfers between devices: 61.6 us -> 55.3 us
  other arithmetic: 6.2 us -> 11 us
  Pallas kernels: 66.5 us -> 62.9 us
  local copies, waits for them, and re-layouts: 11 us -> 8.86 us
    convert_element_type x0 -> x4, other arithmetic: none -> 6.64 us  [halving_sum(): sent = sum((term.astype(jnp.float32) for term in sent)).astype(jnp.bfloat16)]
    ppermute x12, waiting for transfers between devices: 41.9 us -> 35.5 us  [turn(): lax.ppermute(value, 'marker', [(d, (d + shift) % devices) for d in range(...]
    convert_element_type x6 -> x0, local copies, waits for them, and re-layouts: 5.27 us -> none  [halving_sum(): got = lax.ppermute(sent.astype(jnp.bfloat16), 'animal', pairs)]
    pallas_call x2, Pallas kernels: 31.5 us -> 27.8 us  [backward_product(): pl.pallas_call(functools.partial(backward_kernel, scale, devices, lanes),...]
    squeeze x0 -> x2, local copies, waits for them, and re-layouts: none -> 3.21 us  [halving_sum(): lax.dynamic_index_in_dim(term, side, axis, keepdims=False)]
    add x6 -> x2, other arithmetic: 4.13 us -> 2.26 us  [halving_sum(): return sum((term.astype(jnp.float32) for term in terms))]
    unnamed x42 -> x36, local copies, waits for them, and re-layouts: 4.26 us -> 4.23 us
  transfers between devices with their start and end apart: 19 -> 19, of which waited for: 11 -> 12; matrix products, arithmetic and copies ran while one was open for 5% -> 7% of each run, Pallas kernels for 18% -> 18%
where the time goes in v3:
time: 161 us
  Pallas kernels  62.9 us (39%)
  waiting for transfers between devices  55.3 us (34%)
  starting transfers between devices  22.5 us (14%)
  other arithmetic  11 us (7%)
  local copies, waits for them, and re-layouts  8.86 us (6%)
    ppermute x12, waiting for transfers between devices, turn(): lax.ppermute(value, 'marker', [(d, (d + shift) % devices) for d in range(...  35.5 us
    pallas_call x2, Pallas kernels, backward_product(): pl.pallas_call(functools.partial(backward_kernel, scale, devices, lanes),...  27.8 us
    pallas_call x2, Pallas kernels, forward_product(): pl.pallas_call(functools.partial(forward_kernel, scale, devices), grid_sp...  23.6 us
    ppermute x12, starting transfers between devices, turn(): lax.ppermute(value, 'marker', [(d, (d + shift) % devices) for d in range(...  15.1 us
    ppermute x6, waiting for transfers between devices, halving_sum(): lax.ppermute(sent, 'animal', [(d, d ^ 1 << bit) for d in range(devices)])  13.6 us
    pallas_call x2, Pallas kernels, pedigree(): pl.pallas_call(functools.partial(pedigree_kernel, group, block_total, sta...  8.21 us
    convert_element_type x4, other arithmetic, halving_sum(): sent = sum((term.astype(jnp.float32) for term in sent)).astype(jnp.bfloat16)  6.64 us
    all_to_all x1, waiting for transfers between devices, local(): lax.all_to_all(outgoing, 'animal', split_axis=0, concat_axis=0, tiled=True)  6.25 us
  transfers between devices with their start and end apart: 19, of which 12 were waited for; matrix products, arithmetic and copies ran while one was open for 7% of the time, Pallas kernels for 18%

profile of v3, /device:TPU:8, one launch (start us, length us, event | category | flops | bytes accessed | tf_op | source)
XLA Modules:
  0.0 160.7 jit_solution(6320910402961079657)
XLA Ops:
  0.0 11.8 %forward_product.2 = (f32[12,64,128]{2,1,0:T(8,128)}, s16[816,128]{1,0:T(8,128)(2,1)}, s16[816,128]{1,0:T(8,128)(2,1)}, s16[816,128]{1,0:T(8,128)(2,1)}) custom-call(s32[1]{0:T(128)} %bitcast.place_ref, bf16[3072,6400]{1,0:T(8,128)(2,1)} %refs_1_.3, bf16[3072,6400]{1,0:T(8,128)(2,1)} %refs_1_.3, bf16[6400,256]{1,0:T(8,128)(2,1)} %direction_ref.3), custom_call_target="tpu_custom_call" | custom-call | flops 5033164800 | bytes 23724032 | tf_op jit(solution)/shard_map/forward_product/pallas_call | solution.py:60
  11.8 1.6 collective-permute-start
  13.4 1.1 collective-permute-start.1
  14.5 1.9 %collective-permute-start.2 = (s16[816,128]{1,0:T(8,128)(2,1)}, s16[816,128]{1,0:T(8,128)(2,1)S(1)}, u32[]{:S(2)}, u32[]{:S(2)}) collective-permute-start(s16[816,128]{1,0:T(8,128)(2,1)} %get-tuple-element.32), channel_id=1, source_target_pairs={{0,3},{1,0},{2,1},{3,2},{4,7},{5,4},{6,5},{7,6},{8,11},{9,8},{10,9... | collective-permute-start | bytes 626696 | tf_op jit(solution)/shard_map/ppermute | solution.py:238
  16.4 11.8 %forward_product.3 = (f32[12,64,128]{2,1,0:T(8,128)}, s16[816,128]{1,0:T(8,128)(2,1)}, s16[816,128]{1,0:T(8,128)(2,1)}, s16[816,128]{1,0:T(8,128)(2,1)}) custom-call(s32[1]{0:T(128)} %bitcast.place_ref, bf16[3072,6400]{1,0:T(8,128)(2,1)} %refs_1_.3, bf16[3072,6400]{1,0:T(8,128)(2,1)} %refs_1_.3, bf16[6400,256]{1,0:T(8,128)(2,1)} %direction_ref.3), custom_call_target="tpu_custom_call" | custom-call | flops 5033164800 | bytes 23724032 | tf_op jit(solution)/shard_map/forward_product/pallas_call | solution.py:60
  28.2 0.0 collective-permute-done.refs_2_
  28.2 3.3 %collective-permute-done.1.refs_4_ = s16[816,128]{1,0:T(8,128)(2,1)S(1)} collective-permute-done((s16[816,128]{1,0:T(8,128)(2,1)}, s16[816,128]{1,0:T(8,128)(2,1)S(1)}, u32[]{:S(2)}, u32[]{:S(2)}) %collective-permute-start.1) | collective-permute-done | bytes 208928 | tf_op jit(solution)/shard_map/ppermute | solution.py:238
  31.5 1.7 %collective-permute-done.2.refs_6_ = s16[816,128]{1,0:T(8,128)(2,1)S(1)} collective-permute-done((s16[816,128]{1,0:T(8,128)(2,1)}, s16[816,128]{1,0:T(8,128)(2,1)S(1)}, u32[]{:S(2)}, u32[]{:S(2)}) %collective-permute-start.2) | collective-permute-done | bytes 208928 | tf_op jit(solution)/shard_map/ppermute | solution.py:238
  33.2 0.0 collective-permute-start.3
  33.2 1.7 %collective-permute-start.4 = (s16[816,128]{1,0:T(8,128)(2,1)}, s16[816,128]{1,0:T(8,128)(2,1)S(1)}, u32[]{:S(2)}, u32[]{:S(2)}) collective-permute-start(s16[816,128]{1,0:T(8,128)(2,1)} %get-tuple-element.36), channel_id=1, source_target_pairs={{0,2},{1,3},{2,0},{3,1},{4,6},{5,7},{6,4},{7,5},{8,10},{9,11},{10,... | collective-permute-start | bytes 626696 | tf_op jit(solution)/shard_map/ppermute | solution.py:238
  34.9 1.9 %collective-permute-start.5 = (s16[816,128]{1,0:T(8,128)(2,1)}, s16[816,128]{1,0:T(8,128)(2,1)S(1)}, u32[]{:S(2)}, u32[]{:S(2)}) collective-permute-start(s16[816,128]{1,0:T(8,128)(2,1)} %get-tuple-element.38), channel_id=1, source_target_pairs={{0,3},{1,0},{2,1},{3,2},{4,7},{5,4},{6,5},{7,6},{8,11},{9,8},{10,9... | collective-permute-start | bytes 626696 | tf_op jit(solution)/shard_map/ppermute | solution.py:238
  36.9 0.1 copy.12
  37.0 0.7 reshape.70.list_ref
  37.6 3.9 %collective-permute-done.3.refs_3_ = s16[816,128]{1,0:T(8,128)(2,1)S(1)} collective-permute-done((s16[816,128]{1,0:T(8,128)(2,1)}, s16[816,128]{1,0:T(8,128)(2,1)S(1)}, u32[]{:S(2)}, u32[]{:S(2)}) %collective-permute-start.3) | collective-permute-done | bytes 208928 | tf_op jit(solution)/shard_map/ppermute | solution.py:238
  41.5 10.4 %collective-permute-done.4.refs_5_ = s16[816,128]{1,0:T(8,128)(2,1)S(1)} collective-permute-done((s16[816,128]{1,0:T(8,128)(2,1)}, s16[816,128]{1,0:T(8,128)(2,1)S(1)}, u32[]{:S(2)}, u32[]{:S(2)}) %collective-permute-start.4) | collective-permute-done | bytes 208928 | tf_op jit(solution)/shard_map/ppermute | solution.py:238
  51.9 0.9 collective-permute-done.5.refs_7_
  52.8 0.6 copy-done.8
  53.5 3.4 %settle.1 = (bf16[24,64,128]{2,1,0:T(8,128)(2,1)}, bf16[16,64,128]{2,1,0:T(8,128)(2,1)}) custom-call(s32[16]{0:T(128)} %reshape.70.list_ref, f32[12,64,128]{2,1,0:T(8,128)} %get-tuple-element.25.refs_0_, f32[12,64,128]{2,1,0:T(8,128)} %get-tuple-element.26.refs_1_, s16[816,128]{1,0:T(8,128)(2,1)} %copy-done.3, s16[816,128]{1,0:T(8,128)(2,1)} %copy-done.6, ...), custom_call_target="tpu_custom_call" | custom-call | tf_op jit(solution)/shard_map/settle/pallas_call | solution.py:110
  56.9 3.7 %all-to-all-start = ((bf16[8,2,64,128]{3,2,1,0:T(8,128)(2,1)}), bf16[8,2,64,128]{3,2,1,0:T(8,128)(2,1)S(1)}, u32[]{:S(2)}, u32[]{:S(2)}) async-start(bf16[8,2,64,128]{3,2,1,0:T(8,128)(2,1)} %bitcast.69), calls=%async_computation | async-start | bytes 524288 | tf_op jit(solution)/shard_map/all_to_all | solution.py:285
  60.6 0.7 copy.13.index_ref
  61.3 6.2 %all-to-all-done = bf16[8,2,64,128]{3,2,1,0:T(8,128)(2,1)S(1)} async-done(((bf16[8,2,64,128]{3,2,1,0:T(8,128)(2,1)}), bf16[8,2,64,128]{3,2,1,0:T(8,128)(2,1)S(1)}, u32[]{:S(2)}, u32[]{:S(2)}) %all-to-all-start) | async-done | bytes 262176 | tf_op jit(solution)/shard_map/all_to_all | solution.py:285
  67.5 0.7 copy-done
  68.2 4.1 %pedigree.3.refs_2_ = bf16[12,64,128]{2,1,0:T(8,128)(2,1)} custom-call(s32[24,4]{1,0:T(8,128)} %copy.13.index_ref, s32[24]{0:T(128)} %count_ref.3, bf16[24,64,128]{2,1,0:T(8,128)(2,1)} %get-tuple-element.39.own_ref, bf16[16,64,128]{2,1,0:T(8,128)(2,1)} %bitcast.59, bf16[24,4,128,128]{3,2,1,0:T(8,128)(2,1)} %prec_ref.3), custom_call_target="tpu_custom_call" | custom-call | tf_op jit(solution)/shard_map/pedigree/pallas_call | solution.py:157
  72.3 2.4 %collective-permute-start.10 = (bf16[12,64,128]{2,1,0:T(8,128)(2,1)}, bf16[12,64,128]{2,1,0:T(8,128)(2,1)S(1)}, u32[]{:S(2)}, u32[]{:S(2)}) collective-permute-start(bf16[12,64,128]{2,1,0:T(8,128)(2,1)} %pedigree.3.refs_2_), channel_id=1, source_target_pairs={{0,2},{1,3},{2,0},{3,1},{4,6},{5,7},{6,4},{7,5},{8,10},{9,11},{10,... | collective-permute-start | bytes 589832 | tf_op jit(solution)/shard_map/ppermute | solution.py:238
  74.7 0.0 collective-permute-start.11
  74.7 2.0 %collective-permute-start.9 = (bf16[12,64,128]{2,1,0:T(8,128)(2,1)}, bf16[12,64,128]{2,1,0:T(8,128)(2,1)S(1)}, u32[]{:S(2)}, u32[]{:S(2)}) collective-permute-start(bf16[12,64,128]{2,1,0:T(8,128)(2,1)} %pedigree.3.refs_2_), channel_id=1, source_target_pairs={{0,1},{1,2},{2,3},{3,0},{4,5},{5,6},{6,7},{7,4},{8,9},{9,10},{10,1... | collective-permute-start | bytes 589832 | tf_op jit(solution)/shard_map/ppermute | solution.py:238
  76.8 4.1 %pedigree.2.refs_2_ = bf16[12,64,128]{2,1,0:T(8,128)(2,1)} custom-call(s32[24,4]{1,0:T(8,128)} %copy.13.index_ref, s32[24]{0:T(128)} %count_ref.3, bf16[24,64,128]{2,1,0:T(8,128)(2,1)} %get-tuple-element.39.own_ref, bf16[16,64,128]{2,1,0:T(8,128)(2,1)} %bitcast.60, bf16[24,4,128,128]{3,2,1,0:T(8,128)(2,1)} %prec_ref.3), custom_call_target="tpu_custom_call" | custom-call | tf_op jit(solution)/shard_map/pedigree/pallas_call | solution.py:157
  80.9 0.0 collective-permute-start.6
  80.9 2.4 %collective-permute-start.7 = (bf16[12,64,128]{2,1,0:T(8,128)(2,1)}, bf16[12,64,128]{2,1,0:T(8,128)(2,1)S(1)}, u32[]{:S(2)}, u32[]{:S(2)}) collective-permute-start(bf16[12,64,128]{2,1,0:T(8,128)(2,1)} %pedigree.2.refs_2_), channel_id=1, source_target_pairs={{0,2},{1,3},{2,0},{3,1},{4,6},{5,7},{6,4},{7,5},{8,10},{9,11},{10,... | collective-permute-start | bytes 589832 | tf_op jit(solution)/shard_map/ppermute | solution.py:238
  83.3 2.0 %collective-permute-done.10.refs_4_ = bf16[12,64,128]{2,1,0:T(8,128)(2,1)S(1)} collective-permute-done((bf16[12,64,128]{2,1,0:T(8,128)(2,1)}, bf16[12,64,128]{2,1,0:T(8,128)(2,1)S(1)}, u32[]{:S(2)}, u32[]{:S(2)}) %collective-permute-start.10) | collective-permute-done | bytes 196640 | tf_op jit(solution)/shard_map/ppermute | solution.py:238
  85.3 0.0 collective-permute-start.8
  85.3 13.3 %collective-permute-done.11.refs_5_ = bf16[12,64,128]{2,1,0:T(8,128)(2,1)S(1)} collective-permute-done((bf16[12,64,128]{2,1,0:T(8,128)(2,1)}, bf16[12,64,128]{2,1,0:T(8,128)(2,1)S(1)}, u32[]{:S(2)}, u32[]{:S(2)}) %collective-permute-start.11) | collective-permute-done | bytes 196640 | tf_op jit(solution)/shard_map/ppermute | solution.py:238
  98.6 0.0 collective-permute-done.9.refs_3_
  98.6 0.7 copy-done.13
  99.2 0.7 copy-done.14
  99.9 13.6 %backward_product.2 = (f32[6400,128]{1,0:T(8,128)}, f32[6400,128]{1,0:T(8,128)}) custom-call(s32[1]{0:T(128)} %bitcast.place_ref, bf16[3072,6400]{1,0:T(8,128)(2,1)} %refs_1_.3, bf16[3072,6400]{1,0:T(8,128)(2,1)} %refs_1_.3, bf16[12,64,128]{2,1,0:T(8,128)(2,1)} %pedigree.3.refs_2_, bf16[12,64,128]{2,1,0:T(8,128)(2,1)} %copy-done.14, ...), custom_call_target="tpu_custom_call" | custom-call | flops 5033164800 | bytes 27000832 | tf_op jit(solution)/shard_map/backward_product/pallas_call | solution.py:215
  113.5 0.0 collective-permute-done.6.refs_3_
  113.5 0.0 copy-start.9
  113.5 0.0 collective-permute-done.7.refs_4_
  113.5 0.6 copy-done.9
  114.2 0.1 copy-done.10
  114.2 0.1 copy-done.11
  114.3 14.2 %backward_product.3 = (bf16[6400,128]{1,0:T(8,128)(2,1)}, bf16[6400,128]{1,0:T(8,128)(2,1)}) custom-call(s32[1]{0:T(128)} %bitcast.place_ref, bf16[3072,6400]{1,0:T(8,128)(2,1)} %refs_1_.3, bf16[3072,6400]{1,0:T(8,128)(2,1)} %refs_1_.3, bf16[12,64,128]{2,1,0:T(8,128)(2,1)} %pedigree.2.refs_2_, bf16[12,64,128]{2,1,0:T(8,128)(2,1)} %copy-done.9, ...), custom_call_target="tpu_custom_call" | custom-call | flops 5033164800 | bytes 33554432 | tf_op jit(solution)/shard_map/backward_product/pallas_call | solution.py:215
  128.5 2.3 %dynamic-slice_bitcast_fusion.1 = bf16[2,2,800,128]{3,2,1,0:T(8,128)(2,1)} fusion(bf16[2,2,2,800,128]{4,3,2,1,0:T(8,128)(2,1)} %bitcast.65, s32[]{:T(128)S(6)} %select_n.60), kind=kLoop, calls=%fused_computation.6 | loop fusion | bytes 1638404 | tf_op jit(solution)/shard_map/jit(dynamic_index_in_dim)/squeeze | solution.py:250
  130.8 0.0 collective-permute-start.12
  130.8 0.9 dynamic-slice_bitcast_fusion
  131.7 0.5 collective-permute-start.15
  132.2 1.2 collective-permute-done.12
  133.4 1.9 %fusion.1 = bf16[2,800,128]{2,1,0:T(8,128)(2,1)} fusion(bf16[2,2,800,128]{3,2,1,0:T(8,128)(2,1)} %collective-permute-done.12, s32[]{:T(128)S(6)} %select_n.61, bf16[2,2,2,800,128]{4,3,2,1,0:T(8,128)(2,1)S(1)} %bitcast.66, s32[]{:T(128)S(6)} %select_n.62, s32[]{:T(128)S(6)} %select_n.59), kind=kLoop, calls=%fused_computation.4 | loop fusion | flops 819200 | bytes 1228812 | tf_op jit(solution)/shard_map/convert_element_type | solution.py:253
  135.3 1.0 collective-permute-start.13
  136.3 1.9 %fusion = bf16[2,800,128]{2,1,0:T(8,128)(2,1)} fusion(bf16[2,2,800,128]{3,2,1,0:T(8,128)(2,1)} %collective-permute-done.15, s32[]{:T(128)S(6)} %select_n.63, bf16[2,2,2,800,128]{4,3,2,1,0:T(8,128)(2,1)S(1)} %bitcast.62, s32[]{:T(128)S(6)} %select_n.64, s32[]{:T(128)S(6)} %select_n.59), kind=kLoop, calls=%fused_computation.2 | loop fusion | flops 819200 | bytes 1228812 | tf_op jit(solution)/shard_map/convert_element_type | solution.py:253
  138.1 0.6 collective-permute-start.16
  138.7 8.4 %collective-permute-done.13 = bf16[2,800,128]{2,1,0:T(8,128)(2,1)} collective-permute-done((bf16[2,800,128]{2,1,0:T(8,128)(2,1)}, bf16[2,800,128]{2,1,0:T(8,128)(2,1)}, u32[]{:S(2)}, u32[]{:S(2)}) %collective-permute-start.13) | collective-permute-done | bytes 409632 | tf_op jit(solution)/shard_map/ppermute | solution.py:254
  147.1 1.8 %fusion.4 = bf16[800,128]{1,0:T(8,128)(2,1)} fusion(bf16[2,800,128]{2,1,0:T(8,128)(2,1)} %collective-permute-done.13, s32[]{:T(128)S(6)} %select_n.63, bf16[2,2,800,128]{3,2,1,0:T(8,128)(2,1)} %collective-permute-done.12, s32[]{:T(128)S(6)} %select_n.64, s32[]{:T(128)S(6)} %select_n.57, bf16[2,2,2,800,128]{4,3,2,1,0:T(8,128)(2,1)S(1)} %bitcast.67, ...), kind=kLoop, calls=%fused_computation.14 | loop fusion | flops 614400 | bytes 819216 | tf_op jit(solution)/shard_map/convert_element_type | solution.py:253
  148.9 0.6 collective-permute-start.14
  149.5 0.8 dynamic_slice.88
  150.3 0.0 collective-permute-done.16
  150.3 1.1 fusion.2
  151.4 1.0 collective-permute-start.17
  152.4 3.0 %collective-permute-done.14 = bf16[800,128]{1,0:T(8,128)(2,1)S(1)} collective-permute-done((bf16[800,128]{1,0:T(8,128)(2,1)}, bf16[800,128]{1,0:T(8,128)(2,1)S(1)}, u32[]{:S(2)}, u32[]{:S(2)}) %collective-permute-start.14) | collective-permute-done | bytes 204832 | tf_op jit(solution)/shard_map/ppermute | solution.py:254
  155.5 1.1 fusion.5
  156.6 0.9 collective-permute-done.17
  157.5 1.1 fusion.3
  158.6 2.1 %maximum_add_fusion = f32[800,256]{1,0:T(8,128)} fusion(f32[800,128]{1,0:T(8,128)S(1)} %fusion.3, f32[800,128]{1,0:T(8,128)S(1)} %fusion.5, bf16[6400,256]{1,0:T(8,128)(2,1)} %direction_ref.3, s32[]{:T(128)S(6)} %select_n.65, f32[800]{0:T(1024)S(1)} %dynamic_slice.88), kind=kLoop, calls=%fused_computation | loop fusion | flops 819200 | bytes 2051204 | tf_op jit(solution)/shard_map/add | solution.py:310
  (28 shorter events, 0.1 us)
Async XLA Ops:
  11.8 16.4 %collective-permute-start = (s16[816,128]{1,0:T(8,128)(2,1)}, s16[816,128]{1,0:T(8,128)(2,1)S(1)}, u32[]{:S(2)}, u32[]{:S(2)}) collective-permute-start(s16[816,128]{1,0:T(8,128)(2,1)} %get-tuple-element.30), channel_id=1, source_target_pairs={{0,1},{1,2},{2,3},{3,0},{4,5},{5,6},{6,7},{7,4},{8,9},{9,10},{10,1... | collective-permute-start | bytes 626696 | tf_op jit(solution)/shard_map/ppermute | solution.py:238
  13.4 18.2 %collective-permute-start.1 = (s16[816,128]{1,0:T(8,128)(2,1)}, s16[816,128]{1,0:T(8,128)(2,1)S(1)}, u32[]{:S(2)}, u32[]{:S(2)}) collective-permute-start(s16[816,128]{1,0:T(8,128)(2,1)} %get-tuple-element.31), channel_id=1, source_target_pairs={{0,2},{1,3},{2,0},{3,1},{4,6},{5,7},{6,4},{7,5},{8,10},{9,11},{10,... | collective-permute-start | bytes 626696 | tf_op jit(solution)/shard_map/ppermute | solution.py:238
  14.5 22.4 %copy-start.16 = (s32[1,8,2]{1,2,0:T(2,128)S(1)}, s32[1,8,2]{1,2,0:T(2,128)}, u32[]{:S(2)}) copy-start(s32[1,8,2]{1,2,0:T(2,128)} %param.10) | copy-start | bytes 196
  14.5 18.8 %collective-permute-start.2 = (s16[816,128]{1,0:T(8,128)(2,1)}, s16[816,128]{1,0:T(8,128)(2,1)S(1)}, u32[]{:S(2)}, u32[]{:S(2)}) collective-permute-start(s16[816,128]{1,0:T(8,128)(2,1)} %get-tuple-element.32), channel_id=1, source_target_pairs={{0,3},{1,0},{2,1},{3,2},{4,7},{5,4},{6,5},{7,6},{8,11},{9,8},{10,9... | collective-permute-start | bytes 626696 | tf_op jit(solution)/shard_map/ppermute | solution.py:238
  28.2 32.4 %copy-start.15 = (s32[24,4]{0,1:T(4,128)S(1)}, s32[24,4]{0,1:T(4,128)}, u32[]{:S(2)}) copy-start(s32[24,4]{0,1:T(4,128)} %param.11) | copy-start | bytes 1156
  28.2 24.6 %copy-start.3 = (s16[816,128]{1,0:T(8,128)(2,1)}, s16[816,128]{1,0:T(8,128)(2,1)S(1)}, u32[]{:S(2)}) copy-start(s16[816,128]{1,0:T(8,128)(2,1)S(1)} %collective-permute-done.refs_2_) | copy-start | bytes 626692
  31.5 21.3 %copy-start.4 = (s16[816,128]{1,0:T(8,128)(2,1)}, s16[816,128]{1,0:T(8,128)(2,1)S(1)}, u32[]{:S(2)}) copy-start(s16[816,128]{1,0:T(8,128)(2,1)S(1)} %collective-permute-done.1.refs_4_) | copy-start | bytes 626692
  33.2 19.6 %copy-start.5 = (s16[816,128]{1,0:T(8,128)(2,1)}, s16[816,128]{1,0:T(8,128)(2,1)S(1)}, u32[]{:S(2)}) copy-start(s16[816,128]{1,0:T(8,128)(2,1)S(1)} %collective-permute-done.2.refs_6_) | copy-start | bytes 626692
  33.2 8.2 %collective-permute-start.3 = (s16[816,128]{1,0:T(8,128)(2,1)}, s16[816,128]{1,0:T(8,128)(2,1)S(1)}, u32[]{:S(2)}, u32[]{:S(2)}) collective-permute-start(s16[816,128]{1,0:T(8,128)(2,1)} %get-tuple-element.34), channel_id=1, source_target_pairs={{0,1},{1,2},{2,3},{3,0},{4,5},{5,6},{6,7},{7,4},{8,9},{9,10},{10,1... | collective-permute-start | bytes 626696 | tf_op jit(solution)/shard_map/ppermute | solution.py:238
  33.2 18.6 %collective-permute-start.4 = (s16[816,128]{1,0:T(8,128)(2,1)}, s16[816,128]{1,0:T(8,128)(2,1)S(1)}, u32[]{:S(2)}, u32[]{:S(2)}) collective-permute-start(s16[816,128]{1,0:T(8,128)(2,1)} %get-tuple-element.36), channel_id=1, source_target_pairs={{0,2},{1,3},{2,0},{3,1},{4,6},{5,7},{6,4},{7,5},{8,10},{9,11},{10,... | collective-permute-start | bytes 626696 | tf_op jit(solution)/shard_map/ppermute | solution.py:238
  34.9 17.9 %collective-permute-start.5 = (s16[816,128]{1,0:T(8,128)(2,1)}, s16[816,128]{1,0:T(8,128)(2,1)S(1)}, u32[]{:S(2)}, u32[]{:S(2)}) collective-permute-start(s16[816,128]{1,0:T(8,128)(2,1)} %get-tuple-element.38), channel_id=1, source_target_pairs={{0,3},{1,0},{2,1},{3,2},{4,7},{5,4},{6,5},{7,6},{8,11},{9,8},{10,9... | collective-permute-start | bytes 626696 | tf_op jit(solution)/shard_map/ppermute | solution.py:238
  41.5 11.3 %copy-start.6 = (s16[816,128]{1,0:T(8,128)(2,1)}, s16[816,128]{1,0:T(8,128)(2,1)S(1)}, u32[]{:S(2)}) copy-start(s16[816,128]{1,0:T(8,128)(2,1)S(1)} %collective-permute-done.3.refs_3_) | copy-start | bytes 626692
  51.9 0.9 copy-start.7
  52.8 0.7 copy-start.8
  56.9 10.7 %all-to-all-start = ((bf16[8,2,64,128]{3,2,1,0:T(8,128)(2,1)}), bf16[8,2,64,128]{3,2,1,0:T(8,128)(2,1)S(1)}, u32[]{:S(2)}, u32[]{:S(2)}) async-start(bf16[8,2,64,128]{3,2,1,0:T(8,128)(2,1)} %bitcast.69), calls=%async_computation | async-start | bytes 524288 | tf_op jit(solution)/shard_map/all_to_all | solution.py:285
  67.5 0.7 copy-start
  72.3 12.9 %collective-permute-start.10 = (bf16[12,64,128]{2,1,0:T(8,128)(2,1)}, bf16[12,64,128]{2,1,0:T(8,128)(2,1)S(1)}, u32[]{:S(2)}, u32[]{:S(2)}) collective-permute-start(bf16[12,64,128]{2,1,0:T(8,128)(2,1)} %pedigree.3.refs_2_), channel_id=1, source_target_pairs={{0,2},{1,3},{2,0},{3,1},{4,6},{5,7},{6,4},{7,5},{8,10},{9,11},{10,... | collective-permute-start | bytes 589832 | tf_op jit(solution)/shard_map/ppermute | solution.py:238
  74.7 23.8 %collective-permute-start.11 = (bf16[12,64,128]{2,1,0:T(8,128)(2,1)}, bf16[12,64,128]{2,1,0:T(8,128)(2,1)S(1)}, u32[]{:S(2)}, u32[]{:S(2)}) collective-permute-start(bf16[12,64,128]{2,1,0:T(8,128)(2,1)} %pedigree.3.refs_2_), channel_id=1, source_target_pairs={{0,3},{1,0},{2,1},{3,2},{4,7},{5,4},{6,5},{7,6},{8,11},{9,8},{10,9... | collective-permute-start | bytes 589832 | tf_op jit(solution)/shard_map/ppermute | solution.py:238
  74.7 23.8 %collective-permute-start.9 = (bf16[12,64,128]{2,1,0:T(8,128)(2,1)}, bf16[12,64,128]{2,1,0:T(8,128)(2,1)S(1)}, u32[]{:S(2)}, u32[]{:S(2)}) collective-permute-start(bf16[12,64,128]{2,1,0:T(8,128)(2,1)} %pedigree.3.refs_2_), channel_id=1, source_target_pairs={{0,1},{1,2},{2,3},{3,0},{4,5},{5,6},{6,7},{7,4},{8,9},{9,10},{10,1... | collective-permute-start | bytes 589832 | tf_op jit(solution)/shard_map/ppermute | solution.py:238
  80.9 32.6 %collective-permute-start.6 = (bf16[12,64,128]{2,1,0:T(8,128)(2,1)}, bf16[12,64,128]{2,1,0:T(8,128)(2,1)S(1)}, u32[]{:S(2)}, u32[]{:S(2)}) collective-permute-start(bf16[12,64,128]{2,1,0:T(8,128)(2,1)} %pedigree.2.refs_2_), channel_id=1, source_target_pairs={{0,1},{1,2},{2,3},{3,0},{4,5},{5,6},{6,7},{7,4},{8,9},{9,10},{10,1... | collective-permute-start | bytes 589832 | tf_op jit(solution)/shard_map/ppermute | solution.py:238
  80.9 32.6 %collective-permute-start.7 = (bf16[12,64,128]{2,1,0:T(8,128)(2,1)}, bf16[12,64,128]{2,1,0:T(8,128)(2,1)S(1)}, u32[]{:S(2)}, u32[]{:S(2)}) collective-permute-start(bf16[12,64,128]{2,1,0:T(8,128)(2,1)} %pedigree.2.refs_2_), channel_id=1, source_target_pairs={{0,2},{1,3},{2,0},{3,1},{4,6},{5,7},{6,4},{7,5},{8,10},{9,11},{10,... | collective-permute-start | bytes 589832 | tf_op jit(solution)/shard_map/ppermute | solution.py:238
  85.3 13.3 %copy-start.12 = (bf16[12,64,128]{2,1,0:T(8,128)(2,1)}, bf16[12,64,128]{2,1,0:T(8,128)(2,1)S(1)}, u32[]{:S(2)}) copy-start(bf16[12,64,128]{2,1,0:T(8,128)(2,1)S(1)} %collective-permute-done.10.refs_4_) | copy-start | bytes 589828
  85.3 28.3 %collective-permute-start.8 = (bf16[12,64,128]{2,1,0:T(8,128)(2,1)}, bf16[12,64,128]{2,1,0:T(8,128)(2,1)S(1)}, u32[]{:S(2)}, u32[]{:S(2)}) collective-permute-start(bf16[12,64,128]{2,1,0:T(8,128)(2,1)} %pedigree.2.refs_2_), channel_id=1, source_target_pairs={{0,3},{1,0},{2,1},{3,2},{4,7},{5,4},{6,5},{7,6},{8,11},{9,8},{10,9... | collective-permute-start | bytes 589832 | tf_op jit(solution)/shard_map/ppermute | solution.py:238
  98.6 0.7 copy-start.13
  99.2 0.7 copy-start.14
  113.5 0.7 copy-start.9
  113.5 0.7 copy-start.10
  113.5 0.8 copy-start.11
  128.5 2.3 %copy-start.1 = (bf16[6400,128]{1,0:T(8,128)(2,1)S(1)}, bf16[6400,128]{1,0:T(8,128)(2,1)}, u32[]{:S(2)}) copy-start(bf16[6400,128]{1,0:T(8,128)(2,1)} %get-tuple-element.44) | copy-start | bytes 4915204
  128.5 5.0 %copy-start.2 = (bf16[6400,128]{1,0:T(8,128)(2,1)S(1)}, bf16[6400,128]{1,0:T(8,128)(2,1)}, u32[]{:S(2)}) copy-start(bf16[6400,128]{1,0:T(8,128)(2,1)} %get-tuple-element.43) | copy-start | bytes 4915204
  130.8 2.7 %collective-permute-start.12 = (bf16[2,2,800,128]{3,2,1,0:T(8,128)(2,1)}, bf16[2,2,800,128]{3,2,1,0:T(8,128)(2,1)}, u32[]{:S(2)}, u32[]{:S(2)}) collective-permute-start(bf16[2,2,800,128]{3,2,1,0:T(8,128)(2,1)} %dynamic-slice_bitcast_fusion.1), channel_id=1, source_target_pairs={{0,4},{4,0},{8,12},{12,8},{16,20},{20,16},{24,28},{28,24},{1,5},{5... | collective-permute-start | bytes 2457608 | tf_op jit(solution)/shard_map/ppermute | solution.py:254
  131.7 4.6 %collective-permute-start.15 = (bf16[2,2,800,128]{3,2,1,0:T(8,128)(2,1)}, bf16[2,2,800,128]{3,2,1,0:T(8,128)(2,1)}, u32[]{:S(2)}, u32[]{:S(2)}) collective-permute-start(bf16[2,2,800,128]{3,2,1,0:T(8,128)(2,1)} %dynamic-slice_bitcast_fusion), channel_id=1, source_target_pairs={{0,4},{4,0},{8,12},{12,8},{16,20},{20,16},{24,28},{28,24},{1,5},{5... | collective-permute-start | bytes 2457608 | tf_op jit(solution)/shard_map/ppermute | solution.py:254
  135.3 11.8 %collective-permute-start.13 = (bf16[2,800,128]{2,1,0:T(8,128)(2,1)}, bf16[2,800,128]{2,1,0:T(8,128)(2,1)}, u32[]{:S(2)}, u32[]{:S(2)}) collective-permute-start(bf16[2,800,128]{2,1,0:T(8,128)(2,1)} %fusion.1), channel_id=1, source_target_pairs={{0,8},{4,12},{8,0},{12,4},{16,24},{20,28},{24,16},{28,20},{1,9},{5... | collective-permute-start | bytes 1228808 | tf_op jit(solution)/shard_map/ppermute | solution.py:254
  138.1 12.1 %collective-permute-start.16 = (bf16[2,800,128]{2,1,0:T(8,128)(2,1)}, bf16[2,800,128]{2,1,0:T(8,128)(2,1)}, u32[]{:S(2)}, u32[]{:S(2)}) collective-permute-start(bf16[2,800,128]{2,1,0:T(8,128)(2,1)} %fusion), channel_id=1, source_target_pairs={{0,16},{4,20},{8,24},{12,28},{16,0},{20,4},{24,8},{28,12},{1,17},{... | collective-permute-start | bytes 1228808 | tf_op jit(solution)/shard_map/ppermute | solution.py:254
  148.9 6.5 %collective-permute-start.14 = (bf16[800,128]{1,0:T(8,128)(2,1)}, bf16[800,128]{1,0:T(8,128)(2,1)S(1)}, u32[]{:S(2)}, u32[]{:S(2)}) collective-permute-start(bf16[800,128]{1,0:T(8,128)(2,1)} %fusion.4), channel_id=1, source_target_pairs={{0,16},{4,20},{8,24},{12,28},{16,0},{20,4},{24,8},{28,12},{1,17},{... | collective-permute-start | bytes 614408 | tf_op jit(solution)/shard_map/ppermute | solution.py:254
  151.4 6.1 %collective-permute-start.17 = (bf16[800,128]{1,0:T(8,128)(2,1)S(1)}, bf16[800,128]{1,0:T(8,128)(2,1)S(1)}, u32[]{:S(2)}, u32[]{:S(2)}) collective-permute-start(bf16[800,128]{1,0:T(8,128)(2,1)S(1)} %fusion.2), channel_id=1, source_target_pairs={{0,8},{4,12},{8,0},{12,4},{16,24},{20,28},{24,16},{28,20},{1,9},{5... | collective-permute-start | bytes 614408 | tf_op jit(solution)/shard_map/ppermute | solution.py:254

commit v4 on v3

v4 whole, which is shorter than its diff:
```python
import functools
import math

import jax
import jax.numpy as jnp
from jax import lax
from jax.experimental import pallas as pl
from jax.experimental.pallas import tpu as pltpu
from jax.sharding import PartitionSpec as P

MARKERS = 25600
BLK = 128
MARK = 16
VMEM_LIMIT = 56 * 1024 * 1024


def divisor(total, unit, most):
    best = unit
    for size in range(unit, most + 1, unit):
        if total % size == 0:
            best = size
    return best


def forward_kernel(scale, devices, place_ref, upper_ref, lower_ref, direction_ref, own_ref, sent_ref, turned):
    blocks, share, _ = own_ref.shape
    product = scale * jnp.concatenate(
        [
            jnp.dot(geno_ref[...], direction_ref[...], preferred_element_type=jnp.float32)
            for geno_ref in (upper_ref, lower_ref)
        ],
        axis=0,
    )
    largest = jnp.max(jnp.abs(product), axis=(0, 1), keepdims=True)
    power = jnp.clip(jnp.ceil(jnp.log2(largest)), -100.0, 120.0)
    grow = jnp.exp2(14.0 - power)
    turned[...] = product.T
    first = pl.multiple_of(place_ref[0] * share, share)
    mark = jnp.broadcast_to(power, (MARK, BLK)).astype(jnp.int32).astype(jnp.int16)
    for b in range(blocks):
        columns = slice(b * BLK, (b + 1) * BLK)
        own_ref[b] = turned[pl.ds(first, share), columns]
        for target in range(devices):
            piece = turned[target * share : (target + 1) * share, columns]
            coded = jnp.round(piece * grow).astype(jnp.int32).astype(jnp.int16)
            sent_ref[target, b * share : (b + 1) * share] = coded
    for target in range(devices):
        sent_ref[target, blocks * share :] = mark


def forward_product(genotypes, direction, place, devices, scale, first, rows, tile):
    depth, cols = direction.shape
    start = first // tile
    share = cols // devices
    blocks = tile // BLK
    coded = blocks * share + MARK
    steps = rows // tile
    return pl.pallas_call(
        functools.partial(forward_kernel, scale, devices),
        grid_spec=pltpu.PrefetchScalarGridSpec(
            num_scalar_prefetch=1,
            grid=(steps,),
            in_specs=[
                pl.BlockSpec((tile // 2, depth), lambda i, *_: (2 * (start + i), 0)),
                pl.BlockSpec((tile // 2, depth), lambda i, *_: (2 * (start + i) + 1, 0)),
                pl.BlockSpec((depth, cols), lambda i, *_: (0, 0), pipeline_mode=pl.Buffered(1)),
            ],
            out_specs=[
                pl.BlockSpec((blocks, share, BLK), lambda i, *_: (i, 0, 0)),
                pl.BlockSpec((devices, coded, BLK), lambda i, *_: (0, i, 0)),
            ],
            scratch_shapes=[pltpu.VMEM((cols, tile), jnp.float32)],
        ),
        out_shape=[
            jax.ShapeDtypeStruct((steps * blocks, share, BLK), jnp.float32),
            jax.ShapeDtypeStruct((devices, steps * coded, BLK), jnp.int16),
        ],
        compiler_params=pltpu.CompilerParams(vmem_limit_bytes=VMEM_LIMIT),
        cost_estimate=pl.CostEstimate(
            flops=2 * rows * depth * cols,
            bytes_accessed=2 * (rows + cols) * depth + 2 * rows * cols,
            transcendentals=0,
        ),
        name="forward_product",
    )(place, genotypes, genotypes, direction)


def settle_kernel(parts, blocks, list_ref, place_ref, *refs):
    owns, coded, (sum_ref, out_ref) = refs[:parts], refs[parts:-2], refs[-2:]
    share = sum_ref.shape[1]
    size = blocks * share + MARK
    at = 0
    for own, ref in zip(owns, coded):
        for step in range(own.shape[0] // blocks):
            row = step * size
            total = own[step * blocks : (step + 1) * blocks]
            for source in range(ref.shape[0]):
                power = ref[source, row + blocks * share : row + size].astype(jnp.float32)[:1]
                steps = ref[source, row : row + blocks * share].astype(jnp.float32)
                factor = jnp.where(place_ref[0] == source, 0.0, jnp.exp2(power - 14.0))
                total = total + (steps * factor).reshape(blocks, share, BLK)
            sum_ref[at : at + blocks] = total.astype(sum_ref.dtype)
            at += blocks
    for i in range(out_ref.shape[0]):
        out_ref[i] = sum_ref[list_ref[i]]


def settle(owns, coded, send_list, place, blocks):
    block_total = sum(own.shape[0] for own in owns)
    share = owns[0].shape[1]
    sends = send_list.size
    return pl.pallas_call(
        functools.partial(settle_kernel, len(owns), blocks),
        grid_spec=pltpu.PrefetchScalarGridSpec(
            num_scalar_prefetch=2,
            grid=(1,),
            in_specs=[pl.BlockSpec(x.shape, lambda i, *_: (0, 0, 0)) for x in (*owns, *coded)],
            out_specs=[
                pl.BlockSpec((block_total, share, BLK), lambda i, *_: (0, 0, 0)),
                pl.BlockSpec((sends, share, BLK), lambda i, *_: (0, 0, 0)),
            ],
        ),
        out_shape=[
            jax.ShapeDtypeStruct((block_total, share, BLK), jnp.bfloat16),
            jax.ShapeDtypeStruct((sends, share, BLK), jnp.bfloat16),
        ],
        compiler_params=pltpu.CompilerParams(vmem_limit_bytes=VMEM_LIMIT),
        name="settle",
    )(send_list.reshape(-1), place, *owns, *coded)


def pedigree_kernel(group, own_total, start, index_ref, count_ref, own_ref, far_ref, prec_ref, out_ref, table):
    step = pl.program_id(0)

    @pl.when(step == 0)
    def _():
        table[:own_total] = own_ref[...]
        table[own_total:] = far_ref[...]

    for b in range(group):
        block = start + step * group + b
        total = None
        for j in range(prec_ref.shape[1]):
            source = table[index_ref[block, j]]
            source = jnp.where(j < count_ref[block], source, jnp.zeros_like(source))
            term = lax.dot_general(
                source, prec_ref[b, j], (((1,), (1,)), ((), ())), preferred_element_type=jnp.float32
            )
            total = term if total is None else total + term
        out_ref[b] = total.astype(out_ref.dtype)


def pedigree(blocked, incoming, rel_index, rel_count, rel_prec, start, count):
    block_total, share, _ = blocked.shape
    far_total = incoming.shape[0]
    slots = rel_prec.shape[1]
    group = divisor(math.gcd(count, start), 1, 6)
    first = start // group
    return pl.pallas_call(
        functools.partial(pedigree_kernel, group, block_total, start),
        grid_spec=pltpu.PrefetchScalarGridSpec(
            num_scalar_prefetch=2,
            grid=(count // group,),
            in_specs=[
                pl.BlockSpec((block_total, share, BLK), lambda i, *_: (0, 0, 0), pipeline_mode=pl.Buffered(1)),
                pl.BlockSpec((far_total, share, BLK), lambda i, *_: (0, 0, 0), pipeline_mode=pl.Buffered(1)),
                pl.BlockSpec((group, slots, BLK, BLK), lambda i, *_: (first + i, 0, 0, 0)),
            ],
            out_specs=pl.BlockSpec((group, share, BLK), lambda i, *_: (i, 0, 0)),
            scratch_shapes=[pltpu.VMEM((block_total + far_total, share, BLK), jnp.bfloat16)],
        ),
        out_shape=jax.ShapeDtypeStruct((count, share, BLK), jnp.bfloat16),
        compiler_params=pltpu.CompilerParams(vmem_limit_bytes=VMEM_LIMIT),
        name="pedigree",
    )(rel_index, rel_count, blocked, incoming, rel_prec)


def origin_share(devices, place, origin):
    away, middle = place - origin, devices // 2
    if away == 0:
        return "own"
    if abs(away) < middle:
        return ("near", away)
    return ("far", abs(away))


def spread(value, devices):
    middle = devices // 2
    everyone = range(devices)

    def send(what, pairs):
        return lax.ppermute(what, "marker", pairs)

    found = {"own": value}
    found["far", middle] = send(value, [(d, (d + middle) % devices) for d in everyone])
    for away in range(1, middle):
        found["near", away] = send(value, [(d, d + away) for d in everyone if d + away < devices])
        found["near", -away] = send(value, [(d, d - away) for d in everyone if d >= away])
    for more in range(1, devices - middle):
        up = [(d, d + more) for d in range(middle, devices) if d + more < devices]
        down = [(d, d - more) for d in range(middle) if d >= more]
        found["far", middle + more] = send(found["far", middle], up + down)
    return found


def backward_kernel(scale, devices, lanes, keys, place_ref, *refs):
    geno, refs = refs[:lanes], refs[lanes:]
    shares, refs = dict(zip(keys, refs)), refs[len(keys) :]
    sums, (out_ref, effects) = refs[:-2], refs[-2:]
    blocks = shares["own"].shape[0]

    @pl.when(pl.program_id(0) == 0)
    def _():
        for b in range(blocks):
            pieces = []
            for origin in range(devices):
                piece = shares[origin_share(devices, 0, origin)][b]
                for place in range(1, devices):
                    other = shares[origin_share(devices, place, origin)][b]
                    piece = jnp.where(place_ref[0] == place, other, piece)
                pieces.append(piece)
            effects[b * BLK : (b + 1) * BLK, :] = jnp.concatenate(pieces, axis=0).T

    for lane, geno_ref in enumerate(geno):
        tile = geno_ref.shape[1]
        rows = slice(lane * tile, (lane + 1) * tile)
        product = scale * lax.dot_general(
            geno_ref[...], effects[...], (((0,), (0,)), ((), ())), preferred_element_type=jnp.float32
        )
        for earlier in sums:
            product = product + earlier[rows, :]
        out_ref[rows, :] = product.astype(out_ref.dtype)


def backward_product(genotypes, shares, place, devices, scale, part, kind, sums=()):
    width = genotypes.shape[1]
    keys = list(shares)
    own = shares["own"]
    rows = own.shape[0] * BLK
    cols = devices * own.shape[1]
    lanes = 2 if width % (2 * BLK) == 0 else 1
    tile = divisor(width // lanes, BLK, 5 * BLK)
    out = pl.BlockSpec((lanes * tile, cols), lambda i, *_: (i, 0))
    return pl.pallas_call(
        functools.partial(backward_kernel, scale, devices, lanes, keys),
        grid_spec=pltpu.PrefetchScalarGridSpec(
            num_scalar_prefetch=1,
            grid=(width // (lanes * tile),),
            in_specs=[pl.BlockSpec((rows, tile), lambda i, *_, k=k: (part, lanes * i + k)) for k in range(lanes)]
            + [pl.BlockSpec(own.shape, lambda i, *_: (0, 0, 0), pipeline_mode=pl.Buffered(1))] * len(keys)
            + [out] * len(sums),
            out_specs=out,
            scratch_shapes=[pltpu.VMEM((rows, cols), jnp.bfloat16)],
        ),
        out_shape=jax.ShapeDtypeStruct((width, cols), kind),
        compiler_params=pltpu.CompilerParams(vmem_limit_bytes=VMEM_LIMIT),
        cost_estimate=pl.CostEstimate(
            flops=2 * rows * width * cols,
            bytes_accessed=2 * rows * (width + cols) + 4 * width * cols * (2 if sums else 1),
            transcendentals=0,
        ),
        name="backward_product",
    )(place, *[genotypes] * lanes, *[shares[key] for key in keys], *sums)


def scatter_sum(blocks, devices):
    here = lax.axis_index("animal")
    core, chip = here & 1, here >> 1
    pairs = blocks.reshape((devices // 2, 2) + blocks.shape[1:])
    sent = lax.dynamic_index_in_dim(pairs, 1 - core, 1, keepdims=False)
    kept = lax.dynamic_index_in_dim(pairs, core, 1, keepdims=False)
    got = lax.ppermute(sent, "animal", [(d, d ^ 1) for d in range(devices)])

    def total(owner):
        return sum(
            lax.dynamic_index_in_dim(term, owner, 0, keepdims=False).astype(jnp.float32) for term in (kept, got)
        )

    arrived = [
        lax.ppermute(
            total(chip ^ away).astype(blocks.dtype), "animal", [(d, d ^ (2 * away)) for d in range(devices)]
        )
        for away in range(devices // 2 - 1, 0, -1)
    ]
    return total(chip) + sum(value.astype(jnp.float32) for value in arrived)


def local(genotypes, direction, ridge, send_list, rel_index, rel_count, rel_prec):
    rows, width = genotypes.shape
    groups = lax.axis_size("animal")
    devices = lax.axis_size("marker")
    place = lax.axis_index("marker").reshape(1)
    parts = 2
    part_rows = rows // parts
    tile = divisor(part_rows, BLK, 4 * BLK)

    owns, coded = [], []
    for part in range(parts):
        own, sent = forward_product(
            genotypes, direction, place, devices, 1.0 / math.sqrt(MARKERS), part * part_rows, part_rows, tile
        )
        if part > 0:
            sent, coded[-1] = lax.optimization_barrier((sent, coded[-1]))
        owns.append(own)
        coded.append(lax.all_to_all(sent, "marker", split_axis=0, concat_axis=0, tiled=True))
    own, outgoing = settle(owns, coded, send_list, place, tile // BLK)

    share = own.shape[1]
    outgoing = outgoing.reshape(groups, -1, share, BLK)
    incoming = lax.all_to_all(outgoing, "animal", split_axis=0, concat_axis=0, tiled=True)
    incoming = incoming.reshape(-1, share, BLK)
    part_blocks = part_rows // BLK
    shares = []
    for part in range(parts):
        relative = pedigree(own, incoming, rel_index, rel_count, rel_prec, part * part_blocks, part_blocks)
        shares.append(spread(relative, devices))

    own_rows = width // groups
    scale = 1.0 / math.sqrt(groups * rows)
    sums = ()
    for part in range(parts):
        kind = jnp.float32 if part < parts - 1 else jnp.bfloat16
        sums = (backward_product(genotypes, shares[part], place, devices, scale, part, kind, sums),)
    gradient = scatter_sum(sums[0].reshape(groups, own_rows, -1), groups)
    start = lax.axis_index("animal") * own_rows
    own_ridge = lax.dynamic_slice_in_dim(ridge, start, own_rows, 0)
    own_direction = lax.dynamic_slice_in_dim(direction, start, own_rows, 0)
    return gradient + own_ridge[:, None] * own_direction.astype(jnp.float32)


def solution(mesh):
    in_specs = (
        P("animal", "marker"),
        P("marker", None),
        P("marker"),
        P("animal", None, None),
        P("animal", None),
        P("animal"),
        P("animal", None, None, None),
    )
    out_specs = P(("marker", "animal"), None)
    return jax.shard_map(local, mesh=mesh, in_specs=in_specs, out_specs=out_specs, check_vma=False)
```

time: 161 us -> 174 us (1.081)
  the two profiles are of different devices: /device:TPU:8 before, /device:TPU:0 now
where the time goes in v4:
time: 174 us; the launch traced here: 173 us
  waiting for transfers between devices  63.7 us (37%)
  Pallas kernels  63.5 us (36%)
  starting transfers between devices  31.6 us (18%)
  local copies, waits for them, and re-layouts  8.74 us (5%)
  other arithmetic  5.16 us (3%)
    all_to_all x2, waiting for transfers between devices, local(): lax.all_to_all(sent, 'marker', split_axis=0, concat_axis=0, tiled=True)  29.2 us
    pallas_call x2, Pallas kernels, backward_product(): pl.pallas_call(functools.partial(backward_kernel, scale, devices, lanes,...  27.9 us
    pallas_call x2, Pallas kernels, forward_product(): pl.pallas_call(functools.partial(forward_kernel, scale, devices), grid_sp...  23.7 us
    ppermute x3, waiting for transfers between devices, scatter_sum(): lax.ppermute(total(chip ^ away).astype(blocks.dtype), 'animal', [(d, d ^...  17.5 us
    ppermute x8, starting transfers between devices, send(): return lax.ppermute(what, 'marker', pairs)  14.5 us
    all_to_all x2, starting transfers between devices, local(): lax.all_to_all(sent, 'marker', split_axis=0, concat_axis=0, tiled=True)  9.82 us
    pallas_call x2, Pallas kernels, pedigree(): pl.pallas_call(functools.partial(pedigree_kernel, group, block_total, sta...  8.25 us
    ppermute x8, waiting for transfers between devices, send(): return lax.ppermute(what, 'marker', pairs)  6.8 us
  transfers between devices with their start and end apart: 15, of which 10 were waited for; matrix products, arithmetic and copies ran while one was open for 1% of the time, Pallas kernels for 17%

profile of v4, /device:TPU:0, one launch (start us, length us, event | category | flops | bytes accessed | tf_op | source)
XLA Modules:
  0.0 172.8 jit_solution(2100192839809495832)
XLA Ops:
  0.0 11.8 %forward_product.2 = (f32[12,64,128]{2,1,0:T(8,128)}, s16[4,816,128]{2,1,0:T(8,128)(2,1)}) custom-call(s32[1]{0:T(128)} %bitcast.place_ref, bf16[3072,6400]{1,0:T(8,128)(2,1)} %refs_1_.3, bf16[3072,6400]{1,0:T(8,128)(2,1)} %refs_1_.3, bf16[6400,256]{1,0:T(8,128)(2,1)} %direction_ref.3), custom_call_target="tpu_custom_call" | custom-call | flops 5033164800 | bytes 23724032 | tf_op jit(solution)/shard_map/forward_product/pallas_call | solution.py:58
  11.8 6.3 %all-to-all-start = ((s16[4,816,128]{2,1,0:T(8,128)(2,1)}), s16[4,816,128]{2,1,0:T(8,128)(2,1)S(1)}, u32[]{:S(2)}, u32[]{:S(2)}) async-start(s16[4,816,128]{2,1,0:T(8,128)(2,1)} %get-tuple-element.16), calls=%async_computation | async-start | bytes 1671168 | tf_op jit(solution)/shard_map/all_to_all | solution.py:305
  18.2 11.9 %forward_product.3 = (f32[12,64,128]{2,1,0:T(8,128)}, s16[4,816,128]{2,1,0:T(8,128)(2,1)}) custom-call(s32[1]{0:T(128)} %bitcast.place_ref, bf16[3072,6400]{1,0:T(8,128)(2,1)} %refs_1_.3, bf16[3072,6400]{1,0:T(8,128)(2,1)} %refs_1_.3, bf16[6400,256]{1,0:T(8,128)(2,1)} %direction_ref.3), custom_call_target="tpu_custom_call" | custom-call | flops 5033164800 | bytes 23724032 | tf_op jit(solution)/shard_map/forward_product/pallas_call | solution.py:58
  30.0 9.3 %all-to-all-done.refs_2_ = s16[4,816,128]{2,1,0:T(8,128)(2,1)S(1)} async-done(((s16[4,816,128]{2,1,0:T(8,128)(2,1)}), s16[4,816,128]{2,1,0:T(8,128)(2,1)S(1)}, u32[]{:S(2)}, u32[]{:S(2)}) %all-to-all-start) | async-done | bytes 835616 | tf_op jit(solution)/shard_map/all_to_all | solution.py:305
  39.3 3.5 %all-to-all-start.1 = ((s16[4,816,128]{2,1,0:T(8,128)(2,1)}), s16[4,816,128]{2,1,0:T(8,128)(2,1)S(1)}, u32[]{:S(2)}, u32[]{:S(2)}) async-start(s16[4,816,128]{2,1,0:T(8,128)(2,1)} %get-tuple-element.18), calls=%async_computation.1 | async-start | bytes 1671168 | tf_op jit(solution)/shard_map/all_to_all | solution.py:305
  42.8 0.0 copy-done.14
  42.8 0.1 copy.11
  42.9 0.6 reshape.38.list_ref
  43.5 20.0 %all-to-all-done.1.refs_3_ = s16[4,816,128]{2,1,0:T(8,128)(2,1)S(1)} async-done(((s16[4,816,128]{2,1,0:T(8,128)(2,1)}), s16[4,816,128]{2,1,0:T(8,128)(2,1)S(1)}, u32[]{:S(2)}, u32[]{:S(2)}) %all-to-all-start.1) | async-done | bytes 835616 | tf_op jit(solution)/shard_map/all_to_all | solution.py:305
  63.5 0.0 copy-done.1
  63.5 0.9 copy-done.2
  64.4 3.7 %settle.1 = (bf16[24,64,128]{2,1,0:T(8,128)(2,1)}, bf16[16,64,128]{2,1,0:T(8,128)(2,1)}) custom-call(s32[16]{0:T(128)} %reshape.38.list_ref, s32[1]{0:T(128)} %bitcast.place_ref, f32[12,64,128]{2,1,0:T(8,128)} %get-tuple-element.13.refs_0_, f32[12,64,128]{2,1,0:T(8,128)} %get-tuple-element.14.refs_1_, s16[4,816,128]{2,1,0:T(8,128)(2,1)} %copy-done.1, ...), custom_call_target="tpu_custom_call" | custom-call | tf_op jit(solution)/shard_map/settle/pallas_call | solution.py:112
  68.0 3.7 %all-to-all-start.2 = ((bf16[8,2,64,128]{3,2,1,0:T(8,128)(2,1)}), bf16[8,2,64,128]{3,2,1,0:T(8,128)(2,1)S(1)}, u32[]{:S(2)}, u32[]{:S(2)}) async-start(bf16[8,2,64,128]{3,2,1,0:T(8,128)(2,1)} %bitcast.35), calls=%async_computation.2 | async-start | bytes 524288 | tf_op jit(solution)/shard_map/all_to_all | solution.py:310
  71.7 0.0 copy-done.13
  71.8 0.7 copy.12.index_ref
  72.4 6.2 %all-to-all-done.2 = bf16[8,2,64,128]{3,2,1,0:T(8,128)(2,1)S(1)} async-done(((bf16[8,2,64,128]{3,2,1,0:T(8,128)(2,1)}), bf16[8,2,64,128]{3,2,1,0:T(8,128)(2,1)S(1)}, u32[]{:S(2)}, u32[]{:S(2)}) %all-to-all-start.2) | async-done | bytes 262176 | tf_op jit(solution)/shard_map/all_to_all | solution.py:310
  78.7 0.7 copy-done.3
  79.4 4.1 %pedigree.3.refs_2_ = bf16[12,64,128]{2,1,0:T(8,128)(2,1)} custom-call(s32[24,4]{1,0:T(8,128)} %copy.12.index_ref, s32[24]{0:T(128)} %count_ref.3, bf16[24,64,128]{2,1,0:T(8,128)(2,1)} %get-tuple-element.19.own_ref, bf16[16,64,128]{2,1,0:T(8,128)(2,1)} %bitcast.33, bf16[24,4,128,128]{3,2,1,0:T(8,128)(2,1)} %prec_ref.3), custom_call_target="tpu_custom_call" | custom-call | tf_op jit(solution)/shard_map/pedigree/pallas_call | solution.py:159
  83.5 0.0 collective-permute-start.4
  83.5 3.9 %collective-permute-start.5 = (bf16[12,64,128]{2,1,0:T(8,128)(2,1)}, bf16[12,64,128]{2,1,0:T(8,128)(2,1)S(1)}, u32[]{:S(2)}, u32[]{:S(2)}) collective-permute-start(bf16[12,64,128]{2,1,0:T(8,128)(2,1)} %pedigree.3.refs_2_), channel_id=1, source_target_pairs={{0,1},{1,2},{2,3},{4,5},{5,6},{6,7},{8,9},{9,10},{10,11},{12,13},{... | collective-permute-start | bytes 589832 | tf_op jit(solution)/shard_map/ppermute | solution.py:192
  87.4 4.1 %pedigree.2.refs_2_ = bf16[12,64,128]{2,1,0:T(8,128)(2,1)} custom-call(s32[24,4]{1,0:T(8,128)} %copy.12.index_ref, s32[24]{0:T(128)} %count_ref.3, bf16[24,64,128]{2,1,0:T(8,128)(2,1)} %get-tuple-element.19.own_ref, bf16[16,64,128]{2,1,0:T(8,128)(2,1)} %bitcast.34, bf16[24,4,128,128]{3,2,1,0:T(8,128)(2,1)} %prec_ref.3), custom_call_target="tpu_custom_call" | custom-call | tf_op jit(solution)/shard_map/pedigree/pallas_call | solution.py:159
  91.6 0.9 collective-permute-start
  92.5 0.0 copy-done.4
  92.5 1.3 collective-permute-start.6
  93.8 0.0 collective-permute-done.4.refs_3_
  93.8 0.0 copy-start.6
  93.8 1.3 collective-permute-start.7
  95.1 4.6 %collective-permute-start.1 = (bf16[12,64,128]{2,1,0:T(8,128)(2,1)}, bf16[12,64,128]{2,1,0:T(8,128)(2,1)S(1)}, u32[]{:S(2)}, u32[]{:S(2)}) collective-permute-start(bf16[12,64,128]{2,1,0:T(8,128)(2,1)} %pedigree.2.refs_2_), channel_id=1, source_target_pairs={{0,1},{1,2},{2,3},{4,5},{5,6},{6,7},{8,9},{9,10},{10,11},{12,13},{... | collective-permute-start | bytes 589832 | tf_op jit(solution)/shard_map/ppermute | solution.py:192
  99.7 0.0 collective-permute-done.5.refs_4_
  99.7 0.0 copy-start.7
  99.7 1.3 collective-permute-start.2
  101.0 2.4 %collective-permute-done.refs_3_ = bf16[12,64,128]{2,1,0:T(8,128)(2,1)S(1)} collective-permute-done((bf16[12,64,128]{2,1,0:T(8,128)(2,1)}, bf16[12,64,128]{2,1,0:T(8,128)(2,1)S(1)}, u32[]{:S(2)}, u32[]{:S(2)}) %collective-permute-start) | collective-permute-done | bytes 196640 | tf_op jit(solution)/shard_map/ppermute | solution.py:192
  103.4 1.3 collective-permute-start.3
  104.7 0.2 collective-permute-done.6.refs_5_
  104.9 4.2 %collective-permute-done.7.refs_6_ = bf16[12,64,128]{2,1,0:T(8,128)(2,1)S(1)} collective-permute-done((bf16[12,64,128]{2,1,0:T(8,128)(2,1)S(1)}, bf16[12,64,128]{2,1,0:T(8,128)(2,1)S(1)}, u32[]{:S(2)}, u32[]{:S(2)}) %collective-permute-start.7) | collective-permute-done | bytes 196640 | tf_op jit(solution)/shard_map/ppermute | solution.py:192
  109.1 0.0 copy-done.6
  109.1 0.0 copy-done.7
  109.1 0.0 copy-done.8
  109.1 0.0 copy-start.9
  109.1 0.7 copy-done.9
  109.8 13.6 %backward_product.2.refs_7_ = f32[6400,256]{1,0:T(8,128)} custom-call(s32[1]{0:T(128)} %bitcast.place_ref, bf16[3072,6400]{1,0:T(8,128)(2,1)} %refs_1_.3, bf16[3072,6400]{1,0:T(8,128)(2,1)} %refs_1_.3, bf16[12,64,128]{2,1,0:T(8,128)(2,1)} %pedigree.3.refs_2_, bf16[12,64,128]{2,1,0:T(8,128)(2,1)} %copy-done.6, bf16[12,64,128]{2,1,0:T(8,128)(2,1)} %copy-done.7, ...), custom_call_target="tpu_custom_call" | custom-call | flops 5033164800 | bytes 27000832 | tf_op jit(solution)/shard_map/backward_product/pallas_call | solution.py:244
  123.4 0.0 copy-done.5
  123.4 0.0 collective-permute-done.1.refs_4_
  123.4 0.0 copy-start.10
  123.4 0.0 collective-permute-done.2.refs_5_
  123.4 0.0 copy-start.11
  123.5 0.0 collective-permute-done.3.refs_6_
  123.5 0.6 copy-done.10
  124.1 0.1 copy-done.11
  124.2 0.7 copy-done.12
  124.9 14.2 %backward_product.3 = bf16[6400,256]{1,0:T(8,128)(2,1)} custom-call(s32[1]{0:T(128)} %bitcast.place_ref, bf16[3072,6400]{1,0:T(8,128)(2,1)} %refs_1_.3, bf16[3072,6400]{1,0:T(8,128)(2,1)} %refs_1_.3, bf16[12,64,128]{2,1,0:T(8,128)(2,1)} %pedigree.2.refs_2_, bf16[12,64,128]{2,1,0:T(8,128)(2,1)} %copy-done.5, bf16[12,64,128]{2,1,0:T(8,128)(2,1)} %copy-done.10, ...), custom_call_target="tpu_custom_call" | custom-call | flops 5033164800 | bytes 33554432 | tf_op jit(solution)/shard_map/backward_product/pallas_call | solution.py:244
  139.1 2.9 %dynamic-slice_bitcast_fusion = bf16[4,800,256]{2,1,0:T(8,128)(2,1)} fusion(bf16[4,2,800,256]{3,2,1,0:T(8,128)(2,1)} %bitcast.30, s32[]{:T(128)S(6)} %select_n.42), kind=kLoop, calls=%fused_computation | loop fusion | bytes 3276804 | tf_op jit(solution)/shard_map/jit(dynamic_index_in_dim)/squeeze | solution.py:270
  142.0 0.0 collective-permute-start.8
  142.0 3.8 %collective-permute-done.8 = bf16[4,800,256]{2,1,0:T(8,128)(2,1)} collective-permute-done((bf16[4,800,256]{2,1,0:T(8,128)(2,1)}, bf16[4,800,256]{2,1,0:T(8,128)(2,1)}, u32[]{:S(2)}, u32[]{:S(2)}) %collective-permute-start.8) | collective-permute-done | bytes 1638432 | tf_op jit(solution)/shard_map/ppermute | solution.py:272
  145.8 0.0 copy-done
  145.8 2.4 %fusion.2 = (bf16[800,256]{1,0:T(8,128)(2,1)}, bf16[800,256]{1,0:T(8,128)(2,1)}, bf16[800,256]{1,0:T(8,128)(2,1)}) fusion(bf16[4,800,256]{2,1,0:T(8,128)(2,1)} %collective-permute-done.8, s32[]{:T(128)S(6)} %select_n.43, bf16[4,2,800,256]{3,2,1,0:T(8,128)(2,1)S(1)} %bitcast.31, s32[]{:T(128)S(6)} %select_n.44, s32[]{:T(128)S(6)} %select_n.41, ...), kind=kLoop, calls=%fused_computation.6 | loop fusion | flops 2457600 | bytes 3686428 | tf_op jit(solution)/shard_map/convert_element_type | solution.py:281
  148.3 0.6 collective-permute-start.10
  148.9 1.1 collective-permute-start.11
  150.0 1.8 %collective-permute-start.9 = (bf16[800,256]{1,0:T(8,128)(2,1)}, bf16[800,256]{1,0:T(8,128)(2,1)}, u32[]{:S(2)}, u32[]{:S(2)}) collective-permute-start(bf16[800,256]{1,0:T(8,128)(2,1)} %get-tuple-element.21), channel_id=1, source_target_pairs={{0,24},{4,28},{8,16},{12,20},{16,8},{20,12},{24,0},{28,4},{1,25},{... | collective-permute-start | bytes 1228808 | tf_op jit(solution)/shard_map/ppermute | solution.py:280
  151.8 0.8 dynamic_slice.45
  152.6 7.6 %collective-permute-done.10 = bf16[800,256]{1,0:T(8,128)(2,1)} collective-permute-done((bf16[800,256]{1,0:T(8,128)(2,1)}, bf16[800,256]{1,0:T(8,128)(2,1)}, u32[]{:S(2)}, u32[]{:S(2)}) %collective-permute-start.10) | collective-permute-done | bytes 409632 | tf_op jit(solution)/shard_map/ppermute | solution.py:280
  160.1 1.4 collective-permute-done.11
  161.5 8.6 %collective-permute-done.9 = bf16[800,256]{1,0:T(8,128)(2,1)} collective-permute-done((bf16[800,256]{1,0:T(8,128)(2,1)}, bf16[800,256]{1,0:T(8,128)(2,1)}, u32[]{:S(2)}, u32[]{:S(2)}) %collective-permute-start.9) | collective-permute-done | bytes 409632 | tf_op jit(solution)/shard_map/ppermute | solution.py:280
  170.1 2.7 %fusion.4 = f32[800,256]{1,0:T(8,128)} fusion(bf16[800,256]{1,0:T(8,128)(2,1)} %collective-permute-done.11, bf16[800,256]{1,0:T(8,128)(2,1)} %collective-permute-done.10, bf16[800,256]{1,0:T(8,128)(2,1)} %collective-permute-done.9, bf16[6400,256]{1,0:T(8,128)(2,1)} %direction_ref.3, s32[]{:T(128)S(6)} %select_n.49, f32[800]{0:T(1024)S(1)} %dynamic_slice.45, ...), kind=kLoop, calls=%fused_computation.9 | loop fusion | flops 2457600 | bytes 3280016 | tf_op jit(solution)/shard_map/add | solution.py:328
  (10 shorter events, 0.0 us)
Async XLA Ops:
  11.8 27.5 %all-to-all-start = ((s16[4,816,128]{2,1,0:T(8,128)(2,1)}), s16[4,816,128]{2,1,0:T(8,128)(2,1)S(1)}, u32[]{:S(2)}, u32[]{:S(2)}) async-start(s16[4,816,128]{2,1,0:T(8,128)(2,1)} %get-tuple-element.16), calls=%async_computation | async-start | bytes 1671168 | tf_op jit(solution)/shard_map/all_to_all | solution.py:305
  18.1 24.7 %copy-start.14 = (s32[1,8,2]{1,2,0:T(2,128)S(1)}, s32[1,8,2]{1,2,0:T(2,128)}, u32[]{:S(2)}) copy-start(s32[1,8,2]{1,2,0:T(2,128)} %param.10) | copy-start | bytes 196
  30.0 41.7 %copy-start.13 = (s32[24,4]{0,1:T(4,128)S(1)}, s32[24,4]{0,1:T(4,128)}, u32[]{:S(2)}) copy-start(s32[24,4]{0,1:T(4,128)} %param.11) | copy-start | bytes 1156
  39.3 24.1 %copy-start.1 = (s16[4,816,128]{2,1,0:T(8,128)(2,1)}, s16[4,816,128]{2,1,0:T(8,128)(2,1)S(1)}, u32[]{:S(2)}) copy-start(s16[4,816,128]{2,1,0:T(8,128)(2,1)S(1)} %all-to-all-done.refs_2_) | copy-start | bytes 2506756
  39.3 24.1 %all-to-all-start.1 = ((s16[4,816,128]{2,1,0:T(8,128)(2,1)}), s16[4,816,128]{2,1,0:T(8,128)(2,1)S(1)}, u32[]{:S(2)}, u32[]{:S(2)}) async-start(s16[4,816,128]{2,1,0:T(8,128)(2,1)} %get-tuple-element.18), calls=%async_computation.1 | async-start | bytes 1671168 | tf_op jit(solution)/shard_map/all_to_all | solution.py:305
  63.5 0.9 copy-start.2
  68.0 10.7 %all-to-all-start.2 = ((bf16[8,2,64,128]{3,2,1,0:T(8,128)(2,1)}), bf16[8,2,64,128]{3,2,1,0:T(8,128)(2,1)S(1)}, u32[]{:S(2)}, u32[]{:S(2)}) async-start(bf16[8,2,64,128]{3,2,1,0:T(8,128)(2,1)} %bitcast.35), calls=%async_computation.2 | async-start | bytes 524288 | tf_op jit(solution)/shard_map/all_to_all | solution.py:310
  78.7 0.7 copy-start.3
  83.5 9.0 %copy-start.4 = (bf16[12,64,128]{2,1,0:T(8,128)(2,1)S(1)}, bf16[12,64,128]{2,1,0:T(8,128)(2,1)}, u32[]{:S(2)}) copy-start(bf16[12,64,128]{2,1,0:T(8,128)(2,1)} %pedigree.3.refs_2_) | copy-start | bytes 589828
  83.5 10.3 %collective-permute-start.4 = (bf16[12,64,128]{2,1,0:T(8,128)(2,1)}, bf16[12,64,128]{2,1,0:T(8,128)(2,1)S(1)}, u32[]{:S(2)}, u32[]{:S(2)}) collective-permute-start(bf16[12,64,128]{2,1,0:T(8,128)(2,1)} %pedigree.3.refs_2_), channel_id=1, source_target_pairs={{0,2},{1,3},{2,0},{3,1},{4,6},{5,7},{6,4},{7,5},{8,10},{9,11},{10,... | collective-permute-start | bytes 589832 | tf_op jit(solution)/shard_map/ppermute | solution.py:192
  83.5 16.2 %collective-permute-start.5 = (bf16[12,64,128]{2,1,0:T(8,128)(2,1)}, bf16[12,64,128]{2,1,0:T(8,128)(2,1)S(1)}, u32[]{:S(2)}, u32[]{:S(2)}) collective-permute-start(bf16[12,64,128]{2,1,0:T(8,128)(2,1)} %pedigree.3.refs_2_), channel_id=1, source_target_pairs={{0,1},{1,2},{2,3},{4,5},{5,6},{6,7},{8,9},{9,10},{10,11},{12,13},{... | collective-permute-start | bytes 589832 | tf_op jit(solution)/shard_map/ppermute | solution.py:192
  91.6 11.8 %collective-permute-start = (bf16[12,64,128]{2,1,0:T(8,128)(2,1)}, bf16[12,64,128]{2,1,0:T(8,128)(2,1)S(1)}, u32[]{:S(2)}, u32[]{:S(2)}) collective-permute-start(bf16[12,64,128]{2,1,0:T(8,128)(2,1)} %pedigree.2.refs_2_), channel_id=1, source_target_pairs={{0,2},{1,3},{2,0},{3,1},{4,6},{5,7},{6,4},{7,5},{8,10},{9,11},{10,... | collective-permute-start | bytes 589832 | tf_op jit(solution)/shard_map/ppermute | solution.py:192
  92.5 12.4 %collective-permute-start.6 = (bf16[12,64,128]{2,1,0:T(8,128)(2,1)S(1)}, bf16[12,64,128]{2,1,0:T(8,128)(2,1)S(1)}, u32[]{:S(2)}, u32[]{:S(2)}) collective-permute-start(bf16[12,64,128]{2,1,0:T(8,128)(2,1)S(1)} %copy-done.4), channel_id=1, source_target_pairs={{1,0},{2,1},{3,2},{5,4},{6,5},{7,6},{9,8},{10,9},{11,10},{13,12},{... | collective-permute-start | bytes 589832 | tf_op jit(solution)/shard_map/ppermute | solution.py:192
  93.8 15.3 %copy-start.6 = (bf16[12,64,128]{2,1,0:T(8,128)(2,1)}, bf16[12,64,128]{2,1,0:T(8,128)(2,1)S(1)}, u32[]{:S(2)}) copy-start(bf16[12,64,128]{2,1,0:T(8,128)(2,1)S(1)} %collective-permute-done.4.refs_3_) | copy-start | bytes 589828
  93.8 15.3 %collective-permute-start.7 = (bf16[12,64,128]{2,1,0:T(8,128)(2,1)S(1)}, bf16[12,64,128]{2,1,0:T(8,128)(2,1)S(1)}, u32[]{:S(2)}, u32[]{:S(2)}) collective-permute-start(bf16[12,64,128]{2,1,0:T(8,128)(2,1)S(1)} %collective-permute-done.4.refs_3_), channel_id=1, source_target_pairs={{2,3},{1,0},{6,7},{5,4},{10,11},{9,8},{14,15},{13,12},{18,19},{17,... | collective-permute-start | bytes 589832 | tf_op jit(solution)/shard_map/ppermute | solution.py:192
  95.1 28.3 %collective-permute-start.1 = (bf16[12,64,128]{2,1,0:T(8,128)(2,1)}, bf16[12,64,128]{2,1,0:T(8,128)(2,1)S(1)}, u32[]{:S(2)}, u32[]{:S(2)}) collective-permute-start(bf16[12,64,128]{2,1,0:T(8,128)(2,1)} %pedigree.2.refs_2_), channel_id=1, source_target_pairs={{0,1},{1,2},{2,3},{4,5},{5,6},{6,7},{8,9},{9,10},{10,11},{12,13},{... | collective-permute-start | bytes 589832 | tf_op jit(solution)/shard_map/ppermute | solution.py:192
  99.7 9.4 %copy-start.7 = (bf16[12,64,128]{2,1,0:T(8,128)(2,1)}, bf16[12,64,128]{2,1,0:T(8,128)(2,1)S(1)}, u32[]{:S(2)}) copy-start(bf16[12,64,128]{2,1,0:T(8,128)(2,1)S(1)} %collective-permute-done.5.refs_4_) | copy-start | bytes 589828
  99.7 23.7 %collective-permute-start.2 = (bf16[12,64,128]{2,1,0:T(8,128)(2,1)}, bf16[12,64,128]{2,1,0:T(8,128)(2,1)S(1)}, u32[]{:S(2)}, u32[]{:S(2)}) collective-permute-start(bf16[12,64,128]{2,1,0:T(8,128)(2,1)} %pedigree.2.refs_2_), channel_id=1, source_target_pairs={{1,0},{2,1},{3,2},{5,4},{6,5},{7,6},{9,8},{10,9},{11,10},{13,12},{... | collective-permute-start | bytes 589832 | tf_op jit(solution)/shard_map/ppermute | solution.py:192
  103.4 20.0 %copy-start.5 = (bf16[12,64,128]{2,1,0:T(8,128)(2,1)}, bf16[12,64,128]{2,1,0:T(8,128)(2,1)S(1)}, u32[]{:S(2)}) copy-start(bf16[12,64,128]{2,1,0:T(8,128)(2,1)S(1)} %collective-permute-done.refs_3_) | copy-start | bytes 589828
  103.4 20.1 %collective-permute-start.3 = (bf16[12,64,128]{2,1,0:T(8,128)(2,1)S(1)}, bf16[12,64,128]{2,1,0:T(8,128)(2,1)S(1)}, u32[]{:S(2)}, u32[]{:S(2)}) collective-permute-start(bf16[12,64,128]{2,1,0:T(8,128)(2,1)S(1)} %collective-permute-done.refs_3_), channel_id=1, source_target_pairs={{2,3},{1,0},{6,7},{5,4},{10,11},{9,8},{14,15},{13,12},{18,19},{17,... | collective-permute-start | bytes 589832 | tf_op jit(solution)/shard_map/ppermute | solution.py:192
  104.9 4.2 %copy-start.8 = (bf16[12,64,128]{2,1,0:T(8,128)(2,1)}, bf16[12,64,128]{2,1,0:T(8,128)(2,1)S(1)}, u32[]{:S(2)}) copy-start(bf16[12,64,128]{2,1,0:T(8,128)(2,1)S(1)} %collective-permute-done.6.refs_5_) | copy-start | bytes 589828
  109.1 0.7 copy-start.9
  123.4 0.7 copy-start.10
  123.4 0.8 copy-start.11
  124.2 0.7 copy-start.12
  139.1 6.7 %copy-start = (bf16[6400,256]{1,0:T(8,128)(2,1)S(1)}, bf16[6400,256]{1,0:T(8,128)(2,1)}, u32[]{:S(2)}) copy-start(bf16[6400,256]{1,0:T(8,128)(2,1)} %backward_product.3) | copy-start | bytes 9830404
  142.0 3.8 %collective-permute-start.8 = (bf16[4,800,256]{2,1,0:T(8,128)(2,1)}, bf16[4,800,256]{2,1,0:T(8,128)(2,1)}, u32[]{:S(2)}, u32[]{:S(2)}) collective-permute-start(bf16[4,800,256]{2,1,0:T(8,128)(2,1)} %dynamic-slice_bitcast_fusion), channel_id=1, source_target_pairs={{0,4},{4,0},{8,12},{12,8},{16,20},{20,16},{24,28},{28,24},{1,5},{5... | collective-permute-start | bytes 4915208 | tf_op jit(solution)/shard_map/ppermute | solution.py:272
  148.3 11.8 %collective-permute-start.10 = (bf16[800,256]{1,0:T(8,128)(2,1)}, bf16[800,256]{1,0:T(8,128)(2,1)}, u32[]{:S(2)}, u32[]{:S(2)}) collective-permute-start(bf16[800,256]{1,0:T(8,128)(2,1)} %get-tuple-element.23), channel_id=1, source_target_pairs={{0,16},{4,20},{8,24},{12,28},{16,0},{20,4},{24,8},{28,12},{1,17},{... | collective-permute-start | bytes 1228808 | tf_op jit(solution)/shard_map/ppermute | solution.py:280
  148.9 12.7 %collective-permute-start.11 = (bf16[800,256]{1,0:T(8,128)(2,1)}, bf16[800,256]{1,0:T(8,128)(2,1)}, u32[]{:S(2)}, u32[]{:S(2)}) collective-permute-start(bf16[800,256]{1,0:T(8,128)(2,1)} %get-tuple-element.22), channel_id=1, source_target_pairs={{0,8},{4,12},{8,0},{12,4},{16,24},{20,28},{24,16},{28,20},{1,9},{5... | collective-permute-start | bytes 1228808 | tf_op jit(solution)/shard_map/ppermute | solution.py:280
  150.0 20.1 %collective-permute-start.9 = (bf16[800,256]{1,0:T(8,128)(2,1)}, bf16[800,256]{1,0:T(8,128)(2,1)}, u32[]{:S(2)}, u32[]{:S(2)}) collective-permute-start(bf16[800,256]{1,0:T(8,128)(2,1)} %get-tuple-element.21), channel_id=1, source_target_pairs={{0,24},{4,28},{8,16},{12,20},{16,8},{20,12},{24,0},{28,4},{1,25},{... | collective-permute-start | bytes 1228808 | tf_op jit(solution)/shard_map/ppermute | solution.py:280

commit v5 on v3

--- a/solution.py
+++ b/solution.py
@@ -142,10 +142,10 @@
             source = table[index_ref[block, j]]
             source = jnp.where(j < count_ref[block], source, jnp.zeros_like(source))
             term = lax.dot_general(
-                source, prec_ref[b, j], (((1,), (1,)), ((), ())), preferred_element_type=jnp.float32
+                prec_ref[b, j], source, (((1,), (1,)), ((), ())), preferred_element_type=jnp.float32
             )
             total = term if total is None else total + term
-        out_ref[b] = total.astype(out_ref.dtype)
+        out_ref[b] = total.T.astype(out_ref.dtype)
 
 
 def pedigree(blocked, incoming, rel_index, rel_count, rel_prec, start, count):
@@ -288,7 +288,10 @@
     shares = []
     for part in range(parts):
         relative = pedigree(own, incoming, rel_index, rel_count, rel_prec, part * part_blocks, part_blocks)
-        shares.append([relative] + [turn(relative, devices, shift) for shift in range(1, devices)])
+        part_shares = [relative, turn(relative, devices, 1)]
+        if part > 0:
+            relative, shares[-1] = lax.optimization_barrier((relative, shares[-1]))
+        shares.append(part_shares + [turn(relative, devices, shift) for shift in range(2, devices)])
 
     own_rows = width // groups
     sums = ()

time: 161 us -> 163 us (1.012)
  the two profiles are of different devices: /device:TPU:8 before, /device:TPU:0 now
where the time goes in v5:
time: 163 us; the launch traced here: 162 us
  Pallas kernels  62.2 us (38%)
  starting transfers between devices  41.1 us (25%)
  waiting for transfers between devices  39.9 us (24%)
  other arithmetic  11 us (7%)
  local copies, waits for them, and re-layouts  7.6 us (5%)
    ppermute x12, starting transfers between devices, turn(): lax.ppermute(value, 'marker', [(d, (d + shift) % devices) for d in range(...  33.3 us
    pallas_call x2, Pallas kernels, backward_product(): pl.pallas_call(functools.partial(backward_kernel, scale, devices, lanes),...  27.8 us
    pallas_call x2, Pallas kernels, forward_product(): pl.pallas_call(functools.partial(forward_kernel, scale, devices), grid_sp...  23.5 us
    ppermute x12, waiting for transfers between devices, turn(): lax.ppermute(value, 'marker', [(d, (d + shift) % devices) for d in range(...  20.5 us
    ppermute x6, waiting for transfers between devices, halving_sum(): lax.ppermute(sent, 'animal', [(d, d ^ 1 << bit) for d in range(devices)])  13.1 us
    pallas_call x2, Pallas kernels, pedigree(): pl.pallas_call(functools.partial(pedigree_kernel, group, block_total, sta...  7.51 us
    convert_element_type x4, other arithmetic, halving_sum(): sent = sum((term.astype(jnp.float32) for term in sent)).astype(jnp.bfloat16)  6.64 us
    all_to_all x1, waiting for transfers between devices, local(): lax.all_to_all(outgoing, 'animal', split_axis=0, concat_axis=0, tiled=True)  6.25 us
  transfers between devices with their start and end apart: 19, of which 9 were waited for; matrix products, arithmetic and copies ran while one was open for 7% of the time, Pallas kernels for 18%

profile of v5, /device:TPU:0, one launch (start us, length us, event | category | flops | bytes accessed | tf_op | source)
XLA Modules:
  0.0 161.9 jit_solution(4245462212059885930)
XLA Ops:
  0.0 11.8 %forward_product.2 = (f32[12,64,128]{2,1,0:T(8,128)}, s16[816,128]{1,0:T(8,128)(2,1)}, s16[816,128]{1,0:T(8,128)(2,1)}, s16[816,128]{1,0:T(8,128)(2,1)}) custom-call(s32[1]{0:T(128)} %bitcast.place_ref, bf16[3072,6400]{1,0:T(8,128)(2,1)} %refs_1_.3, bf16[3072,6400]{1,0:T(8,128)(2,1)} %refs_1_.3, bf16[6400,256]{1,0:T(8,128)(2,1)} %direction_ref.3), custom_call_target="tpu_custom_call" | custom-call | flops 5033164800 | bytes 23724032 | tf_op jit(solution)/shard_map/forward_product/pallas_call | solution.py:60
  11.8 3.1 %collective-permute-start = (s16[816,128]{1,0:T(8,128)(2,1)}, s16[816,128]{1,0:T(8,128)(2,1)S(1)}, u32[]{:S(2)}, u32[]{:S(2)}) collective-permute-start(s16[816,128]{1,0:T(8,128)(2,1)} %get-tuple-element.35), channel_id=1, source_target_pairs={{0,1},{1,2},{2,3},{3,0},{4,5},{5,6},{6,7},{7,4},{8,9},{9,10},{10,1... | collective-permute-start | bytes 626696 | tf_op jit(solution)/shard_map/ppermute | solution.py:238
  14.8 2.6 %collective-permute-start.1 = (s16[816,128]{1,0:T(8,128)(2,1)}, s16[816,128]{1,0:T(8,128)(2,1)S(1)}, u32[]{:S(2)}, u32[]{:S(2)}) collective-permute-start(s16[816,128]{1,0:T(8,128)(2,1)} %get-tuple-element.36), channel_id=1, source_target_pairs={{0,2},{1,3},{2,0},{3,1},{4,6},{5,7},{6,4},{7,5},{8,10},{9,11},{10,... | collective-permute-start | bytes 626696 | tf_op jit(solution)/shard_map/ppermute | solution.py:238
  17.4 1.3 collective-permute-start.2
  18.7 11.8 %forward_product.3 = (f32[12,64,128]{2,1,0:T(8,128)}, s16[816,128]{1,0:T(8,128)(2,1)}, s16[816,128]{1,0:T(8,128)(2,1)}, s16[816,128]{1,0:T(8,128)(2,1)}) custom-call(s32[1]{0:T(128)} %bitcast.place_ref, bf16[3072,6400]{1,0:T(8,128)(2,1)} %refs_1_.3, bf16[3072,6400]{1,0:T(8,128)(2,1)} %refs_1_.3, bf16[6400,256]{1,0:T(8,128)(2,1)} %direction_ref.3), custom_call_target="tpu_custom_call" | custom-call | flops 5033164800 | bytes 23724032 | tf_op jit(solution)/shard_map/forward_product/pallas_call | solution.py:60
  30.5 0.0 collective-permute-done.refs_2_
  30.5 0.8 collective-permute-done.1.refs_4_
  31.3 0.0 collective-permute-done.2.refs_6_
  31.3 4.9 %collective-permute-start.3 = (s16[816,128]{1,0:T(8,128)(2,1)}, s16[816,128]{1,0:T(8,128)(2,1)S(1)}, u32[]{:S(2)}, u32[]{:S(2)}) collective-permute-start(s16[816,128]{1,0:T(8,128)(2,1)} %get-tuple-element.39), channel_id=1, source_target_pairs={{0,1},{1,2},{2,3},{3,0},{4,5},{5,6},{6,7},{7,4},{8,9},{9,10},{10,1... | collective-permute-start | bytes 626696 | tf_op jit(solution)/shard_map/ppermute | solution.py:238
  36.3 1.6 %collective-permute-start.4 = (s16[816,128]{1,0:T(8,128)(2,1)}, s16[816,128]{1,0:T(8,128)(2,1)S(1)}, u32[]{:S(2)}, u32[]{:S(2)}) collective-permute-start(s16[816,128]{1,0:T(8,128)(2,1)} %get-tuple-element.41), channel_id=1, source_target_pairs={{0,2},{1,3},{2,0},{3,1},{4,6},{5,7},{6,4},{7,5},{8,10},{9,11},{10,... | collective-permute-start | bytes 626696 | tf_op jit(solution)/shard_map/ppermute | solution.py:238
  37.9 0.7 collective-permute-start.5
  38.6 0.1 copy.12
  38.7 0.7 reshape.70.list_ref
  39.4 4.3 %collective-permute-done.3.refs_3_ = s16[816,128]{1,0:T(8,128)(2,1)S(1)} collective-permute-done((s16[816,128]{1,0:T(8,128)(2,1)}, s16[816,128]{1,0:T(8,128)(2,1)S(1)}, u32[]{:S(2)}, u32[]{:S(2)}) %collective-permute-start.3) | collective-permute-done | bytes 208928 | tf_op jit(solution)/shard_map/ppermute | solution.py:238
  43.7 7.2 %collective-permute-done.4.refs_5_ = s16[816,128]{1,0:T(8,128)(2,1)S(1)} collective-permute-done((s16[816,128]{1,0:T(8,128)(2,1)}, s16[816,128]{1,0:T(8,128)(2,1)S(1)}, u32[]{:S(2)}, u32[]{:S(2)}) %collective-permute-start.4) | collective-permute-done | bytes 208928 | tf_op jit(solution)/shard_map/ppermute | solution.py:238
  50.9 0.0 collective-permute-done.5.refs_7_
  50.9 0.6 copy-done.7
  51.5 0.1 copy-done.8
  51.6 3.4 %settle.1 = (bf16[24,64,128]{2,1,0:T(8,128)(2,1)}, bf16[16,64,128]{2,1,0:T(8,128)(2,1)}) custom-call(s32[16]{0:T(128)} %reshape.70.list_ref, f32[12,64,128]{2,1,0:T(8,128)} %get-tuple-element.30.refs_0_, f32[12,64,128]{2,1,0:T(8,128)} %get-tuple-element.31.refs_1_, s16[816,128]{1,0:T(8,128)(2,1)} %copy-done.3, s16[816,128]{1,0:T(8,128)(2,1)} %copy-done.6, ...), custom_call_target="tpu_custom_call" | custom-call | tf_op jit(solution)/shard_map/settle/pallas_call | solution.py:110
  55.0 3.7 %all-to-all-start = ((bf16[8,2,64,128]{3,2,1,0:T(8,128)(2,1)}), bf16[8,2,64,128]{3,2,1,0:T(8,128)(2,1)S(1)}, u32[]{:S(2)}, u32[]{:S(2)}) async-start(bf16[8,2,64,128]{3,2,1,0:T(8,128)(2,1)} %bitcast.69), calls=%async_computation | async-start | bytes 524288 | tf_op jit(solution)/shard_map/all_to_all | solution.py:285
  58.7 0.7 copy.13.index_ref
  59.4 6.2 %all-to-all-done = bf16[8,2,64,128]{3,2,1,0:T(8,128)(2,1)S(1)} async-done(((bf16[8,2,64,128]{3,2,1,0:T(8,128)(2,1)}), bf16[8,2,64,128]{3,2,1,0:T(8,128)(2,1)S(1)}, u32[]{:S(2)}, u32[]{:S(2)}) %all-to-all-start) | async-done | bytes 262176 | tf_op jit(solution)/shard_map/all_to_all | solution.py:285
  65.7 0.7 copy-done
  66.4 3.7 %pedigree.3.refs_2_ = bf16[12,64,128]{2,1,0:T(8,128)(2,1)} custom-call(s32[24,4]{1,0:T(8,128)} %copy.13.index_ref, s32[24]{0:T(128)} %count_ref.3, bf16[24,64,128]{2,1,0:T(8,128)(2,1)} %get-tuple-element.44.own_ref, bf16[16,64,128]{2,1,0:T(8,128)(2,1)} %bitcast.59, bf16[24,4,128,128]{3,2,1,0:T(8,128)(2,1)} %prec_ref.3), custom_call_target="tpu_custom_call" | custom-call | tf_op jit(solution)/shard_map/pedigree/pallas_call | solution.py:157
  70.1 4.9 %collective-permute-start.7 = (bf16[12,64,128]{2,1,0:T(8,128)(2,1)}, bf16[12,64,128]{2,1,0:T(8,128)(2,1)S(1)}, u32[]{:S(2)}, u32[]{:S(2)}) collective-permute-start(bf16[12,64,128]{2,1,0:T(8,128)(2,1)} %pedigree.3.refs_2_), channel_id=1, source_target_pairs={{0,1},{1,2},{2,3},{3,0},{4,5},{5,6},{6,7},{7,4},{8,9},{9,10},{10,1... | collective-permute-start | bytes 589832 | tf_op jit(solution)/shard_map/ppermute | solution.py:238
  75.0 2.4 %collective-permute-start.8 = (bf16[12,64,128]{2,1,0:T(8,128)(2,1)}, bf16[12,64,128]{2,1,0:T(8,128)(2,1)S(1)}, u32[]{:S(2)}, u32[]{:S(2)}) collective-permute-start(bf16[12,64,128]{2,1,0:T(8,128)(2,1)} %pedigree.3.refs_2_), channel_id=1, source_target_pairs={{0,2},{1,3},{2,0},{3,1},{4,6},{5,7},{6,4},{7,5},{8,10},{9,11},{10,... | collective-permute-start | bytes 589832 | tf_op jit(solution)/shard_map/ppermute | solution.py:238
  77.4 0.0 collective-permute-start.9
  77.4 3.8 %pedigree.2.refs_2_ = bf16[12,64,128]{2,1,0:T(8,128)(2,1)} custom-call(s32[24,4]{1,0:T(8,128)} %copy.13.index_ref, s32[24]{0:T(128)} %count_ref.3, bf16[24,64,128]{2,1,0:T(8,128)(2,1)} %get-tuple-element.44.own_ref, bf16[16,64,128]{2,1,0:T(8,128)(2,1)} %bitcast.60, bf16[24,4,128,128]{3,2,1,0:T(8,128)(2,1)} %prec_ref.3), custom_call_target="tpu_custom_call" | custom-call | tf_op jit(solution)/shard_map/pedigree/pallas_call | solution.py:157
  81.2 2.0 %collective-permute-start.6 = (bf16[12,64,128]{2,1,0:T(8,128)(2,1)}, bf16[12,64,128]{2,1,0:T(8,128)(2,1)S(1)}, u32[]{:S(2)}, u32[]{:S(2)}) collective-permute-start(bf16[12,64,128]{2,1,0:T(8,128)(2,1)} %pedigree.2.refs_2_), channel_id=1, source_target_pairs={{0,1},{1,2},{2,3},{3,0},{4,5},{5,6},{6,7},{7,4},{8,9},{9,10},{10,1... | collective-permute-start | bytes 589832 | tf_op jit(solution)/shard_map/ppermute | solution.py:238
  83.2 0.0 collective-permute-done.7.refs_3_
  83.2 8.2 %collective-permute-done.8.refs_4_ = bf16[12,64,128]{2,1,0:T(8,128)(2,1)S(1)} collective-permute-done((bf16[12,64,128]{2,1,0:T(8,128)(2,1)}, bf16[12,64,128]{2,1,0:T(8,128)(2,1)S(1)}, u32[]{:S(2)}, u32[]{:S(2)}) %collective-permute-start.8) | collective-permute-done | bytes 196640 | tf_op jit(solution)/shard_map/ppermute | solution.py:238
  91.4 0.0 collective-permute-done.9.refs_5_
  91.4 6.4 %collective-permute-start.10 = (bf16[12,64,128]{2,1,0:T(8,128)(2,1)}, bf16[12,64,128]{2,1,0:T(8,128)(2,1)S(1)}, u32[]{:S(2)}, u32[]{:S(2)}) collective-permute-start(bf16[12,64,128]{2,1,0:T(8,128)(2,1)} %pedigree.2.refs_2_), channel_id=1, source_target_pairs={{0,2},{1,3},{2,0},{3,1},{4,6},{5,7},{6,4},{7,5},{8,10},{9,11},{10,... | collective-permute-start | bytes 589832 | tf_op jit(solution)/shard_map/ppermute | solution.py:238
  97.8 3.3 %collective-permute-start.11 = (bf16[12,64,128]{2,1,0:T(8,128)(2,1)}, bf16[12,64,128]{2,1,0:T(8,128)(2,1)S(1)}, u32[]{:S(2)}, u32[]{:S(2)}) collective-permute-start(bf16[12,64,128]{2,1,0:T(8,128)(2,1)} %pedigree.2.refs_2_), channel_id=1, source_target_pairs={{0,3},{1,0},{2,1},{3,2},{4,7},{5,4},{6,5},{7,6},{8,11},{9,8},{10,9... | collective-permute-start | bytes 589832 | tf_op jit(solution)/shard_map/ppermute | solution.py:238
  101.1 13.6 %backward_product.2 = (f32[6400,128]{1,0:T(8,128)}, f32[6400,128]{1,0:T(8,128)}) custom-call(s32[1]{0:T(128)} %bitcast.place_ref, bf16[3072,6400]{1,0:T(8,128)(2,1)} %refs_1_.3, bf16[3072,6400]{1,0:T(8,128)(2,1)} %refs_1_.3, bf16[12,64,128]{2,1,0:T(8,128)(2,1)} %pedigree.3.refs_2_, bf16[12,64,128]{2,1,0:T(8,128)(2,1)} %copy-done.12, ...), custom_call_target="tpu_custom_call" | custom-call | flops 5033164800 | bytes 27000832 | tf_op jit(solution)/shard_map/backward_product/pallas_call | solution.py:215
  114.7 0.0 collective-permute-done.6.refs_3_
  114.7 0.0 copy-start.9
  114.7 0.0 collective-permute-done.11.refs_5_
  114.8 0.6 copy-done.9
  115.4 0.1 copy-done.10
  115.5 0.1 copy-done.11
  115.5 14.2 %backward_product.3 = (bf16[6400,128]{1,0:T(8,128)(2,1)}, bf16[6400,128]{1,0:T(8,128)(2,1)}) custom-call(s32[1]{0:T(128)} %bitcast.place_ref, bf16[3072,6400]{1,0:T(8,128)(2,1)} %refs_1_.3, bf16[3072,6400]{1,0:T(8,128)(2,1)} %refs_1_.3, bf16[12,64,128]{2,1,0:T(8,128)(2,1)} %pedigree.2.refs_2_, bf16[12,64,128]{2,1,0:T(8,128)(2,1)} %copy-done.9, ...), custom_call_target="tpu_custom_call" | custom-call | flops 5033164800 | bytes 33554432 | tf_op jit(solution)/shard_map/backward_product/pallas_call | solution.py:215
  129.7 2.3 %dynamic-slice_bitcast_fusion.1 = bf16[2,2,800,128]{3,2,1,0:T(8,128)(2,1)} fusion(bf16[2,2,2,800,128]{4,3,2,1,0:T(8,128)(2,1)} %bitcast.65, s32[]{:T(128)S(6)} %select_n.60), kind=kLoop, calls=%fused_computation.6 | loop fusion | bytes 1638404 | tf_op jit(solution)/shard_map/jit(dynamic_index_in_dim)/squeeze | solution.py:250
  132.0 0.0 collective-permute-start.12
  132.0 0.9 dynamic-slice_bitcast_fusion
  132.9 0.5 collective-permute-start.15
  133.4 1.2 collective-permute-done.12
  134.6 1.9 %fusion.1 = bf16[2,800,128]{2,1,0:T(8,128)(2,1)} fusion(bf16[2,2,800,128]{3,2,1,0:T(8,128)(2,1)} %collective-permute-done.12, s32[]{:T(128)S(6)} %select_n.61, bf16[2,2,2,800,128]{4,3,2,1,0:T(8,128)(2,1)S(1)} %bitcast.66, s32[]{:T(128)S(6)} %select_n.62, s32[]{:T(128)S(6)} %select_n.59), kind=kLoop, calls=%fused_computation.4 | loop fusion | flops 819200 | bytes 1228812 | tf_op jit(solution)/shard_map/convert_element_type | solution.py:253
  136.5 1.3 collective-permute-start.13
  137.9 0.0 collective-permute-done.15
  137.9 1.9 %fusion = bf16[2,800,128]{2,1,0:T(8,128)(2,1)} fusion(bf16[2,2,800,128]{3,2,1,0:T(8,128)(2,1)} %collective-permute-done.15, s32[]{:T(128)S(6)} %select_n.63, bf16[2,2,2,800,128]{4,3,2,1,0:T(8,128)(2,1)S(1)} %bitcast.62, s32[]{:T(128)S(6)} %select_n.64, s32[]{:T(128)S(6)} %select_n.59), kind=kLoop, calls=%fused_computation.2 | loop fusion | flops 819200 | bytes 1228812 | tf_op jit(solution)/shard_map/convert_element_type | solution.py:253
  139.7 0.4 collective-permute-start.16
  140.1 8.2 %collective-permute-done.13 = bf16[2,800,128]{2,1,0:T(8,128)(2,1)} collective-permute-done((bf16[2,800,128]{2,1,0:T(8,128)(2,1)}, bf16[2,800,128]{2,1,0:T(8,128)(2,1)}, u32[]{:S(2)}, u32[]{:S(2)}) %collective-permute-start.13) | collective-permute-done | bytes 409632 | tf_op jit(solution)/shard_map/ppermute | solution.py:254
  148.4 1.8 %fusion.4 = bf16[800,128]{1,0:T(8,128)(2,1)} fusion(bf16[2,800,128]{2,1,0:T(8,128)(2,1)} %collective-permute-done.13, s32[]{:T(128)S(6)} %select_n.63, bf16[2,2,800,128]{3,2,1,0:T(8,128)(2,1)} %collective-permute-done.12, s32[]{:T(128)S(6)} %select_n.64, s32[]{:T(128)S(6)} %select_n.57, bf16[2,2,2,800,128]{4,3,2,1,0:T(8,128)(2,1)S(1)} %bitcast.67, ...), kind=kLoop, calls=%fused_computation.14 | loop fusion | flops 614400 | bytes 819216 | tf_op jit(solution)/shard_map/convert_element_type | solution.py:253
  150.1 0.6 collective-permute-start.14
  150.7 0.8 dynamic_slice.88
  151.5 0.0 collective-permute-done.16
  151.5 1.1 fusion.2
  152.6 1.3 collective-permute-start.17
  153.9 2.8 %collective-permute-done.14 = bf16[800,128]{1,0:T(8,128)(2,1)S(1)} collective-permute-done((bf16[800,128]{1,0:T(8,128)(2,1)}, bf16[800,128]{1,0:T(8,128)(2,1)S(1)}, u32[]{:S(2)}, u32[]{:S(2)}) %collective-permute-start.14) | collective-permute-done | bytes 204832 | tf_op jit(solution)/shard_map/ppermute | solution.py:254
  156.7 1.1 fusion.5
  157.8 0.9 collective-permute-done.17
  158.7 1.1 fusion.3
  159.8 2.1 %maximum_add_fusion = f32[800,256]{1,0:T(8,128)} fusion(f32[800,128]{1,0:T(8,128)S(1)} %fusion.3, f32[800,128]{1,0:T(8,128)S(1)} %fusion.5, bf16[6400,256]{1,0:T(8,128)(2,1)} %direction_ref.3, s32[]{:T(128)S(6)} %select_n.65, f32[800]{0:T(1024)S(1)} %dynamic_slice.88), kind=kLoop, calls=%fused_computation | loop fusion | flops 819200 | bytes 2051204 | tf_op jit(solution)/shard_map/add | solution.py:313
  (28 shorter events, 0.1 us)
Async XLA Ops:
  11.8 18.8 %collective-permute-start = (s16[816,128]{1,0:T(8,128)(2,1)}, s16[816,128]{1,0:T(8,128)(2,1)S(1)}, u32[]{:S(2)}, u32[]{:S(2)}) collective-permute-start(s16[816,128]{1,0:T(8,128)(2,1)} %get-tuple-element.35), channel_id=1, source_target_pairs={{0,1},{1,2},{2,3},{3,0},{4,5},{5,6},{6,7},{7,4},{8,9},{9,10},{10,1... | collective-permute-start | bytes 626696 | tf_op jit(solution)/shard_map/ppermute | solution.py:238
  14.8 16.5 %collective-permute-start.1 = (s16[816,128]{1,0:T(8,128)(2,1)}, s16[816,128]{1,0:T(8,128)(2,1)S(1)}, u32[]{:S(2)}, u32[]{:S(2)}) collective-permute-start(s16[816,128]{1,0:T(8,128)(2,1)} %get-tuple-element.36), channel_id=1, source_target_pairs={{0,2},{1,3},{2,0},{3,1},{4,6},{5,7},{6,4},{7,5},{8,10},{9,11},{10,... | collective-permute-start | bytes 626696 | tf_op jit(solution)/shard_map/ppermute | solution.py:238
  17.4 21.2 %copy-start.16 = (s32[1,8,2]{1,2,0:T(2,128)S(1)}, s32[1,8,2]{1,2,0:T(2,128)}, u32[]{:S(2)}) copy-start(s32[1,8,2]{1,2,0:T(2,128)} %param.10) | copy-start | bytes 196
  17.4 13.9 %collective-permute-start.2 = (s16[816,128]{1,0:T(8,128)(2,1)}, s16[816,128]{1,0:T(8,128)(2,1)S(1)}, u32[]{:S(2)}, u32[]{:S(2)}) collective-permute-start(s16[816,128]{1,0:T(8,128)(2,1)} %get-tuple-element.37), channel_id=1, source_target_pairs={{0,3},{1,0},{2,1},{3,2},{4,7},{5,4},{6,5},{7,6},{8,11},{9,8},{10,9... | collective-permute-start | bytes 626696 | tf_op jit(solution)/shard_map/ppermute | solution.py:238
  30.5 28.2 %copy-start.15 = (s32[24,4]{0,1:T(4,128)S(1)}, s32[24,4]{0,1:T(4,128)}, u32[]{:S(2)}) copy-start(s32[24,4]{0,1:T(4,128)} %param.11) | copy-start | bytes 1156
  30.5 20.4 %copy-start.3 = (s16[816,128]{1,0:T(8,128)(2,1)}, s16[816,128]{1,0:T(8,128)(2,1)S(1)}, u32[]{:S(2)}) copy-start(s16[816,128]{1,0:T(8,128)(2,1)S(1)} %collective-permute-done.refs_2_) | copy-start | bytes 626692
  31.3 19.6 %copy-start.4 = (s16[816,128]{1,0:T(8,128)(2,1)}, s16[816,128]{1,0:T(8,128)(2,1)S(1)}, u32[]{:S(2)}) copy-start(s16[816,128]{1,0:T(8,128)(2,1)S(1)} %collective-permute-done.1.refs_4_) | copy-start | bytes 626692
  31.3 19.6 %copy-start.5 = (s16[816,128]{1,0:T(8,128)(2,1)}, s16[816,128]{1,0:T(8,128)(2,1)S(1)}, u32[]{:S(2)}) copy-start(s16[816,128]{1,0:T(8,128)(2,1)S(1)} %collective-permute-done.2.refs_6_) | copy-start | bytes 626692
  31.3 12.4 %collective-permute-start.3 = (s16[816,128]{1,0:T(8,128)(2,1)}, s16[816,128]{1,0:T(8,128)(2,1)S(1)}, u32[]{:S(2)}, u32[]{:S(2)}) collective-permute-start(s16[816,128]{1,0:T(8,128)(2,1)} %get-tuple-element.39), channel_id=1, source_target_pairs={{0,1},{1,2},{2,3},{3,0},{4,5},{5,6},{6,7},{7,4},{8,9},{9,10},{10,1... | collective-permute-start | bytes 626696 | tf_op jit(solution)/shard_map/ppermute | solution.py:238
  36.3 14.6 %collective-permute-start.4 = (s16[816,128]{1,0:T(8,128)(2,1)}, s16[816,128]{1,0:T(8,128)(2,1)S(1)}, u32[]{:S(2)}, u32[]{:S(2)}) collective-permute-start(s16[816,128]{1,0:T(8,128)(2,1)} %get-tuple-element.41), channel_id=1, source_target_pairs={{0,2},{1,3},{2,0},{3,1},{4,6},{5,7},{6,4},{7,5},{8,10},{9,11},{10,... | collective-permute-start | bytes 626696 | tf_op jit(solution)/shard_map/ppermute | solution.py:238
  37.9 13.0 %collective-permute-start.5 = (s16[816,128]{1,0:T(8,128)(2,1)}, s16[816,128]{1,0:T(8,128)(2,1)S(1)}, u32[]{:S(2)}, u32[]{:S(2)}) collective-permute-start(s16[816,128]{1,0:T(8,128)(2,1)} %get-tuple-element.43), channel_id=1, source_target_pairs={{0,3},{1,0},{2,1},{3,2},{4,7},{5,4},{6,5},{7,6},{8,11},{9,8},{10,9... | collective-permute-start | bytes 626696 | tf_op jit(solution)/shard_map/ppermute | solution.py:238
  43.7 7.2 %copy-start.6 = (s16[816,128]{1,0:T(8,128)(2,1)}, s16[816,128]{1,0:T(8,128)(2,1)S(1)}, u32[]{:S(2)}) copy-start(s16[816,128]{1,0:T(8,128)(2,1)S(1)} %collective-permute-done.3.refs_3_) | copy-start | bytes 626692
  50.9 0.7 copy-start.7
  50.9 0.7 copy-start.8
  55.0 10.7 %all-to-all-start = ((bf16[8,2,64,128]{3,2,1,0:T(8,128)(2,1)}), bf16[8,2,64,128]{3,2,1,0:T(8,128)(2,1)S(1)}, u32[]{:S(2)}, u32[]{:S(2)}) async-start(bf16[8,2,64,128]{3,2,1,0:T(8,128)(2,1)} %bitcast.69), calls=%async_computation | async-start | bytes 524288 | tf_op jit(solution)/shard_map/all_to_all | solution.py:285
  65.7 0.7 copy-start
  70.1 13.1 %collective-permute-start.7 = (bf16[12,64,128]{2,1,0:T(8,128)(2,1)}, bf16[12,64,128]{2,1,0:T(8,128)(2,1)S(1)}, u32[]{:S(2)}, u32[]{:S(2)}) collective-permute-start(bf16[12,64,128]{2,1,0:T(8,128)(2,1)} %pedigree.3.refs_2_), channel_id=1, source_target_pairs={{0,1},{1,2},{2,3},{3,0},{4,5},{5,6},{6,7},{7,4},{8,9},{9,10},{10,1... | collective-permute-start | bytes 589832 | tf_op jit(solution)/shard_map/ppermute | solution.py:238
  75.0 16.4 %collective-permute-start.8 = (bf16[12,64,128]{2,1,0:T(8,128)(2,1)}, bf16[12,64,128]{2,1,0:T(8,128)(2,1)S(1)}, u32[]{:S(2)}, u32[]{:S(2)}) collective-permute-start(bf16[12,64,128]{2,1,0:T(8,128)(2,1)} %pedigree.3.refs_2_), channel_id=1, source_target_pairs={{0,2},{1,3},{2,0},{3,1},{4,6},{5,7},{6,4},{7,5},{8,10},{9,11},{10,... | collective-permute-start | bytes 589832 | tf_op jit(solution)/shard_map/ppermute | solution.py:238
  77.4 14.0 %collective-permute-start.9 = (bf16[12,64,128]{2,1,0:T(8,128)(2,1)}, bf16[12,64,128]{2,1,0:T(8,128)(2,1)S(1)}, u32[]{:S(2)}, u32[]{:S(2)}) collective-permute-start(bf16[12,64,128]{2,1,0:T(8,128)(2,1)} %pedigree.3.refs_2_), channel_id=1, source_target_pairs={{0,3},{1,0},{2,1},{3,2},{4,7},{5,4},{6,5},{7,6},{8,11},{9,8},{10,9... | collective-permute-start | bytes 589832 | tf_op jit(solution)/shard_map/ppermute | solution.py:238
  81.2 33.5 %collective-permute-start.6 = (bf16[12,64,128]{2,1,0:T(8,128)(2,1)}, bf16[12,64,128]{2,1,0:T(8,128)(2,1)S(1)}, u32[]{:S(2)}, u32[]{:S(2)}) collective-permute-start(bf16[12,64,128]{2,1,0:T(8,128)(2,1)} %pedigree.2.refs_2_), channel_id=1, source_target_pairs={{0,1},{1,2},{2,3},{3,0},{4,5},{5,6},{6,7},{7,4},{8,9},{9,10},{10,1... | collective-permute-start | bytes 589832 | tf_op jit(solution)/shard_map/ppermute | solution.py:238
  83.2 17.9 %copy-start.12 = (bf16[12,64,128]{2,1,0:T(8,128)(2,1)}, bf16[12,64,128]{2,1,0:T(8,128)(2,1)S(1)}, u32[]{:S(2)}) copy-start(bf16[12,64,128]{2,1,0:T(8,128)(2,1)S(1)} %collective-permute-done.7.refs_3_) | copy-start | bytes 589828
  91.4 9.7 %copy-start.13 = (bf16[12,64,128]{2,1,0:T(8,128)(2,1)}, bf16[12,64,128]{2,1,0:T(8,128)(2,1)S(1)}, u32[]{:S(2)}) copy-start(bf16[12,64,128]{2,1,0:T(8,128)(2,1)S(1)} %collective-permute-done.8.refs_4_) | copy-start | bytes 589828
  91.4 9.7 %copy-start.14 = (bf16[12,64,128]{2,1,0:T(8,128)(2,1)}, bf16[12,64,128]{2,1,0:T(8,128)(2,1)S(1)}, u32[]{:S(2)}) copy-start(bf16[12,64,128]{2,1,0:T(8,128)(2,1)S(1)} %collective-permute-done.9.refs_5_) | copy-start | bytes 589828
  91.4 23.3 %collective-permute-start.10 = (bf16[12,64,128]{2,1,0:T(8,128)(2,1)}, bf16[12,64,128]{2,1,0:T(8,128)(2,1)S(1)}, u32[]{:S(2)}, u32[]{:S(2)}) collective-permute-start(bf16[12,64,128]{2,1,0:T(8,128)(2,1)} %pedigree.2.refs_2_), channel_id=1, source_target_pairs={{0,2},{1,3},{2,0},{3,1},{4,6},{5,7},{6,4},{7,5},{8,10},{9,11},{10,... | collective-permute-start | bytes 589832 | tf_op jit(solution)/shard_map/ppermute | solution.py:238
  97.8 16.9 %collective-permute-start.11 = (bf16[12,64,128]{2,1,0:T(8,128)(2,1)}, bf16[12,64,128]{2,1,0:T(8,128)(2,1)S(1)}, u32[]{:S(2)}, u32[]{:S(2)}) collective-permute-start(bf16[12,64,128]{2,1,0:T(8,128)(2,1)} %pedigree.2.refs_2_), channel_id=1, source_target_pairs={{0,3},{1,0},{2,1},{3,2},{4,7},{5,4},{6,5},{7,6},{8,11},{9,8},{10,9... | collective-permute-start | bytes 589832 | tf_op jit(solution)/shard_map/ppermute | solution.py:238
  114.7 0.7 copy-start.9
  114.7 0.7 copy-start.10
  114.7 0.8 copy-start.11
  129.7 2.3 %copy-start.1 = (bf16[6400,128]{1,0:T(8,128)(2,1)S(1)}, bf16[6400,128]{1,0:T(8,128)(2,1)}, u32[]{:S(2)}) copy-start(bf16[6400,128]{1,0:T(8,128)(2,1)} %get-tuple-element.54) | copy-start | bytes 4915204
  129.7 5.0 %copy-start.2 = (bf16[6400,128]{1,0:T(8,128)(2,1)S(1)}, bf16[6400,128]{1,0:T(8,128)(2,1)}, u32[]{:S(2)}) copy-start(bf16[6400,128]{1,0:T(8,128)(2,1)} %get-tuple-element.53) | copy-start | bytes 4915204
  132.0 2.7 %collective-permute-start.12 = (bf16[2,2,800,128]{3,2,1,0:T(8,128)(2,1)}, bf16[2,2,800,128]{3,2,1,0:T(8,128)(2,1)}, u32[]{:S(2)}, u32[]{:S(2)}) collective-permute-start(bf16[2,2,800,128]{3,2,1,0:T(8,128)(2,1)} %dynamic-slice_bitcast_fusion.1), channel_id=1, source_target_pairs={{0,4},{4,0},{8,12},{12,8},{16,20},{20,16},{24,28},{28,24},{1,5},{5... | collective-permute-start | bytes 2457608 | tf_op jit(solution)/shard_map/ppermute | solution.py:254
  132.9 4.9 %collective-permute-start.15 = (bf16[2,2,800,128]{3,2,1,0:T(8,128)(2,1)}, bf16[2,2,800,128]{3,2,1,0:T(8,128)(2,1)}, u32[]{:S(2)}, u32[]{:S(2)}) collective-permute-start(bf16[2,2,800,128]{3,2,1,0:T(8,128)(2,1)} %dynamic-slice_bitcast_fusion), channel_id=1, source_target_pairs={{0,4},{4,0},{8,12},{12,8},{16,20},{20,16},{24,28},{28,24},{1,5},{5... | collective-permute-start | bytes 2457608 | tf_op jit(solution)/shard_map/ppermute | solution.py:254
  136.5 11.8 %collective-permute-start.13 = (bf16[2,800,128]{2,1,0:T(8,128)(2,1)}, bf16[2,800,128]{2,1,0:T(8,128)(2,1)}, u32[]{:S(2)}, u32[]{:S(2)}) collective-permute-start(bf16[2,800,128]{2,1,0:T(8,128)(2,1)} %fusion.1), channel_id=1, source_target_pairs={{0,8},{4,12},{8,0},{12,4},{16,24},{20,28},{24,16},{28,20},{1,9},{5... | collective-permute-start | bytes 1228808 | tf_op jit(solution)/shard_map/ppermute | solution.py:254
  139.7 11.8 %collective-permute-start.16 = (bf16[2,800,128]{2,1,0:T(8,128)(2,1)}, bf16[2,800,128]{2,1,0:T(8,128)(2,1)}, u32[]{:S(2)}, u32[]{:S(2)}) collective-permute-start(bf16[2,800,128]{2,1,0:T(8,128)(2,1)} %fusion), channel_id=1, source_target_pairs={{0,16},{4,20},{8,24},{12,28},{16,0},{20,4},{24,8},{28,12},{1,17},{... | collective-permute-start | bytes 1228808 | tf_op jit(solution)/shard_map/ppermute | solution.py:254
  150.1 6.5 %collective-permute-start.14 = (bf16[800,128]{1,0:T(8,128)(2,1)}, bf16[800,128]{1,0:T(8,128)(2,1)S(1)}, u32[]{:S(2)}, u32[]{:S(2)}) collective-permute-start(bf16[800,128]{1,0:T(8,128)(2,1)} %fusion.4), channel_id=1, source_target_pairs={{0,16},{4,20},{8,24},{12,28},{16,0},{20,4},{24,8},{28,12},{1,17},{... | collective-permute-start | bytes 614408 | tf_op jit(solution)/shard_map/ppermute | solution.py:254
  152.6 6.1 %collective-permute-start.17 = (bf16[800,128]{1,0:T(8,128)(2,1)S(1)}, bf16[800,128]{1,0:T(8,128)(2,1)S(1)}, u32[]{:S(2)}, u32[]{:S(2)}) collective-permute-start(bf16[800,128]{1,0:T(8,128)(2,1)S(1)} %fusion.2), channel_id=1, source_target_pairs={{0,8},{4,12},{8,0},{12,4},{16,24},{20,28},{24,16},{28,20},{1,9},{5... | collective-permute-start | bytes 614408 | tf_op jit(solution)/shard_map/ppermute | solution.py:254

commit v6 on v3

--- a/solution.py
+++ b/solution.py
@@ -11,7 +11,7 @@
 MARKERS = 25600
 BLK = 128
 MARK = 16
-VMEM_LIMIT = 56 * 1024 * 1024
+VMEM_LIMIT = 63 * 1024 * 1024
 
 
 def divisor(total, unit, most):
@@ -142,10 +142,10 @@
             source = table[index_ref[block, j]]
             source = jnp.where(j < count_ref[block], source, jnp.zeros_like(source))
             term = lax.dot_general(
-                source, prec_ref[b, j], (((1,), (1,)), ((), ())), preferred_element_type=jnp.float32
+                prec_ref[b, j], source, (((1,), (1,)), ((), ())), preferred_element_type=jnp.float32
             )
             total = term if total is None else total + term
-        out_ref[b] = total.astype(out_ref.dtype)
+        out_ref[b] = total.T.astype(out_ref.dtype)
 
 
 def pedigree(blocked, incoming, rel_index, rel_count, rel_prec, start, count):
@@ -238,22 +238,107 @@
     return lax.ppermute(value, "marker", [(d, (d + shift) % devices) for d in range(devices)])
 
 
-def halving_sum(blocks, devices, bits):
+def combine_kernel(counts, index_ref, *refs):
+    terms, outs = refs[: sum(counts)], refs[sum(counts) :]
+    for count, out_ref in zip(counts, outs):
+        total = sum(term[0].astype(jnp.float32) for term in terms[:count])
+        out_ref[0] = total.astype(out_ref.dtype)
+        terms = terms[count:]
+
+
+def finish_kernel(counts, index_ref, ridge_ref, direction_ref, *refs):
+    terms, out_ref = refs[:-1], refs[-1]
+    half = out_ref.shape[1] // len(counts)
+    for flow, count in enumerate(counts):
+        columns = slice(flow * half, (flow + 1) * half)
+        total = sum(term[0].astype(jnp.float32) for term in terms[:count])
+        out_ref[:, columns] = total + ridge_ref[...] * direction_ref[0, :, columns].astype(jnp.float32)
+        terms = terms[count:]
+
+
+def combine(flows, places, blocks):
+    terms = [term for flow in flows for term in flow]
+    shape = terms[0].shape[1:]
+
+    def at(k):
+        return pl.BlockSpec((1,) + shape, lambda i, index: (index[k * blocks + i], 0, 0))
+
+    return pl.pallas_call(
+        functools.partial(combine_kernel, [len(flow) for flow in flows]),
+        grid_spec=pltpu.PrefetchScalarGridSpec(
+            num_scalar_prefetch=1,
+            grid=(blocks,),
+            in_specs=[at(k) for k in range(len(terms))],
+            out_specs=[pl.BlockSpec((1,) + shape, lambda i, index: (i, 0, 0))] * len(flows),
+        ),
+        out_shape=[jax.ShapeDtypeStruct((blocks,) + shape, terms[0].dtype)] * len(flows),
+        compiler_params=pltpu.CompilerParams(vmem_limit_bytes=VMEM_LIMIT),
+        name="combine",
+    )(places, *terms)
+
+
+def finish(flows, places, own_ridge, direction, here):
+    terms = [term for flow in flows for term in flow]
+    shape = terms[0].shape[1:]
+    cols = direction.shape[-1]
+    last = len(terms)
+
+    def at(k):
+        return pl.BlockSpec((1,) + shape, lambda i, index: (index[k], 0, 0))
+
+    return pl.pallas_call(
+        functools.partial(finish_kernel, [len(flow) for flow in flows]),
+        grid_spec=pltpu.PrefetchScalarGridSpec(
+            num_scalar_prefetch=1,
+            grid=(1,),
+            in_specs=[
+                pl.BlockSpec(own_ridge.shape, lambda i, index: (0, 0)),
+                pl.BlockSpec((1, shape[0], cols), lambda i, index: (index[last], 0, 0)),
+            ]
+            + [at(k) for k in range(last)],
+            out_specs=pl.BlockSpec((shape[0], cols), lambda i, index: (0, 0)),
+        ),
+        out_shape=jax.ShapeDtypeStruct((shape[0], cols), jnp.float32),
+        compiler_params=pltpu.CompilerParams(vmem_limit_bytes=VMEM_LIMIT),
+        name="finish",
+    )(jnp.concatenate([places, here.reshape(1)]), own_ridge, direction, *terms)
+
+
+def halving_sum(halves, devices, orders, own_ridge, direction):
     levels = devices.bit_length() - 1
     here = lax.axis_index("animal")
-    terms = [blocks.reshape((2,) * levels + blocks.shape[1:])]
-    left = list(range(levels - 1, -1, -1))
-    for bit in bits:
-        axis = left.index(bit)
-        mine = (here >> bit) & 1
-        sent, kept = [
-            [lax.dynamic_index_in_dim(term, side, axis, keepdims=False) for term in terms]
-            for side in (1 - mine, mine)
-        ]
-        sent = sum(term.astype(jnp.float32) for term in sent).astype(jnp.bfloat16)
-        terms = kept + [lax.ppermute(sent, "animal", [(d, d ^ (1 << bit)) for d in range(devices)])]
-        left.pop(axis)
-    return sum(term.astype(jnp.float32) for term in terms)
+    every = list(range(levels - 1, -1, -1))
+    terms = [[(half, every)] for half in halves]
+
+    def place(bits, left, block, bit, side):
+        index = jnp.int32(0)
+        for b in bits:
+            if b in left:
+                value = (block >> (len(left) - 1 - left.index(b))) & 1
+            else:
+                value = (here >> b) & 1
+                if b == bit:
+                    value = value ^ side
+            index = index * 2 + value
+        return index
+
+    for step in range(levels):
+        lefts = [[b for b in every if b not in order[: step + 1]] for order in orders]
+        blocks = 1 << (levels - 1 - step)
+        places = jnp.stack(
+            [
+                place(bits, left, block, order[step], 1)
+                for flow, left, order in zip(terms, lefts, orders)
+                for _, bits in flow
+                for block in range(blocks)
+            ]
+        )
+        sent = combine([[array for array, _ in flow] for flow in terms], places, blocks)
+        for flow, left, order, value in zip(terms, lefts, orders, sent):
+            pairs = [(d, d ^ (1 << order[step])) for d in range(devices)]
+            flow.append((lax.ppermute(value, "animal", pairs), left))
+    places = jnp.stack([place(bits, [], 0, None, 0) for flow in terms for _, bits in flow])
+    return finish([[array for array, _ in flow] for flow in terms], places, own_ridge, direction, here)
 
 
 def local(genotypes, direction, ridge, send_list, rel_index, rel_count, rel_prec):
@@ -297,17 +382,11 @@
         sums = backward_product(genotypes, shares[part], place, 1.0 / math.sqrt(groups * rows), part, kind, sums)
     low, high = [total.reshape(groups, own_rows, half) for total in sums]
     levels = list(range(groups.bit_length() - 1))
-    gradient = jnp.concatenate(
-        [
-            halving_sum(low, groups, levels),
-            halving_sum(high, groups, levels[:1] + levels[:0:-1]),
-        ],
-        axis=1,
-    )
+    orders = [levels, levels[:1] + levels[:0:-1]]
     start = lax.axis_index("animal") * own_rows
-    own_ridge = lax.dynamic_slice_in_dim(ridge, start, own_rows, 0)
-    own_direction = lax.dynamic_slice_in_dim(direction, start, own_rows, 0)
-    return gradient + own_ridge[:, None] * own_direction.astype(jnp.float32)
+    own_ridge = lax.dynamic_slice_in_dim(ridge, start, own_rows, 0).reshape(own_rows, 1)
+    by_owner = direction.reshape(groups, own_rows, -1)
+    return halving_sum([low, high], groups, orders, own_ridge, by_owner)
 
 
 def solution(mesh):

time: 161 us -> 166 us (1.031)
  Pallas kernels: 62.9 us -> 76 us
  other arithmetic: 11 us -> 0 us
    pallas_call x0 -> x4, Pallas kernels: none -> 13.8 us  [the longest x3 10.3 us: combine(): pl.pallas_call(functools.partial(combine_kernel, [len(flow) for flow in f...]
    convert_element_type x4 -> x0, other arithmetic: 6.64 us -> none  [halving_sum(): sent = sum((term.astype(jnp.float32) for term in sent)).astype(jnp.bfloat16)]
    add x3 -> x0, other arithmetic: 4.34 us -> none  [the longest x2 2.26 us: halving_sum(): return sum((term.astype(jnp.float32) for term in terms))]
    squeeze x2 -> x0, local copies, waits for them, and re-layouts: 3.21 us -> none  [halving_sum(): lax.dynamic_index_in_dim(term, side, axis, keepdims=False)]
    ppermute x6, waiting for transfers between devices: 13.6 us -> 15.8 us  [halving_sum(): flow.append((lax.ppermute(value, 'animal', pairs), left))]
    another operation x0 -> x3, local copies, waits for them, and re-layouts: none -> 1.85 us  [halving_sum(): jnp.stack([place(bits, left, block, order[step], 1) for flow, left, order...]
  transfers between devices with their start and end apart: 19 -> 19, of which waited for: 12 -> 14; matrix products, arithmetic and copies ran while one was open for 7% -> 3% of each run, Pallas kernels for 18% -> 18%
where the time goes in v6:
time: 166 us
  Pallas kernels  76 us (46%)
  waiting for transfers between devices  56.8 us (34%)
  starting transfers between devices  22.9 us (14%)
  local copies, waits for them, and re-layouts  9.7 us (6%)
    ppermute x12, waiting for transfers between devices, turn(): lax.ppermute(value, 'marker', [(d, (d + shift) % devices) for d in range(...  34.8 us
    pallas_call x2, Pallas kernels, backward_product(): pl.pallas_call(functools.partial(backward_kernel, scale, devices, lanes),...  27.8 us
    pallas_call x2, Pallas kernels, forward_product(): pl.pallas_call(functools.partial(forward_kernel, scale, devices), grid_sp...  23.6 us
    ppermute x6, waiting for transfers between devices, halving_sum(): flow.append((lax.ppermute(value, 'animal', pairs), left))  15.8 us
    ppermute x12, starting transfers between devices, turn(): lax.ppermute(value, 'marker', [(d, (d + shift) % devices) for d in range(...  15.4 us
    pallas_call x3, Pallas kernels, combine(): pl.pallas_call(functools.partial(combine_kernel, [len(flow) for flow in f...  10.3 us
    pallas_call x2, Pallas kernels, pedigree(): pl.pallas_call(functools.partial(pedigree_kernel, group, block_total, sta...  7.54 us
    all_to_all x1, waiting for transfers between devices, local(): lax.all_to_all(outgoing, 'animal', split_axis=0, concat_axis=0, tiled=True)  6.25 us
  transfers between devices with their start and end apart: 19, of which 14 were waited for; matrix products, arithmetic and copies ran while one was open for 3% of the time, Pallas kernels for 18%

profile of v6, /device:TPU:8, one launch (start us, length us, event | category | flops | bytes accessed | tf_op | source)
XLA Modules:
  0.0 165.5 jit_solution(10842410522198953218)
XLA Ops:
  0.0 11.8 %forward_product.2 = (f32[12,64,128]{2,1,0:T(8,128)}, s16[816,128]{1,0:T(8,128)(2,1)}, s16[816,128]{1,0:T(8,128)(2,1)}, s16[816,128]{1,0:T(8,128)(2,1)}) custom-call(s32[1]{0:T(128)} %bitcast.6.place_ref, bf16[3072,6400]{1,0:T(8,128)(2,1)} %refs_1_.3, bf16[3072,6400]{1,0:T(8,128)(2,1)} %refs_1_.3, bf16[6400,256]{1,0:T(8,128)(2,1)} %direction_ref.3), custom_call_target="tpu_custom_call" | custom-call | flops 5033164800 | bytes 23724032 | tf_op jit(solution)/shard_map/forward_product/pallas_call | solution.py:60
  11.8 1.6 collective-permute-start
  13.4 1.1 collective-permute-start.1
  14.5 1.9 %collective-permute-start.2 = (s16[816,128]{1,0:T(8,128)(2,1)}, s16[816,128]{1,0:T(8,128)(2,1)S(1)}, u32[]{:S(2)}, u32[]{:S(2)}) collective-permute-start(s16[816,128]{1,0:T(8,128)(2,1)} %get-tuple-element.38), channel_id=1, source_target_pairs={{0,3},{1,0},{2,1},{3,2},{4,7},{5,4},{6,5},{7,6},{8,11},{9,8},{10,9... | collective-permute-start | bytes 626696 | tf_op jit(solution)/shard_map/ppermute | solution.py:238
  16.4 11.8 %forward_product.3 = (f32[12,64,128]{2,1,0:T(8,128)}, s16[816,128]{1,0:T(8,128)(2,1)}, s16[816,128]{1,0:T(8,128)(2,1)}, s16[816,128]{1,0:T(8,128)(2,1)}) custom-call(s32[1]{0:T(128)} %bitcast.6.place_ref, bf16[3072,6400]{1,0:T(8,128)(2,1)} %refs_1_.3, bf16[3072,6400]{1,0:T(8,128)(2,1)} %refs_1_.3, bf16[6400,256]{1,0:T(8,128)(2,1)} %direction_ref.3), custom_call_target="tpu_custom_call" | custom-call | flops 5033164800 | bytes 23724032 | tf_op jit(solution)/shard_map/forward_product/pallas_call | solution.py:60
  28.2 0.0 collective-permute-done.refs_2_
  28.2 3.3 %collective-permute-done.1.refs_4_ = s16[816,128]{1,0:T(8,128)(2,1)S(1)} collective-permute-done((s16[816,128]{1,0:T(8,128)(2,1)}, s16[816,128]{1,0:T(8,128)(2,1)S(1)}, u32[]{:S(2)}, u32[]{:S(2)}) %collective-permute-start.1) | collective-permute-done | bytes 208928 | tf_op jit(solution)/shard_map/ppermute | solution.py:238
  31.5 1.7 %collective-permute-done.2.refs_6_ = s16[816,128]{1,0:T(8,128)(2,1)S(1)} collective-permute-done((s16[816,128]{1,0:T(8,128)(2,1)}, s16[816,128]{1,0:T(8,128)(2,1)S(1)}, u32[]{:S(2)}, u32[]{:S(2)}) %collective-permute-start.2) | collective-permute-done | bytes 208928 | tf_op jit(solution)/shard_map/ppermute | solution.py:238
  33.2 0.0 collective-permute-start.3
  33.2 1.7 %collective-permute-start.4 = (s16[816,128]{1,0:T(8,128)(2,1)}, s16[816,128]{1,0:T(8,128)(2,1)}, u32[]{:S(2)}, u32[]{:S(2)}) collective-permute-start(s16[816,128]{1,0:T(8,128)(2,1)} %get-tuple-element.42), channel_id=1, source_target_pairs={{0,2},{1,3},{2,0},{3,1},{4,6},{5,7},{6,4},{7,5},{8,10},{9,11},{10,... | collective-permute-start | bytes 626696 | tf_op jit(solution)/shard_map/ppermute | solution.py:238
  34.9 1.9 %collective-permute-start.5 = (s16[816,128]{1,0:T(8,128)(2,1)}, s16[816,128]{1,0:T(8,128)(2,1)}, u32[]{:S(2)}, u32[]{:S(2)}) collective-permute-start(s16[816,128]{1,0:T(8,128)(2,1)} %get-tuple-element.44), channel_id=1, source_target_pairs={{0,3},{1,0},{2,1},{3,2},{4,7},{5,4},{6,5},{7,6},{8,11},{9,8},{10,9... | collective-permute-start | bytes 626696 | tf_op jit(solution)/shard_map/ppermute | solution.py:238
  36.9 0.1 copy.11
  37.0 0.7 reshape.31.list_ref
  37.6 3.8 %collective-permute-done.3.refs_3_ = s16[816,128]{1,0:T(8,128)(2,1)S(1)} collective-permute-done((s16[816,128]{1,0:T(8,128)(2,1)}, s16[816,128]{1,0:T(8,128)(2,1)S(1)}, u32[]{:S(2)}, u32[]{:S(2)}) %collective-permute-start.3) | collective-permute-done | bytes 208928 | tf_op jit(solution)/shard_map/ppermute | solution.py:238
  41.5 10.4 %collective-permute-done.4.refs_5_ = s16[816,128]{1,0:T(8,128)(2,1)} collective-permute-done((s16[816,128]{1,0:T(8,128)(2,1)}, s16[816,128]{1,0:T(8,128)(2,1)}, u32[]{:S(2)}, u32[]{:S(2)}) %collective-permute-start.4) | collective-permute-done | bytes 208928 | tf_op jit(solution)/shard_map/ppermute | solution.py:238
  51.9 1.0 collective-permute-done.5.refs_7_
  52.9 3.4 %settle.1 = (bf16[24,64,128]{2,1,0:T(8,128)(2,1)}, bf16[16,64,128]{2,1,0:T(8,128)(2,1)}) custom-call(s32[16]{0:T(128)} %reshape.31.list_ref, f32[12,64,128]{2,1,0:T(8,128)} %get-tuple-element.31.refs_0_, f32[12,64,128]{2,1,0:T(8,128)} %get-tuple-element.32.refs_1_, s16[816,128]{1,0:T(8,128)(2,1)} %copy-done.4, s16[816,128]{1,0:T(8,128)(2,1)} %copy-done.7, ...), custom_call_target="tpu_custom_call" | custom-call | tf_op jit(solution)/shard_map/settle/pallas_call | solution.py:110
  56.3 3.7 %all-to-all-start = ((bf16[8,2,64,128]{3,2,1,0:T(8,128)(2,1)}), bf16[8,2,64,128]{3,2,1,0:T(8,128)(2,1)S(1)}, u32[]{:S(2)}, u32[]{:S(2)}) async-start(bf16[8,2,64,128]{3,2,1,0:T(8,128)(2,1)} %bitcast.39), calls=%async_computation | async-start | bytes 524288 | tf_op jit(solution)/shard_map/all_to_all | solution.py:370
  60.0 0.7 copy.12.index_ref
  60.7 6.2 %all-to-all-done = bf16[8,2,64,128]{3,2,1,0:T(8,128)(2,1)S(1)} async-done(((bf16[8,2,64,128]{3,2,1,0:T(8,128)(2,1)}), bf16[8,2,64,128]{3,2,1,0:T(8,128)(2,1)S(1)}, u32[]{:S(2)}, u32[]{:S(2)}) %all-to-all-start) | async-done | bytes 262176 | tf_op jit(solution)/shard_map/all_to_all | solution.py:370
  67.0 0.7 copy-done.1
  67.7 3.8 %pedigree.3.refs_2_ = bf16[12,64,128]{2,1,0:T(8,128)(2,1)} custom-call(s32[24,4]{1,0:T(8,128)} %copy.12.index_ref, s32[24]{0:T(128)} %count_ref.3, bf16[24,64,128]{2,1,0:T(8,128)(2,1)} %get-tuple-element.45.own_ref, bf16[16,64,128]{2,1,0:T(8,128)(2,1)} %bitcast.37, bf16[24,4,128,128]{3,2,1,0:T(8,128)(2,1)} %prec_ref.3), custom_call_target="tpu_custom_call" | custom-call | tf_op jit(solution)/shard_map/pedigree/pallas_call | solution.py:157
  71.4 2.3 %collective-permute-start.10 = (bf16[12,64,128]{2,1,0:T(8,128)(2,1)}, bf16[12,64,128]{2,1,0:T(8,128)(2,1)S(1)}, u32[]{:S(2)}, u32[]{:S(2)}) collective-permute-start(bf16[12,64,128]{2,1,0:T(8,128)(2,1)} %pedigree.3.refs_2_), channel_id=1, source_target_pairs={{0,2},{1,3},{2,0},{3,1},{4,6},{5,7},{6,4},{7,5},{8,10},{9,11},{10,... | collective-permute-start | bytes 589832 | tf_op jit(solution)/shard_map/ppermute | solution.py:238
  73.8 2.0 %collective-permute-start.9 = (bf16[12,64,128]{2,1,0:T(8,128)(2,1)}, bf16[12,64,128]{2,1,0:T(8,128)(2,1)}, u32[]{:S(2)}, u32[]{:S(2)}) collective-permute-start(bf16[12,64,128]{2,1,0:T(8,128)(2,1)} %pedigree.3.refs_2_), channel_id=1, source_target_pairs={{0,1},{1,2},{2,3},{3,0},{4,5},{5,6},{6,7},{7,4},{8,9},{9,10},{10,1... | collective-permute-start | bytes 589832 | tf_op jit(solution)/shard_map/ppermute | solution.py:238
  75.8 0.6 stack.87.index_ref
  76.4 3.8 %pedigree.2.refs_2_ = bf16[12,64,128]{2,1,0:T(8,128)(2,1)} custom-call(s32[24,4]{1,0:T(8,128)} %copy.12.index_ref, s32[24]{0:T(128)} %count_ref.3, bf16[24,64,128]{2,1,0:T(8,128)(2,1)} %get-tuple-element.45.own_ref, bf16[16,64,128]{2,1,0:T(8,128)(2,1)} %bitcast.38, bf16[24,4,128,128]{3,2,1,0:T(8,128)(2,1)} %prec_ref.3), custom_call_target="tpu_custom_call" | custom-call | tf_op jit(solution)/shard_map/pedigree/pallas_call | solution.py:157
  80.2 0.0 collective-permute-start.6
  80.2 2.4 %collective-permute-start.7 = (bf16[12,64,128]{2,1,0:T(8,128)(2,1)}, bf16[12,64,128]{2,1,0:T(8,128)(2,1)S(1)}, u32[]{:S(2)}, u32[]{:S(2)}) collective-permute-start(bf16[12,64,128]{2,1,0:T(8,128)(2,1)} %pedigree.2.refs_2_), channel_id=1, source_target_pairs={{0,2},{1,3},{2,0},{3,1},{4,6},{5,7},{6,4},{7,5},{8,10},{9,11},{10,... | collective-permute-start | bytes 589832 | tf_op jit(solution)/shard_map/ppermute | solution.py:238
  82.6 1.7 %collective-permute-done.10.refs_4_ = bf16[12,64,128]{2,1,0:T(8,128)(2,1)S(1)} collective-permute-done((bf16[12,64,128]{2,1,0:T(8,128)(2,1)}, bf16[12,64,128]{2,1,0:T(8,128)(2,1)S(1)}, u32[]{:S(2)}, u32[]{:S(2)}) %collective-permute-start.10) | collective-permute-done | bytes 196640 | tf_op jit(solution)/shard_map/ppermute | solution.py:238
  84.3 0.4 collective-permute-start.8
  84.6 12.8 %collective-permute-done.11.refs_5_ = bf16[12,64,128]{2,1,0:T(8,128)(2,1)S(1)} collective-permute-done((bf16[12,64,128]{2,1,0:T(8,128)(2,1)}, bf16[12,64,128]{2,1,0:T(8,128)(2,1)S(1)}, u32[]{:S(2)}, u32[]{:S(2)}) %collective-permute-start.11) | collective-permute-done | bytes 196640 | tf_op jit(solution)/shard_map/ppermute | solution.py:238
  97.4 0.0 collective-permute-done.9.refs_3_
  97.5 0.7 copy-done.14
  98.1 13.6 %backward_product.2 = (f32[6400,128]{1,0:T(8,128)}, f32[6400,128]{1,0:T(8,128)}) custom-call(s32[1]{0:T(128)} %bitcast.6.place_ref, bf16[3072,6400]{1,0:T(8,128)(2,1)} %refs_1_.3, bf16[3072,6400]{1,0:T(8,128)(2,1)} %refs_1_.3, bf16[12,64,128]{2,1,0:T(8,128)(2,1)} %pedigree.3.refs_2_, bf16[12,64,128]{2,1,0:T(8,128)(2,1)} %collective-permute-done.9.refs_3_, ...), custom_call_target="tpu_custom_call" | custom-call | flops 5033164800 | bytes 27000832 | tf_op jit(solution)/shard_map/backward_product/pallas_call | solution.py:215
  111.7 0.0 copy-start.10
  111.7 0.0 collective-permute-done.7.refs_4_
  111.8 0.6 copy-done.10
  112.4 0.1 copy-done.11
  112.5 0.0 copy-done.12
  112.5 14.2 %backward_product.3 = (bf16[6400,128]{1,0:T(8,128)(2,1)}, bf16[6400,128]{1,0:T(8,128)(2,1)}) custom-call(s32[1]{0:T(128)} %bitcast.6.place_ref, bf16[3072,6400]{1,0:T(8,128)(2,1)} %refs_1_.3, bf16[3072,6400]{1,0:T(8,128)(2,1)} %refs_1_.3, bf16[12,64,128]{2,1,0:T(8,128)(2,1)} %pedigree.2.refs_2_, bf16[12,64,128]{2,1,0:T(8,128)(2,1)} %copy-done.10, ...), custom_call_target="tpu_custom_call" | custom-call | flops 5033164800 | bytes 33554432 | tf_op jit(solution)/shard_map/backward_product/pallas_call | solution.py:215
  126.7 4.4 %combine.3 = (bf16[4,800,128]{2,1,0:T(8,128)(2,1)}, bf16[4,800,128]{2,1,0:T(8,128)(2,1)}) custom-call(s32[8]{0:T(128)} %stack.87.index_ref, bf16[8,800,128]{2,1,0:T(8,128)(2,1)} %bitcast.29, bf16[8,800,128]{2,1,0:T(8,128)(2,1)} %bitcast.33), custom_call_target="tpu_custom_call" | custom-call | tf_op jit(solution)/shard_map/combine/pallas_call | solution.py:266
  131.1 0.5 collective-permute-start.13
  131.6 0.6 stack.96.index_ref
  132.3 2.3 %collective-permute-done.12.refs_1_ = bf16[4,800,128]{2,1,0:T(8,128)(2,1)S(1)} collective-permute-done((bf16[4,800,128]{2,1,0:T(8,128)(2,1)}, bf16[4,800,128]{2,1,0:T(8,128)(2,1)S(1)}, u32[]{:S(2)}, u32[]{:S(2)}) %collective-permute-start.12) | collective-permute-done | bytes 819232 | tf_op jit(solution)/shard_map/ppermute | solution.py:339
  134.6 0.4 collective-permute-done.13.refs_3_.refs_4_.refs_5_
  135.0 0.5 copy-done
  135.5 3.0 %combine.4 = (bf16[2,800,128]{2,1,0:T(8,128)(2,1)}, bf16[2,800,128]{2,1,0:T(8,128)(2,1)}) custom-call(s32[8]{0:T(128)} %stack.96.index_ref, bf16[8,800,128]{2,1,0:T(8,128)(2,1)} %bitcast.30, bf16[4,800,128]{2,1,0:T(8,128)(2,1)} %copy-done, bf16[8,800,128]{2,1,0:T(8,128)(2,1)} %bitcast.34, bf16[4,800,128]{2,1,0:T(8,128)(2,1)} %collective-permute-done.13.refs_3_.refs_4_.refs_5_), custom_call_target="tpu_custom_call" | custom-call | tf_op jit(solution)/shard_map/combine/pallas_call | solution.py:266
  138.5 1.1 collective-permute-start.14
  139.6 0.6 collective-permute-start.15
  140.2 0.6 stack.102.index_ref
  140.8 9.5 %collective-permute-done.14.refs_2_ = bf16[2,800,128]{2,1,0:T(8,128)(2,1)S(1)} collective-permute-done((bf16[2,800,128]{2,1,0:T(8,128)(2,1)}, bf16[2,800,128]{2,1,0:T(8,128)(2,1)S(1)}, u32[]{:S(2)}, u32[]{:S(2)}) %collective-permute-start.14) | collective-permute-done | bytes 409632 | tf_op jit(solution)/shard_map/ppermute | solution.py:339
  150.2 0.8 collective-permute-done.15.refs_5_.refs_6_
  151.0 0.8 copy-done.3
  151.8 2.8 %combine.5 = (bf16[1,800,128]{2,1,0:T(8,128)(2,1)}, bf16[1,800,128]{2,1,0:T(8,128)(2,1)}) custom-call(s32[6]{0:T(128)} %stack.102.index_ref, bf16[8,800,128]{2,1,0:T(8,128)(2,1)} %bitcast.31, bf16[4,800,128]{2,1,0:T(8,128)(2,1)} %copy-done, bf16[2,800,128]{2,1,0:T(8,128)(2,1)} %copy-done.2, bf16[8,800,128]{2,1,0:T(8,128)(2,1)} %bitcast.35, ...), custom_call_target="tpu_custom_call" | custom-call | tf_op jit(solution)/shard_map/combine/pallas_call | solution.py:266
  154.6 0.6 collective-permute-start.16
  155.2 1.0 collective-permute-start.17
  156.2 0.8 dynamic_slice.3
  157.0 0.9 reshape.36.ridge_ref
  157.9 0.6 concatenate.3.index_ref
  158.5 2.5 %collective-permute-done.16.refs_3_ = bf16[1,800,128]{2,1,0:T(8,128)(2,1)S(1)} collective-permute-done((bf16[1,800,128]{2,1,0:T(8,128)(2,1)}, bf16[1,800,128]{2,1,0:T(8,128)(2,1)S(1)}, u32[]{:S(2)}, u32[]{:S(2)}) %collective-permute-start.16) | collective-permute-done | bytes 204832 | tf_op jit(solution)/shard_map/ppermute | solution.py:339
  161.1 0.3 collective-permute-done.17.refs_7_
  161.4 0.4 copy-done.8
  161.7 0.3 copy-done.9
  162.0 3.5 %finish.1 = f32[800,256]{1,0:T(8,128)} custom-call(s32[9]{0:T(128)} %concatenate.3.index_ref, f32[800,1]{1,0:T(8,128)} %reshape.36.ridge_ref, bf16[8,800,256]{2,1,0:T(8,128)(2,1)} %bitcast.28, bf16[8,800,128]{2,1,0:T(8,128)(2,1)} %bitcast.32, bf16[4,800,128]{2,1,0:T(8,128)(2,1)} %copy-done, bf16[2,800,128]{2,1,0:T(8,128)(2,1)} %copy-done.2, ...), custom_call_target="tpu_custom_call" | custom-call | tf_op jit(solution)/shard_map/finish/pallas_call | solution.py:289
  (28 shorter events, 0.1 us)
Async XLA Ops:
  11.8 16.4 %collective-permute-start = (s16[816,128]{1,0:T(8,128)(2,1)}, s16[816,128]{1,0:T(8,128)(2,1)S(1)}, u32[]{:S(2)}, u32[]{:S(2)}) collective-permute-start(s16[816,128]{1,0:T(8,128)(2,1)} %get-tuple-element.36), channel_id=1, source_target_pairs={{0,1},{1,2},{2,3},{3,0},{4,5},{5,6},{6,7},{7,4},{8,9},{9,10},{10,1... | collective-permute-start | bytes 626696 | tf_op jit(solution)/shard_map/ppermute | solution.py:238
  13.4 18.2 %collective-permute-start.1 = (s16[816,128]{1,0:T(8,128)(2,1)}, s16[816,128]{1,0:T(8,128)(2,1)S(1)}, u32[]{:S(2)}, u32[]{:S(2)}) collective-permute-start(s16[816,128]{1,0:T(8,128)(2,1)} %get-tuple-element.37), channel_id=1, source_target_pairs={{0,2},{1,3},{2,0},{3,1},{4,6},{5,7},{6,4},{7,5},{8,10},{9,11},{10,... | collective-permute-start | bytes 626696 | tf_op jit(solution)/shard_map/ppermute | solution.py:238
  14.5 22.4 %copy-start.16 = (s32[1,8,2]{1,2,0:T(2,128)S(1)}, s32[1,8,2]{1,2,0:T(2,128)}, u32[]{:S(2)}) copy-start(s32[1,8,2]{1,2,0:T(2,128)} %param.10) | copy-start | bytes 196
  14.5 45.6 %copy-start.15 = (s32[24,4]{0,1:T(4,128)S(1)}, s32[24,4]{0,1:T(4,128)}, u32[]{:S(2)}) copy-start(s32[24,4]{0,1:T(4,128)} %param.11) | copy-start | bytes 1156
  14.5 18.8 %collective-permute-start.2 = (s16[816,128]{1,0:T(8,128)(2,1)}, s16[816,128]{1,0:T(8,128)(2,1)S(1)}, u32[]{:S(2)}, u32[]{:S(2)}) collective-permute-start(s16[816,128]{1,0:T(8,128)(2,1)} %get-tuple-element.38), channel_id=1, source_target_pairs={{0,3},{1,0},{2,1},{3,2},{4,7},{5,4},{6,5},{7,6},{8,11},{9,8},{10,9... | collective-permute-start | bytes 626696 | tf_op jit(solution)/shard_map/ppermute | solution.py:238
  28.2 24.7 %copy-start.4 = (s16[816,128]{1,0:T(8,128)(2,1)}, s16[816,128]{1,0:T(8,128)(2,1)S(1)}, u32[]{:S(2)}) copy-start(s16[816,128]{1,0:T(8,128)(2,1)S(1)} %collective-permute-done.refs_2_) | copy-start | bytes 626692
  31.5 21.4 %copy-start.5 = (s16[816,128]{1,0:T(8,128)(2,1)}, s16[816,128]{1,0:T(8,128)(2,1)S(1)}, u32[]{:S(2)}) copy-start(s16[816,128]{1,0:T(8,128)(2,1)S(1)} %collective-permute-done.1.refs_4_) | copy-start | bytes 626692
  33.2 19.7 %copy-start.6 = (s16[816,128]{1,0:T(8,128)(2,1)}, s16[816,128]{1,0:T(8,128)(2,1)S(1)}, u32[]{:S(2)}) copy-start(s16[816,128]{1,0:T(8,128)(2,1)S(1)} %collective-permute-done.2.refs_6_) | copy-start | bytes 626692
  33.2 8.2 %collective-permute-start.3 = (s16[816,128]{1,0:T(8,128)(2,1)}, s16[816,128]{1,0:T(8,128)(2,1)S(1)}, u32[]{:S(2)}, u32[]{:S(2)}) collective-permute-start(s16[816,128]{1,0:T(8,128)(2,1)} %get-tuple-element.40), channel_id=1, source_target_pairs={{0,1},{1,2},{2,3},{3,0},{4,5},{5,6},{6,7},{7,4},{8,9},{9,10},{10,1... | collective-permute-start | bytes 626696 | tf_op jit(solution)/shard_map/ppermute | solution.py:238
  33.2 18.6 %collective-permute-start.4 = (s16[816,128]{1,0:T(8,128)(2,1)}, s16[816,128]{1,0:T(8,128)(2,1)}, u32[]{:S(2)}, u32[]{:S(2)}) collective-permute-start(s16[816,128]{1,0:T(8,128)(2,1)} %get-tuple-element.42), channel_id=1, source_target_pairs={{0,2},{1,3},{2,0},{3,1},{4,6},{5,7},{6,4},{7,5},{8,10},{9,11},{10,... | collective-permute-start | bytes 626696 | tf_op jit(solution)/shard_map/ppermute | solution.py:238
  34.9 18.0 %collective-permute-start.5 = (s16[816,128]{1,0:T(8,128)(2,1)}, s16[816,128]{1,0:T(8,128)(2,1)}, u32[]{:S(2)}, u32[]{:S(2)}) collective-permute-start(s16[816,128]{1,0:T(8,128)(2,1)} %get-tuple-element.44), channel_id=1, source_target_pairs={{0,3},{1,0},{2,1},{3,2},{4,7},{5,4},{6,5},{7,6},{8,11},{9,8},{10,9... | collective-permute-start | bytes 626696 | tf_op jit(solution)/shard_map/ppermute | solution.py:238
  41.5 11.4 %copy-start.7 = (s16[816,128]{1,0:T(8,128)(2,1)}, s16[816,128]{1,0:T(8,128)(2,1)S(1)}, u32[]{:S(2)}) copy-start(s16[816,128]{1,0:T(8,128)(2,1)S(1)} %collective-permute-done.3.refs_3_) | copy-start | bytes 626692
  56.3 10.7 %all-to-all-start = ((bf16[8,2,64,128]{3,2,1,0:T(8,128)(2,1)}), bf16[8,2,64,128]{3,2,1,0:T(8,128)(2,1)S(1)}, u32[]{:S(2)}, u32[]{:S(2)}) async-start(bf16[8,2,64,128]{3,2,1,0:T(8,128)(2,1)} %bitcast.39), calls=%async_computation | async-start | bytes 524288 | tf_op jit(solution)/shard_map/all_to_all | solution.py:370
  67.0 0.7 copy-start.1
  71.4 12.8 %collective-permute-start.10 = (bf16[12,64,128]{2,1,0:T(8,128)(2,1)}, bf16[12,64,128]{2,1,0:T(8,128)(2,1)S(1)}, u32[]{:S(2)}, u32[]{:S(2)}) collective-permute-start(bf16[12,64,128]{2,1,0:T(8,128)(2,1)} %pedigree.3.refs_2_), channel_id=1, source_target_pairs={{0,2},{1,3},{2,0},{3,1},{4,6},{5,7},{6,4},{7,5},{8,10},{9,11},{10,... | collective-permute-start | bytes 589832 | tf_op jit(solution)/shard_map/ppermute | solution.py:238
  73.8 23.7 %collective-permute-start.11 = (bf16[12,64,128]{2,1,0:T(8,128)(2,1)}, bf16[12,64,128]{2,1,0:T(8,128)(2,1)S(1)}, u32[]{:S(2)}, u32[]{:S(2)}) collective-permute-start(bf16[12,64,128]{2,1,0:T(8,128)(2,1)} %pedigree.3.refs_2_), channel_id=1, source_target_pairs={{0,3},{1,0},{2,1},{3,2},{4,7},{5,4},{6,5},{7,6},{8,11},{9,8},{10,9... | collective-permute-start | bytes 589832 | tf_op jit(solution)/shard_map/ppermute | solution.py:238
  73.8 23.7 %collective-permute-start.9 = (bf16[12,64,128]{2,1,0:T(8,128)(2,1)}, bf16[12,64,128]{2,1,0:T(8,128)(2,1)}, u32[]{:S(2)}, u32[]{:S(2)}) collective-permute-start(bf16[12,64,128]{2,1,0:T(8,128)(2,1)} %pedigree.3.refs_2_), channel_id=1, source_target_pairs={{0,1},{1,2},{2,3},{3,0},{4,5},{5,6},{6,7},{7,4},{8,9},{9,10},{10,1... | collective-permute-start | bytes 589832 | tf_op jit(solution)/shard_map/ppermute | solution.py:238
  80.2 31.5 %collective-permute-start.6 = (bf16[12,64,128]{2,1,0:T(8,128)(2,1)}, bf16[12,64,128]{2,1,0:T(8,128)(2,1)S(1)}, u32[]{:S(2)}, u32[]{:S(2)}) collective-permute-start(bf16[12,64,128]{2,1,0:T(8,128)(2,1)} %pedigree.2.refs_2_), channel_id=1, source_target_pairs={{0,1},{1,2},{2,3},{3,0},{4,5},{5,6},{6,7},{7,4},{8,9},{9,10},{10,1... | collective-permute-start | bytes 589832 | tf_op jit(solution)/shard_map/ppermute | solution.py:238
  80.2 31.5 %collective-permute-start.7 = (bf16[12,64,128]{2,1,0:T(8,128)(2,1)}, bf16[12,64,128]{2,1,0:T(8,128)(2,1)S(1)}, u32[]{:S(2)}, u32[]{:S(2)}) collective-permute-start(bf16[12,64,128]{2,1,0:T(8,128)(2,1)} %pedigree.2.refs_2_), channel_id=1, source_target_pairs={{0,2},{1,3},{2,0},{3,1},{4,6},{5,7},{6,4},{7,5},{8,10},{9,11},{10,... | collective-permute-start | bytes 589832 | tf_op jit(solution)/shard_map/ppermute | solution.py:238
  84.2 13.2 %copy-start.13 = (bf16[12,64,128]{2,1,0:T(8,128)(2,1)}, bf16[12,64,128]{2,1,0:T(8,128)(2,1)S(1)}, u32[]{:S(2)}) copy-start(bf16[12,64,128]{2,1,0:T(8,128)(2,1)S(1)} %collective-permute-done.10.refs_4_) | copy-start | bytes 589828
  84.3 27.5 %collective-permute-start.8 = (bf16[12,64,128]{2,1,0:T(8,128)(2,1)}, bf16[12,64,128]{2,1,0:T(8,128)(2,1)S(1)}, u32[]{:S(2)}, u32[]{:S(2)}) collective-permute-start(bf16[12,64,128]{2,1,0:T(8,128)(2,1)} %pedigree.2.refs_2_), channel_id=1, source_target_pairs={{0,3},{1,0},{2,1},{3,2},{4,7},{5,4},{6,5},{7,6},{8,11},{9,8},{10,9... | collective-permute-start | bytes 589832 | tf_op jit(solution)/shard_map/ppermute | solution.py:238
  97.4 0.7 copy-start.14
  111.7 0.7 copy-start.10
  111.8 0.7 copy-start.11
  111.8 0.8 copy-start.12
  131.1 3.5 %collective-permute-start.12 = (bf16[4,800,128]{2,1,0:T(8,128)(2,1)}, bf16[4,800,128]{2,1,0:T(8,128)(2,1)S(1)}, u32[]{:S(2)}, u32[]{:S(2)}) collective-permute-start(bf16[4,800,128]{2,1,0:T(8,128)(2,1)} %get-tuple-element.51), channel_id=1, source_target_pairs={{0,4},{4,0},{8,12},{12,8},{16,20},{20,16},{24,28},{28,24},{1,5},{5... | collective-permute-start | bytes 2457608 | tf_op jit(solution)/shard_map/ppermute | solution.py:339
  131.1 3.8 %collective-permute-start.13 = (bf16[4,800,128]{2,1,0:T(8,128)(2,1)}, bf16[4,800,128]{2,1,0:T(8,128)(2,1)}, u32[]{:S(2)}, u32[]{:S(2)}) collective-permute-start(bf16[4,800,128]{2,1,0:T(8,128)(2,1)} %get-tuple-element.52), channel_id=1, source_target_pairs={{0,4},{4,0},{8,12},{12,8},{16,20},{20,16},{24,28},{28,24},{1,5},{5... | collective-permute-start | bytes 2457608 | tf_op jit(solution)/shard_map/ppermute | solution.py:339
  134.6 0.9 copy-start
  138.5 11.7 %collective-permute-start.14 = (bf16[2,800,128]{2,1,0:T(8,128)(2,1)}, bf16[2,800,128]{2,1,0:T(8,128)(2,1)S(1)}, u32[]{:S(2)}, u32[]{:S(2)}) collective-permute-start(bf16[2,800,128]{2,1,0:T(8,128)(2,1)} %get-tuple-element.53), channel_id=1, source_target_pairs={{0,8},{4,12},{8,0},{12,4},{16,24},{20,28},{24,16},{28,20},{1,9},{5... | collective-permute-start | bytes 1228808 | tf_op jit(solution)/shard_map/ppermute | solution.py:339
  139.6 11.4 %collective-permute-start.15 = (bf16[2,800,128]{2,1,0:T(8,128)(2,1)}, bf16[2,800,128]{2,1,0:T(8,128)(2,1)S(1)}, u32[]{:S(2)}, u32[]{:S(2)}) collective-permute-start(bf16[2,800,128]{2,1,0:T(8,128)(2,1)} %get-tuple-element.54), channel_id=1, source_target_pairs={{0,16},{4,20},{8,24},{12,28},{16,0},{20,4},{24,8},{28,12},{1,17},{... | collective-permute-start | bytes 1228808 | tf_op jit(solution)/shard_map/ppermute | solution.py:339
  150.2 0.8 copy-start.2
  151.0 0.8 copy-start.3
  154.6 6.5 %collective-permute-start.16 = (bf16[1,800,128]{2,1,0:T(8,128)(2,1)}, bf16[1,800,128]{2,1,0:T(8,128)(2,1)S(1)}, u32[]{:S(2)}, u32[]{:S(2)}) collective-permute-start(bf16[1,800,128]{2,1,0:T(8,128)(2,1)} %get-tuple-element.55), channel_id=1, source_target_pairs={{0,16},{4,20},{8,24},{12,28},{16,0},{20,4},{24,8},{28,12},{1,17},{... | collective-permute-start | bytes 614408 | tf_op jit(solution)/shard_map/ppermute | solution.py:339
  155.2 6.1 %collective-permute-start.17 = (bf16[1,800,128]{2,1,0:T(8,128)(2,1)}, bf16[1,800,128]{2,1,0:T(8,128)(2,1)S(1)}, u32[]{:S(2)}, u32[]{:S(2)}) collective-permute-start(bf16[1,800,128]{2,1,0:T(8,128)(2,1)} %get-tuple-element.56), channel_id=1, source_target_pairs={{0,8},{4,12},{8,0},{12,4},{16,24},{20,28},{24,16},{28,20},{1,9},{5... | collective-permute-start | bytes 614408 | tf_op jit(solution)/shard_map/ppermute | solution.py:339
  161.1 0.7 copy-start.8
  161.4 0.7 copy-start.9

commit v7 on v3

--- a/solution.py
+++ b/solution.py
@@ -11,7 +11,7 @@
 MARKERS = 25600
 BLK = 128
 MARK = 16
-VMEM_LIMIT = 56 * 1024 * 1024
+VMEM_LIMIT = 63 * 1024 * 1024
 
 
 def divisor(total, unit, most):
@@ -142,10 +142,10 @@
             source = table[index_ref[block, j]]
             source = jnp.where(j < count_ref[block], source, jnp.zeros_like(source))
             term = lax.dot_general(
-                source, prec_ref[b, j], (((1,), (1,)), ((), ())), preferred_element_type=jnp.float32
+                prec_ref[b, j], source, (((1,), (1,)), ((), ())), preferred_element_type=jnp.float32
             )
             total = term if total is None else total + term
-        out_ref[b] = total.astype(out_ref.dtype)
+        out_ref[b] = total.T.astype(out_ref.dtype)
 
 
 def pedigree(blocked, incoming, rel_index, rel_count, rel_prec, start, count):

time: 161 us -> 160 us (level)
    unnamed x36 -> x30, local copies, waits for them, and re-layouts: 4.23 us -> 2.93 us
where the time goes in v7:
time: 160 us; the launch traced here: 159 us
  Pallas kernels  62.2 us (39%)
  waiting for transfers between devices  55.4 us (35%)
  starting transfers between devices  22.7 us (14%)
  other arithmetic  11 us (7%)
  local copies, waits for them, and re-layouts  7.52 us (5%)
    ppermute x12, waiting for transfers between devices, turn(): lax.ppermute(value, 'marker', [(d, (d + shift) % devices) for d in range(...  35.8 us
    pallas_call x2, Pallas kernels, backward_product(): pl.pallas_call(functools.partial(backward_kernel, scale, devices, lanes),...  27.8 us
    pallas_call x2, Pallas kernels, forward_product(): pl.pallas_call(functools.partial(forward_kernel, scale, devices), grid_sp...  23.6 us
    ppermute x12, starting transfers between devices, turn(): lax.ppermute(value, 'marker', [(d, (d + shift) % devices) for d in range(...  15 us
    ppermute x6, waiting for transfers between devices, halving_sum(): lax.ppermute(sent, 'animal', [(d, d ^ 1 << bit) for d in range(devices)])  13.4 us
    pallas_call x2, Pallas kernels, pedigree(): pl.pallas_call(functools.partial(pedigree_kernel, group, block_total, sta...  7.52 us
    convert_element_type x4, other arithmetic, halving_sum(): sent = sum((term.astype(jnp.float32) for term in sent)).astype(jnp.bfloat16)  6.66 us
    all_to_all x1, waiting for transfers between devices, local(): lax.all_to_all(outgoing, 'animal', split_axis=0, concat_axis=0, tiled=True)  6.25 us
  transfers between devices with their start and end apart: 19, of which 12 were waited for; matrix products, arithmetic and copies ran while one was open for 7% of the time, Pallas kernels for 18%

profile of v7, /device:TPU:8, one launch (start us, length us, event | category | flops | bytes accessed | tf_op | source)
XLA Modules:
  0.0 158.9 jit_solution(9932069791252005684)
XLA Ops:
  0.0 11.8 %forward_product.2 = (f32[12,64,128]{2,1,0:T(8,128)}, s16[816,128]{1,0:T(8,128)(2,1)}, s16[816,128]{1,0:T(8,128)(2,1)}, s16[816,128]{1,0:T(8,128)(2,1)}) custom-call(s32[1]{0:T(128)} %bitcast.place_ref, bf16[3072,6400]{1,0:T(8,128)(2,1)} %refs_1_.3, bf16[3072,6400]{1,0:T(8,128)(2,1)} %refs_1_.3, bf16[6400,256]{1,0:T(8,128)(2,1)} %direction_ref.3), custom_call_target="tpu_custom_call" | custom-call | flops 5033164800 | bytes 23724032 | tf_op jit(solution)/shard_map/forward_product/pallas_call | solution.py:60
  11.8 1.6 collective-permute-start
  13.4 1.1 collective-permute-start.1
  14.5 1.9 %collective-permute-start.2 = (s16[816,128]{1,0:T(8,128)(2,1)}, s16[816,128]{1,0:T(8,128)(2,1)S(1)}, u32[]{:S(2)}, u32[]{:S(2)}) collective-permute-start(s16[816,128]{1,0:T(8,128)(2,1)} %get-tuple-element.32), channel_id=1, source_target_pairs={{0,3},{1,0},{2,1},{3,2},{4,7},{5,4},{6,5},{7,6},{8,11},{9,8},{10,9... | collective-permute-start | bytes 626696 | tf_op jit(solution)/shard_map/ppermute | solution.py:238
  16.4 11.8 %forward_product.3 = (f32[12,64,128]{2,1,0:T(8,128)}, s16[816,128]{1,0:T(8,128)(2,1)}, s16[816,128]{1,0:T(8,128)(2,1)}, s16[816,128]{1,0:T(8,128)(2,1)}) custom-call(s32[1]{0:T(128)} %bitcast.place_ref, bf16[3072,6400]{1,0:T(8,128)(2,1)} %refs_1_.3, bf16[3072,6400]{1,0:T(8,128)(2,1)} %refs_1_.3, bf16[6400,256]{1,0:T(8,128)(2,1)} %direction_ref.3), custom_call_target="tpu_custom_call" | custom-call | flops 5033164800 | bytes 23724032 | tf_op jit(solution)/shard_map/forward_product/pallas_call | solution.py:60
  28.2 0.0 collective-permute-done.refs_2_
  28.2 3.3 %collective-permute-done.1.refs_4_ = s16[816,128]{1,0:T(8,128)(2,1)S(1)} collective-permute-done((s16[816,128]{1,0:T(8,128)(2,1)}, s16[816,128]{1,0:T(8,128)(2,1)S(1)}, u32[]{:S(2)}, u32[]{:S(2)}) %collective-permute-start.1) | collective-permute-done | bytes 208928 | tf_op jit(solution)/shard_map/ppermute | solution.py:238
  31.5 1.7 %collective-permute-done.2.refs_6_ = s16[816,128]{1,0:T(8,128)(2,1)S(1)} collective-permute-done((s16[816,128]{1,0:T(8,128)(2,1)}, s16[816,128]{1,0:T(8,128)(2,1)S(1)}, u32[]{:S(2)}, u32[]{:S(2)}) %collective-permute-start.2) | collective-permute-done | bytes 208928 | tf_op jit(solution)/shard_map/ppermute | solution.py:238
  33.2 0.0 collective-permute-start.3
  33.2 1.7 %collective-permute-start.4 = (s16[816,128]{1,0:T(8,128)(2,1)}, s16[816,128]{1,0:T(8,128)(2,1)}, u32[]{:S(2)}, u32[]{:S(2)}) collective-permute-start(s16[816,128]{1,0:T(8,128)(2,1)} %get-tuple-element.36), channel_id=1, source_target_pairs={{0,2},{1,3},{2,0},{3,1},{4,6},{5,7},{6,4},{7,5},{8,10},{9,11},{10,... | collective-permute-start | bytes 626696 | tf_op jit(solution)/shard_map/ppermute | solution.py:238
  34.9 1.9 %collective-permute-start.5 = (s16[816,128]{1,0:T(8,128)(2,1)}, s16[816,128]{1,0:T(8,128)(2,1)}, u32[]{:S(2)}, u32[]{:S(2)}) collective-permute-start(s16[816,128]{1,0:T(8,128)(2,1)} %get-tuple-element.38), channel_id=1, source_target_pairs={{0,3},{1,0},{2,1},{3,2},{4,7},{5,4},{6,5},{7,6},{8,11},{9,8},{10,9... | collective-permute-start | bytes 626696 | tf_op jit(solution)/shard_map/ppermute | solution.py:238
  36.9 0.1 copy.12
  37.0 0.6 reshape.70.list_ref
  37.6 3.9 %collective-permute-done.3.refs_3_ = s16[816,128]{1,0:T(8,128)(2,1)S(1)} collective-permute-done((s16[816,128]{1,0:T(8,128)(2,1)}, s16[816,128]{1,0:T(8,128)(2,1)S(1)}, u32[]{:S(2)}, u32[]{:S(2)}) %collective-permute-start.3) | collective-permute-done | bytes 208928 | tf_op jit(solution)/shard_map/ppermute | solution.py:238
  41.5 10.4 %collective-permute-done.4.refs_5_ = s16[816,128]{1,0:T(8,128)(2,1)} collective-permute-done((s16[816,128]{1,0:T(8,128)(2,1)}, s16[816,128]{1,0:T(8,128)(2,1)}, u32[]{:S(2)}, u32[]{:S(2)}) %collective-permute-start.4) | collective-permute-done | bytes 208928 | tf_op jit(solution)/shard_map/ppermute | solution.py:238
  51.9 1.0 collective-permute-done.5.refs_7_
  52.9 3.4 %settle.1 = (bf16[24,64,128]{2,1,0:T(8,128)(2,1)}, bf16[16,64,128]{2,1,0:T(8,128)(2,1)}) custom-call(s32[16]{0:T(128)} %reshape.70.list_ref, f32[12,64,128]{2,1,0:T(8,128)} %get-tuple-element.25.refs_0_, f32[12,64,128]{2,1,0:T(8,128)} %get-tuple-element.26.refs_1_, s16[816,128]{1,0:T(8,128)(2,1)} %copy-done.3, s16[816,128]{1,0:T(8,128)(2,1)} %copy-done.6, ...), custom_call_target="tpu_custom_call" | custom-call | tf_op jit(solution)/shard_map/settle/pallas_call | solution.py:110
  56.3 3.7 %all-to-all-start = ((bf16[8,2,64,128]{3,2,1,0:T(8,128)(2,1)}), bf16[8,2,64,128]{3,2,1,0:T(8,128)(2,1)S(1)}, u32[]{:S(2)}, u32[]{:S(2)}) async-start(bf16[8,2,64,128]{3,2,1,0:T(8,128)(2,1)} %bitcast.69), calls=%async_computation | async-start | bytes 524288 | tf_op jit(solution)/shard_map/all_to_all | solution.py:285
  60.0 0.7 copy.13.index_ref
  60.7 6.3 %all-to-all-done = bf16[8,2,64,128]{3,2,1,0:T(8,128)(2,1)S(1)} async-done(((bf16[8,2,64,128]{3,2,1,0:T(8,128)(2,1)}), bf16[8,2,64,128]{3,2,1,0:T(8,128)(2,1)S(1)}, u32[]{:S(2)}, u32[]{:S(2)}) %all-to-all-start) | async-done | bytes 262176 | tf_op jit(solution)/shard_map/all_to_all | solution.py:285
  67.0 0.7 copy-done
  67.7 3.8 %pedigree.3.refs_2_ = bf16[12,64,128]{2,1,0:T(8,128)(2,1)} custom-call(s32[24,4]{1,0:T(8,128)} %copy.13.index_ref, s32[24]{0:T(128)} %count_ref.3, bf16[24,64,128]{2,1,0:T(8,128)(2,1)} %get-tuple-element.39.own_ref, bf16[16,64,128]{2,1,0:T(8,128)(2,1)} %bitcast.59, bf16[24,4,128,128]{3,2,1,0:T(8,128)(2,1)} %prec_ref.3), custom_call_target="tpu_custom_call" | custom-call | tf_op jit(solution)/shard_map/pedigree/pallas_call | solution.py:157
  71.4 2.4 %collective-permute-start.10 = (bf16[12,64,128]{2,1,0:T(8,128)(2,1)}, bf16[12,64,128]{2,1,0:T(8,128)(2,1)S(1)}, u32[]{:S(2)}, u32[]{:S(2)}) collective-permute-start(bf16[12,64,128]{2,1,0:T(8,128)(2,1)} %pedigree.3.refs_2_), channel_id=1, source_target_pairs={{0,2},{1,3},{2,0},{3,1},{4,6},{5,7},{6,4},{7,5},{8,10},{9,11},{10,... | collective-permute-start | bytes 589832 | tf_op jit(solution)/shard_map/ppermute | solution.py:238
  73.8 0.0 collective-permute-start.11
  73.8 2.0 %collective-permute-start.9 = (bf16[12,64,128]{2,1,0:T(8,128)(2,1)}, bf16[12,64,128]{2,1,0:T(8,128)(2,1)}, u32[]{:S(2)}, u32[]{:S(2)}) collective-permute-start(bf16[12,64,128]{2,1,0:T(8,128)(2,1)} %pedigree.3.refs_2_), channel_id=1, source_target_pairs={{0,1},{1,2},{2,3},{3,0},{4,5},{5,6},{6,7},{7,4},{8,9},{9,10},{10,1... | collective-permute-start | bytes 589832 | tf_op jit(solution)/shard_map/ppermute | solution.py:238
  75.8 3.8 %pedigree.2.refs_2_ = bf16[12,64,128]{2,1,0:T(8,128)(2,1)} custom-call(s32[24,4]{1,0:T(8,128)} %copy.13.index_ref, s32[24]{0:T(128)} %count_ref.3, bf16[24,64,128]{2,1,0:T(8,128)(2,1)} %get-tuple-element.39.own_ref, bf16[16,64,128]{2,1,0:T(8,128)(2,1)} %bitcast.60, bf16[24,4,128,128]{3,2,1,0:T(8,128)(2,1)} %prec_ref.3), custom_call_target="tpu_custom_call" | custom-call | tf_op jit(solution)/shard_map/pedigree/pallas_call | solution.py:157
  79.6 0.0 collective-permute-start.6
  79.6 2.4 %collective-permute-start.7 = (bf16[12,64,128]{2,1,0:T(8,128)(2,1)}, bf16[12,64,128]{2,1,0:T(8,128)(2,1)S(1)}, u32[]{:S(2)}, u32[]{:S(2)}) collective-permute-start(bf16[12,64,128]{2,1,0:T(8,128)(2,1)} %pedigree.2.refs_2_), channel_id=1, source_target_pairs={{0,2},{1,3},{2,0},{3,1},{4,6},{5,7},{6,4},{7,5},{8,10},{9,11},{10,... | collective-permute-start | bytes 589832 | tf_op jit(solution)/shard_map/ppermute | solution.py:238
  81.9 2.3 %collective-permute-done.10.refs_4_ = bf16[12,64,128]{2,1,0:T(8,128)(2,1)S(1)} collective-permute-done((bf16[12,64,128]{2,1,0:T(8,128)(2,1)}, bf16[12,64,128]{2,1,0:T(8,128)(2,1)S(1)}, u32[]{:S(2)}, u32[]{:S(2)}) %collective-permute-start.10) | collective-permute-done | bytes 196640 | tf_op jit(solution)/shard_map/ppermute | solution.py:238
  84.2 0.0 collective-permute-start.8
  84.2 13.2 %collective-permute-done.11.refs_5_ = bf16[12,64,128]{2,1,0:T(8,128)(2,1)S(1)} collective-permute-done((bf16[12,64,128]{2,1,0:T(8,128)(2,1)}, bf16[12,64,128]{2,1,0:T(8,128)(2,1)S(1)}, u32[]{:S(2)}, u32[]{:S(2)}) %collective-permute-start.11) | collective-permute-done | bytes 196640 | tf_op jit(solution)/shard_map/ppermute | solution.py:238
  97.4 0.0 collective-permute-done.9.refs_3_
  97.4 0.7 copy-done.11
  98.1 13.6 %backward_product.2 = (f32[6400,128]{1,0:T(8,128)}, f32[6400,128]{1,0:T(8,128)}) custom-call(s32[1]{0:T(128)} %bitcast.place_ref, bf16[3072,6400]{1,0:T(8,128)(2,1)} %refs_1_.3, bf16[3072,6400]{1,0:T(8,128)(2,1)} %refs_1_.3, bf16[12,64,128]{2,1,0:T(8,128)(2,1)} %pedigree.3.refs_2_, bf16[12,64,128]{2,1,0:T(8,128)(2,1)} %collective-permute-done.9.refs_3_, ...), custom_call_target="tpu_custom_call" | custom-call | flops 5033164800 | bytes 27000832 | tf_op jit(solution)/shard_map/backward_product/pallas_call | solution.py:215
  111.7 0.0 collective-permute-done.6.refs_3_
  111.7 0.0 copy-start.7
  111.7 0.0 collective-permute-done.7.refs_4_
  111.7 0.0 collective-permute-done.8.refs_5_
  111.7 0.6 copy-done.7
  112.4 0.1 copy-done.8
  112.4 0.1 copy-done.9
  112.5 14.2 %backward_product.3 = (bf16[6400,128]{1,0:T(8,128)(2,1)}, bf16[6400,128]{1,0:T(8,128)(2,1)}) custom-call(s32[1]{0:T(128)} %bitcast.place_ref, bf16[3072,6400]{1,0:T(8,128)(2,1)} %refs_1_.3, bf16[3072,6400]{1,0:T(8,128)(2,1)} %refs_1_.3, bf16[12,64,128]{2,1,0:T(8,128)(2,1)} %pedigree.2.refs_2_, bf16[12,64,128]{2,1,0:T(8,128)(2,1)} %copy-done.7, ...), custom_call_target="tpu_custom_call" | custom-call | flops 5033164800 | bytes 33554432 | tf_op jit(solution)/shard_map/backward_product/pallas_call | solution.py:215
  126.7 2.3 %dynamic-slice_bitcast_fusion.1 = bf16[2,2,800,128]{3,2,1,0:T(8,128)(2,1)} fusion(bf16[2,2,2,800,128]{4,3,2,1,0:T(8,128)(2,1)} %bitcast.65, s32[]{:T(128)S(6)} %select_n.60), kind=kLoop, calls=%fused_computation.6 | loop fusion | bytes 1638404 | tf_op jit(solution)/shard_map/jit(dynamic_index_in_dim)/squeeze | solution.py:250
  129.0 0.0 collective-permute-start.12
  129.0 0.9 dynamic-slice_bitcast_fusion
  129.9 0.5 collective-permute-start.15
  130.4 1.2 collective-permute-done.12
  131.6 1.9 %fusion.1 = bf16[2,800,128]{2,1,0:T(8,128)(2,1)} fusion(bf16[2,2,800,128]{3,2,1,0:T(8,128)(2,1)} %collective-permute-done.12, s32[]{:T(128)S(6)} %select_n.61, bf16[2,2,2,800,128]{4,3,2,1,0:T(8,128)(2,1)S(1)} %bitcast.66, s32[]{:T(128)S(6)} %select_n.62, s32[]{:T(128)S(6)} %select_n.59), kind=kLoop, calls=%fused_computation.4 | loop fusion | flops 819200 | bytes 1228812 | tf_op jit(solution)/shard_map/convert_element_type | solution.py:253
  133.5 1.1 collective-permute-start.13
  134.6 0.0 collective-permute-done.15
  134.6 1.9 %fusion = bf16[2,800,128]{2,1,0:T(8,128)(2,1)} fusion(bf16[2,2,800,128]{3,2,1,0:T(8,128)(2,1)} %collective-permute-done.15, s32[]{:T(128)S(6)} %select_n.63, bf16[2,2,2,800,128]{4,3,2,1,0:T(8,128)(2,1)S(1)} %bitcast.62, s32[]{:T(128)S(6)} %select_n.64, s32[]{:T(128)S(6)} %select_n.59), kind=kLoop, calls=%fused_computation.2 | loop fusion | flops 819200 | bytes 1228812 | tf_op jit(solution)/shard_map/convert_element_type | solution.py:253
  136.5 0.6 collective-permute-start.16
  137.0 8.3 %collective-permute-done.13 = bf16[2,800,128]{2,1,0:T(8,128)(2,1)} collective-permute-done((bf16[2,800,128]{2,1,0:T(8,128)(2,1)}, bf16[2,800,128]{2,1,0:T(8,128)(2,1)}, u32[]{:S(2)}, u32[]{:S(2)}) %collective-permute-start.13) | collective-permute-done | bytes 409632 | tf_op jit(solution)/shard_map/ppermute | solution.py:254
  145.3 1.8 %fusion.4 = bf16[800,128]{1,0:T(8,128)(2,1)} fusion(bf16[2,800,128]{2,1,0:T(8,128)(2,1)} %collective-permute-done.13, s32[]{:T(128)S(6)} %select_n.63, bf16[2,2,800,128]{3,2,1,0:T(8,128)(2,1)} %collective-permute-done.12, s32[]{:T(128)S(6)} %select_n.64, s32[]{:T(128)S(6)} %select_n.57, bf16[2,2,2,800,128]{4,3,2,1,0:T(8,128)(2,1)S(1)} %bitcast.67, ...), kind=kLoop, calls=%fused_computation.14 | loop fusion | flops 614400 | bytes 819216 | tf_op jit(solution)/shard_map/convert_element_type | solution.py:253
  147.2 0.6 collective-permute-start.14
  147.7 0.8 dynamic_slice.88
  148.5 0.0 collective-permute-done.16
  148.5 1.1 fusion.2
  149.6 1.1 collective-permute-start.17
  150.8 2.9 %collective-permute-done.14 = bf16[800,128]{1,0:T(8,128)(2,1)S(1)} collective-permute-done((bf16[800,128]{1,0:T(8,128)(2,1)}, bf16[800,128]{1,0:T(8,128)(2,1)S(1)}, u32[]{:S(2)}, u32[]{:S(2)}) %collective-permute-start.14) | collective-permute-done | bytes 204832 | tf_op jit(solution)/shard_map/ppermute | solution.py:254
  153.7 1.1 fusion.5
  154.8 0.9 collective-permute-done.17
  155.7 1.1 fusion.3
  156.9 2.1 %maximum_add_fusion = f32[800,256]{1,0:T(8,128)} fusion(f32[800,128]{1,0:T(8,128)S(1)} %fusion.3, f32[800,128]{1,0:T(8,128)S(1)} %fusion.5, bf16[6400,256]{1,0:T(8,128)(2,1)} %direction_ref.3, s32[]{:T(128)S(6)} %select_n.65, f32[800]{0:T(1024)S(1)} %dynamic_slice.88), kind=kLoop, calls=%fused_computation | loop fusion | flops 819200 | bytes 2051204 | tf_op jit(solution)/shard_map/add | solution.py:310
  (22 shorter events, 0.0 us)
Async XLA Ops:
  11.8 16.4 %collective-permute-start = (s16[816,128]{1,0:T(8,128)(2,1)}, s16[816,128]{1,0:T(8,128)(2,1)S(1)}, u32[]{:S(2)}, u32[]{:S(2)}) collective-permute-start(s16[816,128]{1,0:T(8,128)(2,1)} %get-tuple-element.30), channel_id=1, source_target_pairs={{0,1},{1,2},{2,3},{3,0},{4,5},{5,6},{6,7},{7,4},{8,9},{9,10},{10,1... | collective-permute-start | bytes 626696 | tf_op jit(solution)/shard_map/ppermute | solution.py:238
  13.4 18.2 %collective-permute-start.1 = (s16[816,128]{1,0:T(8,128)(2,1)}, s16[816,128]{1,0:T(8,128)(2,1)S(1)}, u32[]{:S(2)}, u32[]{:S(2)}) collective-permute-start(s16[816,128]{1,0:T(8,128)(2,1)} %get-tuple-element.31), channel_id=1, source_target_pairs={{0,2},{1,3},{2,0},{3,1},{4,6},{5,7},{6,4},{7,5},{8,10},{9,11},{10,... | collective-permute-start | bytes 626696 | tf_op jit(solution)/shard_map/ppermute | solution.py:238
  14.5 22.4 %copy-start.13 = (s32[1,8,2]{1,2,0:T(2,128)S(1)}, s32[1,8,2]{1,2,0:T(2,128)}, u32[]{:S(2)}) copy-start(s32[1,8,2]{1,2,0:T(2,128)} %param.10) | copy-start | bytes 196
  14.5 18.8 %collective-permute-start.2 = (s16[816,128]{1,0:T(8,128)(2,1)}, s16[816,128]{1,0:T(8,128)(2,1)S(1)}, u32[]{:S(2)}, u32[]{:S(2)}) collective-permute-start(s16[816,128]{1,0:T(8,128)(2,1)} %get-tuple-element.32), channel_id=1, source_target_pairs={{0,3},{1,0},{2,1},{3,2},{4,7},{5,4},{6,5},{7,6},{8,11},{9,8},{10,9... | collective-permute-start | bytes 626696 | tf_op jit(solution)/shard_map/ppermute | solution.py:238
  28.2 31.8 %copy-start.12 = (s32[24,4]{0,1:T(4,128)S(1)}, s32[24,4]{0,1:T(4,128)}, u32[]{:S(2)}) copy-start(s32[24,4]{0,1:T(4,128)} %param.11) | copy-start | bytes 1156
  28.2 24.7 %copy-start.3 = (s16[816,128]{1,0:T(8,128)(2,1)}, s16[816,128]{1,0:T(8,128)(2,1)S(1)}, u32[]{:S(2)}) copy-start(s16[816,128]{1,0:T(8,128)(2,1)S(1)} %collective-permute-done.refs_2_) | copy-start | bytes 626692
  31.5 21.4 %copy-start.4 = (s16[816,128]{1,0:T(8,128)(2,1)}, s16[816,128]{1,0:T(8,128)(2,1)S(1)}, u32[]{:S(2)}) copy-start(s16[816,128]{1,0:T(8,128)(2,1)S(1)} %collective-permute-done.1.refs_4_) | copy-start | bytes 626692
  33.2 19.7 %copy-start.5 = (s16[816,128]{1,0:T(8,128)(2,1)}, s16[816,128]{1,0:T(8,128)(2,1)S(1)}, u32[]{:S(2)}) copy-start(s16[816,128]{1,0:T(8,128)(2,1)S(1)} %collective-permute-done.2.refs_6_) | copy-start | bytes 626692
  33.2 8.2 %collective-permute-start.3 = (s16[816,128]{1,0:T(8,128)(2,1)}, s16[816,128]{1,0:T(8,128)(2,1)S(1)}, u32[]{:S(2)}, u32[]{:S(2)}) collective-permute-start(s16[816,128]{1,0:T(8,128)(2,1)} %get-tuple-element.34), channel_id=1, source_target_pairs={{0,1},{1,2},{2,3},{3,0},{4,5},{5,6},{6,7},{7,4},{8,9},{9,10},{10,1... | collective-permute-start | bytes 626696 | tf_op jit(solution)/shard_map/ppermute | solution.py:238
  33.2 18.6 %collective-permute-start.4 = (s16[816,128]{1,0:T(8,128)(2,1)}, s16[816,128]{1,0:T(8,128)(2,1)}, u32[]{:S(2)}, u32[]{:S(2)}) collective-permute-start(s16[816,128]{1,0:T(8,128)(2,1)} %get-tuple-element.36), channel_id=1, source_target_pairs={{0,2},{1,3},{2,0},{3,1},{4,6},{5,7},{6,4},{7,5},{8,10},{9,11},{10,... | collective-permute-start | bytes 626696 | tf_op jit(solution)/shard_map/ppermute | solution.py:238
  34.9 18.0 %collective-permute-start.5 = (s16[816,128]{1,0:T(8,128)(2,1)}, s16[816,128]{1,0:T(8,128)(2,1)}, u32[]{:S(2)}, u32[]{:S(2)}) collective-permute-start(s16[816,128]{1,0:T(8,128)(2,1)} %get-tuple-element.38), channel_id=1, source_target_pairs={{0,3},{1,0},{2,1},{3,2},{4,7},{5,4},{6,5},{7,6},{8,11},{9,8},{10,9... | collective-permute-start | bytes 626696 | tf_op jit(solution)/shard_map/ppermute | solution.py:238
  41.5 11.4 %copy-start.6 = (s16[816,128]{1,0:T(8,128)(2,1)}, s16[816,128]{1,0:T(8,128)(2,1)S(1)}, u32[]{:S(2)}) copy-start(s16[816,128]{1,0:T(8,128)(2,1)S(1)} %collective-permute-done.3.refs_3_) | copy-start | bytes 626692
  56.3 10.7 %all-to-all-start = ((bf16[8,2,64,128]{3,2,1,0:T(8,128)(2,1)}), bf16[8,2,64,128]{3,2,1,0:T(8,128)(2,1)S(1)}, u32[]{:S(2)}, u32[]{:S(2)}) async-start(bf16[8,2,64,128]{3,2,1,0:T(8,128)(2,1)} %bitcast.69), calls=%async_computation | async-start | bytes 524288 | tf_op jit(solution)/shard_map/all_to_all | solution.py:285
  67.0 0.7 copy-start
  71.4 12.8 %collective-permute-start.10 = (bf16[12,64,128]{2,1,0:T(8,128)(2,1)}, bf16[12,64,128]{2,1,0:T(8,128)(2,1)S(1)}, u32[]{:S(2)}, u32[]{:S(2)}) collective-permute-start(bf16[12,64,128]{2,1,0:T(8,128)(2,1)} %pedigree.3.refs_2_), channel_id=1, source_target_pairs={{0,2},{1,3},{2,0},{3,1},{4,6},{5,7},{6,4},{7,5},{8,10},{9,11},{10,... | collective-permute-start | bytes 589832 | tf_op jit(solution)/shard_map/ppermute | solution.py:238
  73.8 23.7 %collective-permute-start.11 = (bf16[12,64,128]{2,1,0:T(8,128)(2,1)}, bf16[12,64,128]{2,1,0:T(8,128)(2,1)S(1)}, u32[]{:S(2)}, u32[]{:S(2)}) collective-permute-start(bf16[12,64,128]{2,1,0:T(8,128)(2,1)} %pedigree.3.refs_2_), channel_id=1, source_target_pairs={{0,3},{1,0},{2,1},{3,2},{4,7},{5,4},{6,5},{7,6},{8,11},{9,8},{10,9... | collective-permute-start | bytes 589832 | tf_op jit(solution)/shard_map/ppermute | solution.py:238
  73.8 23.7 %collective-permute-start.9 = (bf16[12,64,128]{2,1,0:T(8,128)(2,1)}, bf16[12,64,128]{2,1,0:T(8,128)(2,1)}, u32[]{:S(2)}, u32[]{:S(2)}) collective-permute-start(bf16[12,64,128]{2,1,0:T(8,128)(2,1)} %pedigree.3.refs_2_), channel_id=1, source_target_pairs={{0,1},{1,2},{2,3},{3,0},{4,5},{5,6},{6,7},{7,4},{8,9},{9,10},{10,1... | collective-permute-start | bytes 589832 | tf_op jit(solution)/shard_map/ppermute | solution.py:238
  79.6 32.1 %collective-permute-start.6 = (bf16[12,64,128]{2,1,0:T(8,128)(2,1)}, bf16[12,64,128]{2,1,0:T(8,128)(2,1)S(1)}, u32[]{:S(2)}, u32[]{:S(2)}) collective-permute-start(bf16[12,64,128]{2,1,0:T(8,128)(2,1)} %pedigree.2.refs_2_), channel_id=1, source_target_pairs={{0,1},{1,2},{2,3},{3,0},{4,5},{5,6},{6,7},{7,4},{8,9},{9,10},{10,1... | collective-permute-start | bytes 589832 | tf_op jit(solution)/shard_map/ppermute | solution.py:238
  79.6 32.1 %collective-permute-start.7 = (bf16[12,64,128]{2,1,0:T(8,128)(2,1)}, bf16[12,64,128]{2,1,0:T(8,128)(2,1)S(1)}, u32[]{:S(2)}, u32[]{:S(2)}) collective-permute-start(bf16[12,64,128]{2,1,0:T(8,128)(2,1)} %pedigree.2.refs_2_), channel_id=1, source_target_pairs={{0,2},{1,3},{2,0},{3,1},{4,6},{5,7},{6,4},{7,5},{8,10},{9,11},{10,... | collective-permute-start | bytes 589832 | tf_op jit(solution)/shard_map/ppermute | solution.py:238
  84.2 13.2 %copy-start.10 = (bf16[12,64,128]{2,1,0:T(8,128)(2,1)}, bf16[12,64,128]{2,1,0:T(8,128)(2,1)S(1)}, u32[]{:S(2)}) copy-start(bf16[12,64,128]{2,1,0:T(8,128)(2,1)S(1)} %collective-permute-done.10.refs_4_) | copy-start | bytes 589828
  84.2 27.5 %collective-permute-start.8 = (bf16[12,64,128]{2,1,0:T(8,128)(2,1)}, bf16[12,64,128]{2,1,0:T(8,128)(2,1)S(1)}, u32[]{:S(2)}, u32[]{:S(2)}) collective-permute-start(bf16[12,64,128]{2,1,0:T(8,128)(2,1)} %pedigree.2.refs_2_), channel_id=1, source_target_pairs={{0,3},{1,0},{2,1},{3,2},{4,7},{5,4},{6,5},{7,6},{8,11},{9,8},{10,9... | collective-permute-start | bytes 589832 | tf_op jit(solution)/shard_map/ppermute | solution.py:238
  97.4 0.7 copy-start.11
  111.7 0.7 copy-start.7
  111.7 0.7 copy-start.8
  111.7 0.8 copy-start.9
  126.7 2.3 %copy-start.1 = (bf16[6400,128]{1,0:T(8,128)(2,1)S(1)}, bf16[6400,128]{1,0:T(8,128)(2,1)}, u32[]{:S(2)}) copy-start(bf16[6400,128]{1,0:T(8,128)(2,1)} %get-tuple-element.44) | copy-start | bytes 4915204
  126.7 4.9 %copy-start.2 = (bf16[6400,128]{1,0:T(8,128)(2,1)S(1)}, bf16[6400,128]{1,0:T(8,128)(2,1)}, u32[]{:S(2)}) copy-start(bf16[6400,128]{1,0:T(8,128)(2,1)} %get-tuple-element.43) | copy-start | bytes 4915204
  129.0 2.7 %collective-permute-start.12 = (bf16[2,2,800,128]{3,2,1,0:T(8,128)(2,1)}, bf16[2,2,800,128]{3,2,1,0:T(8,128)(2,1)}, u32[]{:S(2)}, u32[]{:S(2)}) collective-permute-start(bf16[2,2,800,128]{3,2,1,0:T(8,128)(2,1)} %dynamic-slice_bitcast_fusion.1), channel_id=1, source_target_pairs={{0,4},{4,0},{8,12},{12,8},{16,20},{20,16},{24,28},{28,24},{1,5},{5... | collective-permute-start | bytes 2457608 | tf_op jit(solution)/shard_map/ppermute | solution.py:254
  129.9 4.7 %collective-permute-start.15 = (bf16[2,2,800,128]{3,2,1,0:T(8,128)(2,1)}, bf16[2,2,800,128]{3,2,1,0:T(8,128)(2,1)}, u32[]{:S(2)}, u32[]{:S(2)}) collective-permute-start(bf16[2,2,800,128]{3,2,1,0:T(8,128)(2,1)} %dynamic-slice_bitcast_fusion), channel_id=1, source_target_pairs={{0,4},{4,0},{8,12},{12,8},{16,20},{20,16},{24,28},{28,24},{1,5},{5... | collective-permute-start | bytes 2457608 | tf_op jit(solution)/shard_map/ppermute | solution.py:254
  133.5 11.8 %collective-permute-start.13 = (bf16[2,800,128]{2,1,0:T(8,128)(2,1)}, bf16[2,800,128]{2,1,0:T(8,128)(2,1)}, u32[]{:S(2)}, u32[]{:S(2)}) collective-permute-start(bf16[2,800,128]{2,1,0:T(8,128)(2,1)} %fusion.1), channel_id=1, source_target_pairs={{0,8},{4,12},{8,0},{12,4},{16,24},{20,28},{24,16},{28,20},{1,9},{5... | collective-permute-start | bytes 1228808 | tf_op jit(solution)/shard_map/ppermute | solution.py:254
  136.5 12.0 %collective-permute-start.16 = (bf16[2,800,128]{2,1,0:T(8,128)(2,1)}, bf16[2,800,128]{2,1,0:T(8,128)(2,1)}, u32[]{:S(2)}, u32[]{:S(2)}) collective-permute-start(bf16[2,800,128]{2,1,0:T(8,128)(2,1)} %fusion), channel_id=1, source_target_pairs={{0,16},{4,20},{8,24},{12,28},{16,0},{20,4},{24,8},{28,12},{1,17},{... | collective-permute-start | bytes 1228808 | tf_op jit(solution)/shard_map/ppermute | solution.py:254
  147.2 6.5 %collective-permute-start.14 = (bf16[800,128]{1,0:T(8,128)(2,1)}, bf16[800,128]{1,0:T(8,128)(2,1)S(1)}, u32[]{:S(2)}, u32[]{:S(2)}) collective-permute-start(bf16[800,128]{1,0:T(8,128)(2,1)} %fusion.4), channel_id=1, source_target_pairs={{0,16},{4,20},{8,24},{12,28},{16,0},{20,4},{24,8},{28,12},{1,17},{... | collective-permute-start | bytes 614408 | tf_op jit(solution)/shard_map/ppermute | solution.py:254
  149.6 6.1 %collective-permute-start.17 = (bf16[800,128]{1,0:T(8,128)(2,1)S(1)}, bf16[800,128]{1,0:T(8,128)(2,1)S(1)}, u32[]{:S(2)}, u32[]{:S(2)}) collective-permute-start(bf16[800,128]{1,0:T(8,128)(2,1)S(1)} %fusion.2), channel_id=1, source_target_pairs={{0,8},{4,12},{8,0},{12,4},{16,24},{20,28},{24,16},{28,20},{1,9},{5... | collective-permute-start | bytes 614408 | tf_op jit(solution)/shard_map/ppermute | solution.py:254

commit v8 on v7

--- a/solution.py
+++ b/solution.py
@@ -273,7 +273,8 @@
         )
         owns.append(own)
         if part > 0:
-            sent, earlier = lax.optimization_barrier((sent, [one[-1] for one in coded]))
+            later, earlier = lax.optimization_barrier((sent[1:], [one[-1] for one in coded]))
+            sent = [sent[0], *later]
             for one, value in zip(coded, earlier):
                 one[-1] = value
         for shift in range(1, devices):

time: 160 us -> 158 us (0.988)
  transfers between devices with their start and end apart: 19 -> 19, of which waited for: 12 -> 12; matrix products, arithmetic and copies ran while one was open for 7% -> 7% of each run, Pallas kernels for 18% -> 19%
where the time goes in v8:
time: 158 us; the launch traced here: 157 us
  Pallas kernels  62.2 us (39%)
  waiting for transfers between devices  54.2 us (34%)
  starting transfers between devices  21.9 us (14%)
  other arithmetic  11 us (7%)
  local copies, waits for them, and re-layouts  7.52 us (5%)
    ppermute x12, waiting for transfers between devices, turn(): lax.ppermute(value, 'marker', [(d, (d + shift) % devices) for d in range(...  34.8 us
    pallas_call x2, Pallas kernels, backward_product(): pl.pallas_call(functools.partial(backward_kernel, scale, devices, lanes),...  27.8 us
    pallas_call x2, Pallas kernels, forward_product(): pl.pallas_call(functools.partial(forward_kernel, scale, devices), grid_sp...  23.6 us
    ppermute x12, starting transfers between devices, turn(): lax.ppermute(value, 'marker', [(d, (d + shift) % devices) for d in range(...  13.6 us
    ppermute x6, waiting for transfers between devices, halving_sum(): lax.ppermute(sent, 'animal', [(d, d ^ 1 << bit) for d in range(devices)])  13.2 us
    pallas_call x2, Pallas kernels, pedigree(): pl.pallas_call(functools.partial(pedigree_kernel, group, block_total, sta...  7.52 us
    convert_element_type x4, other arithmetic, halving_sum(): sent = sum((term.astype(jnp.float32) for term in sent)).astype(jnp.bfloat16)  6.66 us
    all_to_all x1, waiting for transfers between devices, local(): lax.all_to_all(outgoing, 'animal', split_axis=0, concat_axis=0, tiled=True)  6.25 us
  transfers between devices with their start and end apart: 19, of which 12 were waited for; matrix products, arithmetic and copies ran while one was open for 7% of the time, Pallas kernels for 19%

profile of v8, /device:TPU:8, one launch (start us, length us, event | category | flops | bytes accessed | tf_op | source)
XLA Modules:
  0.0 157.0 jit_solution(17132258636361758377)
XLA Ops:
  0.0 11.8 %forward_product.2 = (f32[12,64,128]{2,1,0:T(8,128)}, s16[816,128]{1,0:T(8,128)(2,1)}, s16[816,128]{1,0:T(8,128)(2,1)}, s16[816,128]{1,0:T(8,128)(2,1)}) custom-call(s32[1]{0:T(128)} %bitcast.place_ref, bf16[3072,6400]{1,0:T(8,128)(2,1)} %refs_1_.3, bf16[3072,6400]{1,0:T(8,128)(2,1)} %refs_1_.3, bf16[6400,256]{1,0:T(8,128)(2,1)} %direction_ref.3), custom_call_target="tpu_custom_call" | custom-call | flops 5033164800 | bytes 23724032 | tf_op jit(solution)/shard_map/forward_product/pallas_call | solution.py:60
  11.8 1.6 %collective-permute-start = (s16[816,128]{1,0:T(8,128)(2,1)}, s16[816,128]{1,0:T(8,128)(2,1)S(1)}, u32[]{:S(2)}, u32[]{:S(2)}) collective-permute-start(s16[816,128]{1,0:T(8,128)(2,1)} %get-tuple-element.28), channel_id=1, source_target_pairs={{0,1},{1,2},{2,3},{3,0},{4,5},{5,6},{6,7},{7,4},{8,9},{9,10},{10,1... | collective-permute-start | bytes 626696 | tf_op jit(solution)/shard_map/ppermute | solution.py:238
  13.4 1.1 collective-permute-start.1
  14.5 1.9 %collective-permute-start.2 = (s16[816,128]{1,0:T(8,128)(2,1)}, s16[816,128]{1,0:T(8,128)(2,1)S(1)}, u32[]{:S(2)}, u32[]{:S(2)}) collective-permute-start(s16[816,128]{1,0:T(8,128)(2,1)} %get-tuple-element.30), channel_id=1, source_target_pairs={{0,3},{1,0},{2,1},{3,2},{4,7},{5,4},{6,5},{7,6},{8,11},{9,8},{10,9... | collective-permute-start | bytes 626696 | tf_op jit(solution)/shard_map/ppermute | solution.py:238
  16.4 11.8 %forward_product.3 = (f32[12,64,128]{2,1,0:T(8,128)}, s16[816,128]{1,0:T(8,128)(2,1)}, s16[816,128]{1,0:T(8,128)(2,1)}, s16[816,128]{1,0:T(8,128)(2,1)}) custom-call(s32[1]{0:T(128)} %bitcast.place_ref, bf16[3072,6400]{1,0:T(8,128)(2,1)} %refs_1_.3, bf16[3072,6400]{1,0:T(8,128)(2,1)} %refs_1_.3, bf16[6400,256]{1,0:T(8,128)(2,1)} %direction_ref.3), custom_call_target="tpu_custom_call" | custom-call | flops 5033164800 | bytes 23724032 | tf_op jit(solution)/shard_map/forward_product/pallas_call | solution.py:60
  28.2 0.1 collective-permute-start.3
  28.3 0.0 collective-permute-done.refs_2_
  28.3 4.4 %collective-permute-done.1.refs_4_ = s16[816,128]{1,0:T(8,128)(2,1)S(1)} collective-permute-done((s16[816,128]{1,0:T(8,128)(2,1)}, s16[816,128]{1,0:T(8,128)(2,1)S(1)}, u32[]{:S(2)}, u32[]{:S(2)}) %collective-permute-start.1) | collective-permute-done | bytes 208928 | tf_op jit(solution)/shard_map/ppermute | solution.py:238
  32.7 5.0 %collective-permute-done.2.refs_6_ = s16[816,128]{1,0:T(8,128)(2,1)S(1)} collective-permute-done((s16[816,128]{1,0:T(8,128)(2,1)}, s16[816,128]{1,0:T(8,128)(2,1)S(1)}, u32[]{:S(2)}, u32[]{:S(2)}) %collective-permute-start.2) | collective-permute-done | bytes 208928 | tf_op jit(solution)/shard_map/ppermute | solution.py:238
  37.7 0.0 collective-permute-start.4
  37.7 1.1 collective-permute-start.5
  38.8 0.1 copy.12
  38.9 0.6 reshape.70.list_ref
  39.5 0.0 collective-permute-done.3.refs_3_
  39.5 12.3 %collective-permute-done.4.refs_5_ = s16[816,128]{1,0:T(8,128)(2,1)} collective-permute-done((s16[816,128]{1,0:T(8,128)(2,1)}, s16[816,128]{1,0:T(8,128)(2,1)}, u32[]{:S(2)}, u32[]{:S(2)}) %collective-permute-start.4) | collective-permute-done | bytes 208928 | tf_op jit(solution)/shard_map/ppermute | solution.py:238
  51.9 0.1 collective-permute-done.5.refs_7_
  52.0 3.4 %settle.1 = (bf16[24,64,128]{2,1,0:T(8,128)(2,1)}, bf16[16,64,128]{2,1,0:T(8,128)(2,1)}) custom-call(s32[16]{0:T(128)} %reshape.70.list_ref, f32[12,64,128]{2,1,0:T(8,128)} %get-tuple-element.24.refs_0_, f32[12,64,128]{2,1,0:T(8,128)} %get-tuple-element.25.refs_1_, s16[816,128]{1,0:T(8,128)(2,1)} %copy-done.3, s16[816,128]{1,0:T(8,128)(2,1)} %copy-done.6, ...), custom_call_target="tpu_custom_call" | custom-call | tf_op jit(solution)/shard_map/settle/pallas_call | solution.py:110
  55.4 3.7 %all-to-all-start = ((bf16[8,2,64,128]{3,2,1,0:T(8,128)(2,1)}), bf16[8,2,64,128]{3,2,1,0:T(8,128)(2,1)S(1)}, u32[]{:S(2)}, u32[]{:S(2)}) async-start(bf16[8,2,64,128]{3,2,1,0:T(8,128)(2,1)} %bitcast.69), calls=%async_computation | async-start | bytes 524288 | tf_op jit(solution)/shard_map/all_to_all | solution.py:286
  59.1 0.7 copy.13.index_ref
  59.8 6.3 %all-to-all-done = bf16[8,2,64,128]{3,2,1,0:T(8,128)(2,1)S(1)} async-done(((bf16[8,2,64,128]{3,2,1,0:T(8,128)(2,1)}), bf16[8,2,64,128]{3,2,1,0:T(8,128)(2,1)S(1)}, u32[]{:S(2)}, u32[]{:S(2)}) %all-to-all-start) | async-done | bytes 262176 | tf_op jit(solution)/shard_map/all_to_all | solution.py:286
  66.0 0.7 copy-done
  66.7 3.8 %pedigree.3.refs_2_ = bf16[12,64,128]{2,1,0:T(8,128)(2,1)} custom-call(s32[24,4]{1,0:T(8,128)} %copy.13.index_ref, s32[24]{0:T(128)} %count_ref.3, bf16[24,64,128]{2,1,0:T(8,128)(2,1)} %get-tuple-element.37.own_ref, bf16[16,64,128]{2,1,0:T(8,128)(2,1)} %bitcast.59, bf16[24,4,128,128]{3,2,1,0:T(8,128)(2,1)} %prec_ref.3), custom_call_target="tpu_custom_call" | custom-call | tf_op jit(solution)/shard_map/pedigree/pallas_call | solution.py:157
  70.5 3.3 %collective-permute-start.10 = (bf16[12,64,128]{2,1,0:T(8,128)(2,1)}, bf16[12,64,128]{2,1,0:T(8,128)(2,1)S(1)}, u32[]{:S(2)}, u32[]{:S(2)}) collective-permute-start(bf16[12,64,128]{2,1,0:T(8,128)(2,1)} %pedigree.3.refs_2_), channel_id=1, source_target_pairs={{0,2},{1,3},{2,0},{3,1},{4,6},{5,7},{6,4},{7,5},{8,10},{9,11},{10,... | collective-permute-start | bytes 589832 | tf_op jit(solution)/shard_map/ppermute | solution.py:238
  73.8 0.0 collective-permute-start.11
  73.8 2.0 %collective-permute-start.9 = (bf16[12,64,128]{2,1,0:T(8,128)(2,1)}, bf16[12,64,128]{2,1,0:T(8,128)(2,1)}, u32[]{:S(2)}, u32[]{:S(2)}) collective-permute-start(bf16[12,64,128]{2,1,0:T(8,128)(2,1)} %pedigree.3.refs_2_), channel_id=1, source_target_pairs={{0,1},{1,2},{2,3},{3,0},{4,5},{5,6},{6,7},{7,4},{8,9},{9,10},{10,1... | collective-permute-start | bytes 589832 | tf_op jit(solution)/shard_map/ppermute | solution.py:238
  75.8 3.8 %pedigree.2.refs_2_ = bf16[12,64,128]{2,1,0:T(8,128)(2,1)} custom-call(s32[24,4]{1,0:T(8,128)} %copy.13.index_ref, s32[24]{0:T(128)} %count_ref.3, bf16[24,64,128]{2,1,0:T(8,128)(2,1)} %get-tuple-element.37.own_ref, bf16[16,64,128]{2,1,0:T(8,128)(2,1)} %bitcast.60, bf16[24,4,128,128]{3,2,1,0:T(8,128)(2,1)} %prec_ref.3), custom_call_target="tpu_custom_call" | custom-call | tf_op jit(solution)/shard_map/pedigree/pallas_call | solution.py:157
  79.6 0.0 collective-permute-start.6
  79.6 2.4 %collective-permute-start.7 = (bf16[12,64,128]{2,1,0:T(8,128)(2,1)}, bf16[12,64,128]{2,1,0:T(8,128)(2,1)S(1)}, u32[]{:S(2)}, u32[]{:S(2)}) collective-permute-start(bf16[12,64,128]{2,1,0:T(8,128)(2,1)} %pedigree.2.refs_2_), channel_id=1, source_target_pairs={{0,2},{1,3},{2,0},{3,1},{4,6},{5,7},{6,4},{7,5},{8,10},{9,11},{10,... | collective-permute-start | bytes 589832 | tf_op jit(solution)/shard_map/ppermute | solution.py:238
  81.9 1.4 collective-permute-done.10.refs_4_
  83.3 0.1 collective-permute-start.8
  83.4 11.6 %collective-permute-done.11.refs_5_ = bf16[12,64,128]{2,1,0:T(8,128)(2,1)S(1)} collective-permute-done((bf16[12,64,128]{2,1,0:T(8,128)(2,1)}, bf16[12,64,128]{2,1,0:T(8,128)(2,1)S(1)}, u32[]{:S(2)}, u32[]{:S(2)}) %collective-permute-start.11) | collective-permute-done | bytes 196640 | tf_op jit(solution)/shard_map/ppermute | solution.py:238
  95.0 0.0 collective-permute-done.9.refs_3_
  95.0 0.7 copy-done.11
  95.7 13.6 %backward_product.2 = (f32[6400,128]{1,0:T(8,128)}, f32[6400,128]{1,0:T(8,128)}) custom-call(s32[1]{0:T(128)} %bitcast.place_ref, bf16[3072,6400]{1,0:T(8,128)(2,1)} %refs_1_.3, bf16[3072,6400]{1,0:T(8,128)(2,1)} %refs_1_.3, bf16[12,64,128]{2,1,0:T(8,128)(2,1)} %pedigree.3.refs_2_, bf16[12,64,128]{2,1,0:T(8,128)(2,1)} %collective-permute-done.9.refs_3_, ...), custom_call_target="tpu_custom_call" | custom-call | flops 5033164800 | bytes 27000832 | tf_op jit(solution)/shard_map/backward_product/pallas_call | solution.py:215
  109.2 0.0 collective-permute-done.6.refs_3_
  109.3 0.0 copy-start.7
  109.3 0.0 collective-permute-done.7.refs_4_
  109.3 0.0 collective-permute-done.8.refs_5_
  109.3 0.6 copy-done.7
  109.9 0.1 copy-done.8
  110.0 0.1 copy-done.9
  110.1 14.2 %backward_product.3 = (bf16[6400,128]{1,0:T(8,128)(2,1)}, bf16[6400,128]{1,0:T(8,128)(2,1)}) custom-call(s32[1]{0:T(128)} %bitcast.place_ref, bf16[3072,6400]{1,0:T(8,128)(2,1)} %refs_1_.3, bf16[3072,6400]{1,0:T(8,128)(2,1)} %refs_1_.3, bf16[12,64,128]{2,1,0:T(8,128)(2,1)} %pedigree.2.refs_2_, bf16[12,64,128]{2,1,0:T(8,128)(2,1)} %copy-done.7, ...), custom_call_target="tpu_custom_call" | custom-call | flops 5033164800 | bytes 33554432 | tf_op jit(solution)/shard_map/backward_product/pallas_call | solution.py:215
  124.3 2.3 %dynamic-slice_bitcast_fusion.1 = bf16[2,2,800,128]{3,2,1,0:T(8,128)(2,1)} fusion(bf16[2,2,2,800,128]{4,3,2,1,0:T(8,128)(2,1)} %bitcast.65, s32[]{:T(128)S(6)} %select_n.60), kind=kLoop, calls=%fused_computation.6 | loop fusion | bytes 1638404 | tf_op jit(solution)/shard_map/jit(dynamic_index_in_dim)/squeeze | solution.py:250
  126.5 0.0 collective-permute-start.12
  126.5 0.9 dynamic-slice_bitcast_fusion
  127.5 0.5 collective-permute-start.15
  128.0 1.2 collective-permute-done.12
  129.2 1.9 %fusion.1 = bf16[2,800,128]{2,1,0:T(8,128)(2,1)} fusion(bf16[2,2,800,128]{3,2,1,0:T(8,128)(2,1)} %collective-permute-done.12, s32[]{:T(128)S(6)} %select_n.61, bf16[2,2,2,800,128]{4,3,2,1,0:T(8,128)(2,1)S(1)} %bitcast.66, s32[]{:T(128)S(6)} %select_n.62, s32[]{:T(128)S(6)} %select_n.59), kind=kLoop, calls=%fused_computation.4 | loop fusion | flops 819200 | bytes 1228812 | tf_op jit(solution)/shard_map/convert_element_type | solution.py:253
  131.1 2.1 %collective-permute-start.13 = (bf16[2,800,128]{2,1,0:T(8,128)(2,1)}, bf16[2,800,128]{2,1,0:T(8,128)(2,1)}, u32[]{:S(2)}, u32[]{:S(2)}) collective-permute-start(bf16[2,800,128]{2,1,0:T(8,128)(2,1)} %fusion.1), channel_id=1, source_target_pairs={{0,8},{4,12},{8,0},{12,4},{16,24},{20,28},{24,16},{28,20},{1,9},{5... | collective-permute-start | bytes 1228808 | tf_op jit(solution)/shard_map/ppermute | solution.py:254
  133.2 0.0 collective-permute-done.15
  133.2 1.9 %fusion = bf16[2,800,128]{2,1,0:T(8,128)(2,1)} fusion(bf16[2,2,800,128]{3,2,1,0:T(8,128)(2,1)} %collective-permute-done.15, s32[]{:T(128)S(6)} %select_n.63, bf16[2,2,2,800,128]{4,3,2,1,0:T(8,128)(2,1)S(1)} %bitcast.62, s32[]{:T(128)S(6)} %select_n.64, s32[]{:T(128)S(6)} %select_n.59), kind=kLoop, calls=%fused_computation.2 | loop fusion | flops 819200 | bytes 1228812 | tf_op jit(solution)/shard_map/convert_element_type | solution.py:253
  135.0 0.3 collective-permute-start.16
  135.3 7.9 %collective-permute-done.13 = bf16[2,800,128]{2,1,0:T(8,128)(2,1)} collective-permute-done((bf16[2,800,128]{2,1,0:T(8,128)(2,1)}, bf16[2,800,128]{2,1,0:T(8,128)(2,1)}, u32[]{:S(2)}, u32[]{:S(2)}) %collective-permute-start.13) | collective-permute-done | bytes 409632 | tf_op jit(solution)/shard_map/ppermute | solution.py:254
  143.3 1.8 %fusion.4 = bf16[800,128]{1,0:T(8,128)(2,1)} fusion(bf16[2,800,128]{2,1,0:T(8,128)(2,1)} %collective-permute-done.13, s32[]{:T(128)S(6)} %select_n.63, bf16[2,2,800,128]{3,2,1,0:T(8,128)(2,1)} %collective-permute-done.12, s32[]{:T(128)S(6)} %select_n.64, s32[]{:T(128)S(6)} %select_n.57, bf16[2,2,2,800,128]{4,3,2,1,0:T(8,128)(2,1)S(1)} %bitcast.67, ...), kind=kLoop, calls=%fused_computation.14 | loop fusion | flops 614400 | bytes 819216 | tf_op jit(solution)/shard_map/convert_element_type | solution.py:253
  145.1 0.3 collective-permute-start.14
  145.4 0.8 dynamic_slice.88
  146.2 0.5 collective-permute-done.16
  146.6 1.1 fusion.2
  147.7 1.4 collective-permute-start.17
  149.1 2.8 %collective-permute-done.14 = bf16[800,128]{1,0:T(8,128)(2,1)S(1)} collective-permute-done((bf16[800,128]{1,0:T(8,128)(2,1)}, bf16[800,128]{1,0:T(8,128)(2,1)S(1)}, u32[]{:S(2)}, u32[]{:S(2)}) %collective-permute-start.14) | collective-permute-done | bytes 204832 | tf_op jit(solution)/shard_map/ppermute | solution.py:254
  151.9 1.1 fusion.5
  153.0 0.8 collective-permute-done.17
  153.8 1.1 fusion.3
  154.9 2.1 %maximum_add_fusion = f32[800,256]{1,0:T(8,128)} fusion(f32[800,128]{1,0:T(8,128)S(1)} %fusion.3, f32[800,128]{1,0:T(8,128)S(1)} %fusion.5, bf16[6400,256]{1,0:T(8,128)(2,1)} %direction_ref.3, s32[]{:T(128)S(6)} %select_n.65, f32[800]{0:T(1024)S(1)} %dynamic_slice.88), kind=kLoop, calls=%fused_computation | loop fusion | flops 819200 | bytes 2051204 | tf_op jit(solution)/shard_map/add | solution.py:311
  (22 shorter events, 0.0 us)
Async XLA Ops:
  11.8 16.5 %collective-permute-start = (s16[816,128]{1,0:T(8,128)(2,1)}, s16[816,128]{1,0:T(8,128)(2,1)S(1)}, u32[]{:S(2)}, u32[]{:S(2)}) collective-permute-start(s16[816,128]{1,0:T(8,128)(2,1)} %get-tuple-element.28), channel_id=1, source_target_pairs={{0,1},{1,2},{2,3},{3,0},{4,5},{5,6},{6,7},{7,4},{8,9},{9,10},{10,1... | collective-permute-start | bytes 626696 | tf_op jit(solution)/shard_map/ppermute | solution.py:238
  13.4 19.4 %collective-permute-start.1 = (s16[816,128]{1,0:T(8,128)(2,1)}, s16[816,128]{1,0:T(8,128)(2,1)S(1)}, u32[]{:S(2)}, u32[]{:S(2)}) collective-permute-start(s16[816,128]{1,0:T(8,128)(2,1)} %get-tuple-element.29), channel_id=1, source_target_pairs={{0,2},{1,3},{2,0},{3,1},{4,6},{5,7},{6,4},{7,5},{8,10},{9,11},{10,... | collective-permute-start | bytes 626696 | tf_op jit(solution)/shard_map/ppermute | solution.py:238
  14.5 24.4 %copy-start.13 = (s32[1,8,2]{1,2,0:T(2,128)S(1)}, s32[1,8,2]{1,2,0:T(2,128)}, u32[]{:S(2)}) copy-start(s32[1,8,2]{1,2,0:T(2,128)} %param.10) | copy-start | bytes 196
  14.5 23.2 %collective-permute-start.2 = (s16[816,128]{1,0:T(8,128)(2,1)}, s16[816,128]{1,0:T(8,128)(2,1)S(1)}, u32[]{:S(2)}, u32[]{:S(2)}) collective-permute-start(s16[816,128]{1,0:T(8,128)(2,1)} %get-tuple-element.30), channel_id=1, source_target_pairs={{0,3},{1,0},{2,1},{3,2},{4,7},{5,4},{6,5},{7,6},{8,11},{9,8},{10,9... | collective-permute-start | bytes 626696 | tf_op jit(solution)/shard_map/ppermute | solution.py:238
  28.2 30.9 %copy-start.12 = (s32[24,4]{0,1:T(4,128)S(1)}, s32[24,4]{0,1:T(4,128)}, u32[]{:S(2)}) copy-start(s32[24,4]{0,1:T(4,128)} %param.11) | copy-start | bytes 1156
  28.2 11.3 %collective-permute-start.3 = (s16[816,128]{1,0:T(8,128)(2,1)}, s16[816,128]{1,0:T(8,128)(2,1)S(1)}, u32[]{:S(2)}, u32[]{:S(2)}) collective-permute-start(s16[816,128]{1,0:T(8,128)(2,1)} %get-tuple-element.32), channel_id=1, source_target_pairs={{0,1},{1,2},{2,3},{3,0},{4,5},{5,6},{6,7},{7,4},{8,9},{9,10},{10,1... | collective-permute-start | bytes 626696 | tf_op jit(solution)/shard_map/ppermute | solution.py:238
  28.3 23.7 %copy-start.3 = (s16[816,128]{1,0:T(8,128)(2,1)}, s16[816,128]{1,0:T(8,128)(2,1)S(1)}, u32[]{:S(2)}) copy-start(s16[816,128]{1,0:T(8,128)(2,1)S(1)} %collective-permute-done.refs_2_) | copy-start | bytes 626692
  32.7 19.3 %copy-start.4 = (s16[816,128]{1,0:T(8,128)(2,1)}, s16[816,128]{1,0:T(8,128)(2,1)S(1)}, u32[]{:S(2)}) copy-start(s16[816,128]{1,0:T(8,128)(2,1)S(1)} %collective-permute-done.1.refs_4_) | copy-start | bytes 626692
  37.7 14.3 %copy-start.5 = (s16[816,128]{1,0:T(8,128)(2,1)}, s16[816,128]{1,0:T(8,128)(2,1)S(1)}, u32[]{:S(2)}) copy-start(s16[816,128]{1,0:T(8,128)(2,1)S(1)} %collective-permute-done.2.refs_6_) | copy-start | bytes 626692
  37.7 14.2 %collective-permute-start.4 = (s16[816,128]{1,0:T(8,128)(2,1)}, s16[816,128]{1,0:T(8,128)(2,1)}, u32[]{:S(2)}, u32[]{:S(2)}) collective-permute-start(s16[816,128]{1,0:T(8,128)(2,1)} %get-tuple-element.34), channel_id=1, source_target_pairs={{0,2},{1,3},{2,0},{3,1},{4,6},{5,7},{6,4},{7,5},{8,10},{9,11},{10,... | collective-permute-start | bytes 626696 | tf_op jit(solution)/shard_map/ppermute | solution.py:238
  37.7 14.3 %collective-permute-start.5 = (s16[816,128]{1,0:T(8,128)(2,1)}, s16[816,128]{1,0:T(8,128)(2,1)}, u32[]{:S(2)}, u32[]{:S(2)}) collective-permute-start(s16[816,128]{1,0:T(8,128)(2,1)} %get-tuple-element.36), channel_id=1, source_target_pairs={{0,3},{1,0},{2,1},{3,2},{4,7},{5,4},{6,5},{7,6},{8,11},{9,8},{10,9... | collective-permute-start | bytes 626696 | tf_op jit(solution)/shard_map/ppermute | solution.py:238
  39.5 12.5 %copy-start.6 = (s16[816,128]{1,0:T(8,128)(2,1)}, s16[816,128]{1,0:T(8,128)(2,1)S(1)}, u32[]{:S(2)}) copy-start(s16[816,128]{1,0:T(8,128)(2,1)S(1)} %collective-permute-done.3.refs_3_) | copy-start | bytes 626692
  55.4 10.6 %all-to-all-start = ((bf16[8,2,64,128]{3,2,1,0:T(8,128)(2,1)}), bf16[8,2,64,128]{3,2,1,0:T(8,128)(2,1)S(1)}, u32[]{:S(2)}, u32[]{:S(2)}) async-start(bf16[8,2,64,128]{3,2,1,0:T(8,128)(2,1)} %bitcast.69), calls=%async_computation | async-start | bytes 524288 | tf_op jit(solution)/shard_map/all_to_all | solution.py:286
  66.0 0.7 copy-start
  70.5 12.8 %collective-permute-start.10 = (bf16[12,64,128]{2,1,0:T(8,128)(2,1)}, bf16[12,64,128]{2,1,0:T(8,128)(2,1)S(1)}, u32[]{:S(2)}, u32[]{:S(2)}) collective-permute-start(bf16[12,64,128]{2,1,0:T(8,128)(2,1)} %pedigree.3.refs_2_), channel_id=1, source_target_pairs={{0,2},{1,3},{2,0},{3,1},{4,6},{5,7},{6,4},{7,5},{8,10},{9,11},{10,... | collective-permute-start | bytes 589832 | tf_op jit(solution)/shard_map/ppermute | solution.py:238
  73.8 21.2 %collective-permute-start.11 = (bf16[12,64,128]{2,1,0:T(8,128)(2,1)}, bf16[12,64,128]{2,1,0:T(8,128)(2,1)S(1)}, u32[]{:S(2)}, u32[]{:S(2)}) collective-permute-start(bf16[12,64,128]{2,1,0:T(8,128)(2,1)} %pedigree.3.refs_2_), channel_id=1, source_target_pairs={{0,3},{1,0},{2,1},{3,2},{4,7},{5,4},{6,5},{7,6},{8,11},{9,8},{10,9... | collective-permute-start | bytes 589832 | tf_op jit(solution)/shard_map/ppermute | solution.py:238
  73.8 21.2 %collective-permute-start.9 = (bf16[12,64,128]{2,1,0:T(8,128)(2,1)}, bf16[12,64,128]{2,1,0:T(8,128)(2,1)}, u32[]{:S(2)}, u32[]{:S(2)}) collective-permute-start(bf16[12,64,128]{2,1,0:T(8,128)(2,1)} %pedigree.3.refs_2_), channel_id=1, source_target_pairs={{0,1},{1,2},{2,3},{3,0},{4,5},{5,6},{6,7},{7,4},{8,9},{9,10},{10,1... | collective-permute-start | bytes 589832 | tf_op jit(solution)/shard_map/ppermute | solution.py:238
  79.6 29.7 %collective-permute-start.6 = (bf16[12,64,128]{2,1,0:T(8,128)(2,1)}, bf16[12,64,128]{2,1,0:T(8,128)(2,1)S(1)}, u32[]{:S(2)}, u32[]{:S(2)}) collective-permute-start(bf16[12,64,128]{2,1,0:T(8,128)(2,1)} %pedigree.2.refs_2_), channel_id=1, source_target_pairs={{0,1},{1,2},{2,3},{3,0},{4,5},{5,6},{6,7},{7,4},{8,9},{9,10},{10,1... | collective-permute-start | bytes 589832 | tf_op jit(solution)/shard_map/ppermute | solution.py:238
  79.6 29.7 %collective-permute-start.7 = (bf16[12,64,128]{2,1,0:T(8,128)(2,1)}, bf16[12,64,128]{2,1,0:T(8,128)(2,1)S(1)}, u32[]{:S(2)}, u32[]{:S(2)}) collective-permute-start(bf16[12,64,128]{2,1,0:T(8,128)(2,1)} %pedigree.2.refs_2_), channel_id=1, source_target_pairs={{0,2},{1,3},{2,0},{3,1},{4,6},{5,7},{6,4},{7,5},{8,10},{9,11},{10,... | collective-permute-start | bytes 589832 | tf_op jit(solution)/shard_map/ppermute | solution.py:238
  83.3 11.7 %copy-start.10 = (bf16[12,64,128]{2,1,0:T(8,128)(2,1)}, bf16[12,64,128]{2,1,0:T(8,128)(2,1)S(1)}, u32[]{:S(2)}) copy-start(bf16[12,64,128]{2,1,0:T(8,128)(2,1)S(1)} %collective-permute-done.10.refs_4_) | copy-start | bytes 589828
  83.3 26.0 %collective-permute-start.8 = (bf16[12,64,128]{2,1,0:T(8,128)(2,1)}, bf16[12,64,128]{2,1,0:T(8,128)(2,1)S(1)}, u32[]{:S(2)}, u32[]{:S(2)}) collective-permute-start(bf16[12,64,128]{2,1,0:T(8,128)(2,1)} %pedigree.2.refs_2_), channel_id=1, source_target_pairs={{0,3},{1,0},{2,1},{3,2},{4,7},{5,4},{6,5},{7,6},{8,11},{9,8},{10,9... | collective-permute-start | bytes 589832 | tf_op jit(solution)/shard_map/ppermute | solution.py:238
  95.0 0.7 copy-start.11
  109.3 0.7 copy-start.7
  109.3 0.7 copy-start.8
  109.3 0.8 copy-start.9
  124.3 2.3 %copy-start.1 = (bf16[6400,128]{1,0:T(8,128)(2,1)S(1)}, bf16[6400,128]{1,0:T(8,128)(2,1)}, u32[]{:S(2)}) copy-start(bf16[6400,128]{1,0:T(8,128)(2,1)} %get-tuple-element.42) | copy-start | bytes 4915204
  124.3 4.9 %copy-start.2 = (bf16[6400,128]{1,0:T(8,128)(2,1)S(1)}, bf16[6400,128]{1,0:T(8,128)(2,1)}, u32[]{:S(2)}) copy-start(bf16[6400,128]{1,0:T(8,128)(2,1)} %get-tuple-element.41) | copy-start | bytes 4915204
  126.5 2.7 %collective-permute-start.12 = (bf16[2,2,800,128]{3,2,1,0:T(8,128)(2,1)}, bf16[2,2,800,128]{3,2,1,0:T(8,128)(2,1)}, u32[]{:S(2)}, u32[]{:S(2)}) collective-permute-start(bf16[2,2,800,128]{3,2,1,0:T(8,128)(2,1)} %dynamic-slice_bitcast_fusion.1), channel_id=1, source_target_pairs={{0,4},{4,0},{8,12},{12,8},{16,20},{20,16},{24,28},{28,24},{1,5},{5... | collective-permute-start | bytes 2457608 | tf_op jit(solution)/shard_map/ppermute | solution.py:254
  127.5 5.7 %collective-permute-start.15 = (bf16[2,2,800,128]{3,2,1,0:T(8,128)(2,1)}, bf16[2,2,800,128]{3,2,1,0:T(8,128)(2,1)}, u32[]{:S(2)}, u32[]{:S(2)}) collective-permute-start(bf16[2,2,800,128]{3,2,1,0:T(8,128)(2,1)} %dynamic-slice_bitcast_fusion), channel_id=1, source_target_pairs={{0,4},{4,0},{8,12},{12,8},{16,20},{20,16},{24,28},{28,24},{1,5},{5... | collective-permute-start | bytes 2457608 | tf_op jit(solution)/shard_map/ppermute | solution.py:254
  131.1 12.2 %collective-permute-start.13 = (bf16[2,800,128]{2,1,0:T(8,128)(2,1)}, bf16[2,800,128]{2,1,0:T(8,128)(2,1)}, u32[]{:S(2)}, u32[]{:S(2)}) collective-permute-start(bf16[2,800,128]{2,1,0:T(8,128)(2,1)} %fusion.1), channel_id=1, source_target_pairs={{0,8},{4,12},{8,0},{12,4},{16,24},{20,28},{24,16},{28,20},{1,9},{5... | collective-permute-start | bytes 1228808 | tf_op jit(solution)/shard_map/ppermute | solution.py:254
  135.0 11.6 %collective-permute-start.16 = (bf16[2,800,128]{2,1,0:T(8,128)(2,1)}, bf16[2,800,128]{2,1,0:T(8,128)(2,1)}, u32[]{:S(2)}, u32[]{:S(2)}) collective-permute-start(bf16[2,800,128]{2,1,0:T(8,128)(2,1)} %fusion), channel_id=1, source_target_pairs={{0,16},{4,20},{8,24},{12,28},{16,0},{20,4},{24,8},{28,12},{1,17},{... | collective-permute-start | bytes 1228808 | tf_op jit(solution)/shard_map/ppermute | solution.py:254
  145.1 6.8 %collective-permute-start.14 = (bf16[800,128]{1,0:T(8,128)(2,1)}, bf16[800,128]{1,0:T(8,128)(2,1)S(1)}, u32[]{:S(2)}, u32[]{:S(2)}) collective-permute-start(bf16[800,128]{1,0:T(8,128)(2,1)} %fusion.4), channel_id=1, source_target_pairs={{0,16},{4,20},{8,24},{12,28},{16,0},{20,4},{24,8},{28,12},{1,17},{... | collective-permute-start | bytes 614408 | tf_op jit(solution)/shard_map/ppermute | solution.py:254
  147.7 6.1 %collective-permute-start.17 = (bf16[800,128]{1,0:T(8,128)(2,1)S(1)}, bf16[800,128]{1,0:T(8,128)(2,1)S(1)}, u32[]{:S(2)}, u32[]{:S(2)}) collective-permute-start(bf16[800,128]{1,0:T(8,128)(2,1)S(1)} %fusion.2), channel_id=1, source_target_pairs={{0,8},{4,12},{8,0},{12,4},{16,24},{20,28},{24,16},{28,20},{1,9},{5... | collective-permute-start | bytes 614408 | tf_op jit(solution)/shard_map/ppermute | solution.py:254
